TPU v7x, 32 devices: a whole 2x2x4 slice. The times are simulated.
32 devices in a mesh: res: 8 (over z, x), samp: 4 (over y, core).
Axes of the slice: x: 2, y: 2, z: 4, core: 2. Of those that a mesh axis runs over, the one named last changes fastest.
Arguments:
- coords_pred: float32 [16, 3, 24576], P('samp', None, 'res'), may hold values from -130 to 130
- coords_true: float32 [3, 24576], P(None, 'res'), may hold values from -55 to 55
- atom_kind: int32 [24576], P('res'), may hold values from 0 to 2
- partners: int32 [192, 5], P('res'), may hold values from 0 to 191, as said below
- noise_level: float32 [16], P('samp'), may hold values from 2 to 32
Outputs:
- copy_loss: float32 [16], P('samp')
- mean_loss: float32 [], replicated
- coord_grad: float32 [16, 3, 24576], P('samp', None, 'res')
Inputs may be any that keep to these rules, and one draw needn't show every extreme that they name: `partners`: slot 0 of tile g holds g; the other used slots hold distinct tiles g' with 0 < |g' - g| <= 2, and unused slots hold g again; the pairing is symmetric (g' is listed for g exactly when g is listed for g'); some tile uses all 5 slots.
All inputs are finite; a program needn't handle non-finite values.
Results may differ from a plain program's by a relative error of at most 0.0005.
Values sent between devices are 32-bit elements; how exact they have to be, the bound alone decides.
No kernel may reach another device: no remote copies, remote signals or barrier semaphores. Data moves between devices by JAX's collectives and lax.ppermute only.
A program may use at most 64 MiB of HBM per device.

v0:
```python
import math

import jax
import jax.numpy as jnp
from jax import lax
from jax.sharding import PartitionSpec as P

BAND = 2


precise = lax.Precision.HIGHEST
thresholds = (0.5, 1.0, 2.0, 4.0)
sigma_data = 16.0


def padded(block, sides, width):
    for axis, dim in sides:
        count = lax.axis_size(axis)
        forward = [(i, i + 1) for i in range(count - 1)]
        backward = [(target, source) for source, target in forward]
        low = lax.ppermute(
            lax.slice_in_dim(block, block.shape[dim] - width, None, axis=dim), axis, forward
        )
        high = lax.ppermute(lax.slice_in_dim(block, 0, width, axis=dim), axis, backward)
        block = jnp.concatenate([low, block, high], axis=dim)
    return block


def atom_weight(atom_kind):
    return jnp.where(atom_kind == 1, 5.0, jnp.where(atom_kind == 2, 10.0, 1.0)).astype(jnp.float32)


def atom_cutoff(atom_kind):
    return jnp.where(atom_kind == 1, 30.0, 15.0).astype(jnp.float32)


def moments(coords_pred, coords_true, weight):
    weight_sum = jnp.sum(weight)
    pred_sum = jnp.einsum("sca,a->sc", coords_pred, weight, precision=precise)
    true_sum = jnp.einsum("ca,a->c", coords_true, weight, precision=precise)
    cross = jnp.einsum("sca,da->scd", coords_pred * weight, coords_true, precision=precise)
    return (weight_sum, pred_sum, true_sum, cross)


def rotation_of(weight_sum, pred_sum, true_sum, cross):
    pred_mean = pred_sum / weight_sum
    true_mean = true_sum / weight_sum
    covariance = cross - pred_sum[:, :, None] * true_mean[None, None, :]
    frobenius = jnp.sqrt(jnp.sum(covariance * covariance, axis=(1, 2)))
    polar_factor = covariance / frobenius[:, None, None]
    for sweep_index in range(20):
        gram_matrix = jnp.einsum("sab,scb->sac", polar_factor, polar_factor, precision=precise)
        polar_factor = 1.5 * polar_factor - 0.5 * jnp.einsum(
            "sac,scd->sad", gram_matrix, polar_factor, precision=precise
        )
    return (polar_factor, pred_mean, true_mean)


def aligned_truth(rotation, pred_mean, true_mean, coords_true):
    centred = coords_true - true_mean[:, None]
    return jnp.einsum("scd,da->sca", rotation, centred, precision=precise) + pred_mean[:, :, None]


def pair_terms(own_rows, partner_rows, own_tile, partner_tiles, copies):
    tile_len = own_rows.shape[-1]
    slot_count = partner_tiles.shape[0]
    own_pred = own_rows[: 3 * copies].reshape(copies, 3, tile_len)
    own_true = own_rows[3 * copies : 3 * copies + 3]
    own_cut = own_rows[3 * copies + 3]
    far_pred = partner_rows[: 3 * copies].reshape(copies, 3, slot_count, tile_len)
    far_true = partner_rows[3 * copies : 3 * copies + 3]
    far_cut = partner_rows[3 * copies + 3]
    pred_terms = []
    true_terms = []
    for component in range(3):
        coord_gap = own_pred[:, component, None, :, None] - far_pred[:, component, :, None, :]
        pred_terms.append(coord_gap * coord_gap)
        true_gap = own_true[component][None, :, None] - far_true[component][:, None, :]
        true_terms.append(true_gap * true_gap)
    pred_dist = jnp.sqrt(pred_terms[0] + pred_terms[1] + pred_terms[2] + 1e-06)
    true_dist = jnp.sqrt(true_terms[0] + true_terms[1] + true_terms[2] + 1e-06)
    slot_used = (jnp.arange(slot_count) == 0) | (partner_tiles != own_tile)
    same_atom = jnp.arange(tile_len)[:, None] == jnp.arange(tile_len)[None, :]
    diagonal = (partner_tiles == own_tile)[:, None, None] & same_atom[None]
    usable = slot_used[:, None, None] & jnp.logical_not(diagonal)
    mask_fwd = jnp.where(usable & (true_dist < far_cut[:, None, :]), 1.0, 0.0).astype(jnp.float32)
    mask_back = jnp.where(usable & (true_dist < own_cut[None, :, None]), 1.0, 0.0).astype(
        jnp.float32
    )
    spread = jnp.abs(pred_dist - true_dist)
    score_parts = []
    slope_parts = []
    for threshold in thresholds:
        squash = jax.nn.sigmoid(threshold - spread)
        score_parts.append(squash)
        slope_parts.append(squash * (1.0 - squash))
    pair_score = 0.25 * (score_parts[0] + score_parts[1] + score_parts[2] + score_parts[3])
    pair_slope = -0.25 * (slope_parts[0] + slope_parts[1] + slope_parts[2] + slope_parts[3])
    pair_count = jnp.sum(mask_fwd)
    score_sum = jnp.sum(mask_fwd * pair_score, axis=(1, 2, 3))
    factor = (mask_fwd + mask_back) * pair_slope * jnp.sign(pred_dist - true_dist) / pred_dist
    weight_row = jnp.sum(factor, axis=(1, 3))
    pull_parts = []
    for component in range(3):
        remote = jnp.einsum("skij,skj->si", factor, far_pred[:, component], precision=precise)
        pull_parts.append(own_pred[:, component] * weight_row - remote)
    return (pair_count, score_sum, jnp.stack(pull_parts, axis=1))


def shards(coords_pred, coords_true, atom_kind, partners, noise_level):
    copies = coords_pred.shape[0]
    local_atoms = coords_pred.shape[2]
    tile_count = partners.shape[0]
    tile_len = local_atoms // tile_count
    res_rank = lax.axis_index("res")
    weight = atom_weight(atom_kind)
    cutoff = atom_cutoff(atom_kind)
    packed = jnp.concatenate(
        [coords_pred.reshape(3 * copies, local_atoms), coords_true, cutoff[None]], axis=0
    )
    window = padded(packed, (("res", 1),), BAND * tile_len)
    first_tile = res_rank * tile_count - BAND
    row_count = packed.shape[0]
    own_tiles = packed.reshape(row_count, tile_count, tile_len)
    far_tiles = window.reshape(row_count, -1, tile_len)
    group_size = math.gcd(tile_count, max(1, 512 // tile_len))
    group_count = tile_count // group_size

    def tile_work(own_rows, partner_rows, own_tile, partner_tiles):
        return pair_terms(own_rows, partner_rows, own_tile, partner_tiles, copies)

    mapped_work = jax.vmap(tile_work, in_axes=(0, 0, 0, 0))

    def visit_group(totals, local_ids):
        own_rows = jnp.moveaxis(jnp.take(own_tiles, local_ids, axis=1), 1, 0)
        partner_tiles = jnp.take(partners, local_ids, axis=0)
        partner_rows = jnp.moveaxis(jnp.take(far_tiles, partner_tiles - first_tile, axis=1), 1, 0)
        pair_count, score_sum, pull_group = mapped_work(
            own_rows, partner_rows, res_rank * tile_count + local_ids, partner_tiles
        )
        return (
            (totals[0] + jnp.sum(pair_count), totals[1] + jnp.sum(score_sum, axis=0)),
            pull_group,
        )

    start_totals = (jnp.float32(0.0), jnp.zeros((copies,), jnp.float32))
    group_ids = jnp.arange(tile_count, dtype=jnp.int32).reshape(group_count, group_size)
    (pair_local, score_local), pull_groups = lax.scan(visit_group, start_totals, group_ids)
    pull_tiles = pull_groups.reshape(tile_count, copies, 3, tile_len)
    pull_field = jnp.moveaxis(pull_tiles, 0, 2).reshape(copies, 3, local_atoms)
    weight_sum, pred_sum, true_sum, cross = moments(coords_pred, coords_true, weight)
    weight_sum, pred_sum, true_sum, cross = lax.psum((weight_sum, pred_sum, true_sum, cross), "res")
    rotation, pred_mean, true_mean = rotation_of(weight_sum, pred_sum, true_sum, cross)
    target = aligned_truth(rotation, pred_mean, true_mean, coords_true)
    deviation = coords_pred - target
    square_local = jnp.sum(weight * deviation * deviation, axis=(1, 2))
    square_err, score_total, pair_sum = lax.psum((square_local, score_local, pair_local), "res")
    loss_weight = (noise_level * noise_level + sigma_data * sigma_data) / (
        noise_level * sigma_data * (noise_level * sigma_data)
    )
    mean_square = square_err / (3.0 * weight_sum)
    copy_loss = loss_weight * mean_square + 1.0 - score_total / pair_sum
    copy_sum = lax.psum(jnp.sum(copy_loss), "samp")
    mean_loss = copy_sum / (copies * lax.axis_size("samp"))
    atom_total = local_atoms * lax.axis_size("res")
    grad_scale = 16.0 * atom_total
    coord_grad = grad_scale * (
        2.0 * loss_weight[:, None, None] * weight * deviation / (3.0 * weight_sum)
        - pull_field / pair_sum
    )
    return (copy_loss, mean_loss, coord_grad)


def solution(mesh):
    in_specs = (P("samp", None, "res"), P(None, "res"), P("res"), P("res", None), P("samp"))
    out_specs = (P("samp"), P(), P("samp", None, "res"))
    return jax.shard_map(shards, mesh=mesh, in_specs=in_specs, out_specs=out_specs, check_vma=False)
```

profile of v0, /device:TPU:0, one launch (start us, length us, event | category | flops | bytes accessed | tf_op | source)
XLA Modules:
  0.0 520.4 jit_solution(4268508525636345049)
XLA Ops:
  5.1 5.5 %collective-permute-start = (f32[16,256]{1,0:T(8,128)S(1)}, f32[16,256]{1,0:T(8,128)S(1)}, u32[]{:S(2)}, u32[]{:S(2)}) collective-permute-start(f32[16,256]{1,0:T(8,128)S(1)} %get-tuple-element.263), channel_id=1, source_target_pairs={{0,4},{4,8},{8,12},{12,16},{16,20},{20,24},{24,28},{1,5},{5,9},{9,... | collective-permute-start | bytes 49160 | tf_op jit(solution)/shard_map/ppermute | solution.py:21
  13.3 21.5 %all-reduce.1 = (f32[4,3]{0,1:T(4,128)S(1)}, f32[]{:T(128)}, f32[3]{0:T(128)S(1)}, f32[4,3,3]{0,2,1:T(4,128)S(1)}) all-reduce(f32[4,3]{0,1:T(4,128)S(1)} %bitcast.273, f32[]{:T(128)} %get-tuple-element.265, f32[3]{0:T(128)S(1)} %convolution_bitcast_fusion, f32[4,3,3]{0,2,1:T(4,128)S(1)} %fusion.38), channel_id=1, replica_groups=mesh['res'=8,'samp'=4] {'res'}, use_global_device_ids=true, to_apply=%region_1.2 | all-reduce | flops 52 | bytes 416 | tf_op jit(solution)/shard_map/psum | solution.py:152
  51.8 438.0 %while.17 = (s32[]{:T(128)}, f32[]{:T(128)}, f32[4]{0:T(128)S(1)}, f32[6,4,4,3,128]{4,2,1,3,0:T(4,128)}, s32[6,4]{1,0:T(8,128)S(1)}, /*index=5*/s32[24,5]{1,0:T(...) while((s32[]{:T(128)}, f32[]{:T(128)}, f32[4]{0:T(128)S(1)}, ...), condition=%wide.region_12.13_spmd.clone, body=%wide.region_8.12_spmd.clone.sunk | while | flops 282550656 | bytes 18752740 | solution.py:148
  54.3 3.3 select_multiply_fusion.2
  58.5 14.9 %fusion.211 = (f32[4,4,128]{2,1,0:T(4,128)S(1)}, f32[4]{0:T(128)S(1)}) fusion(f32[4,5,128,128]{3,2,1,0:T(8,128)S(1)} %get-tuple-element.383, f32[4,5,128,128]{3,2,1,0:T(8,128)S(1)} %get-tuple-element.384, f32[4,4,5,128]{3,2,1,0:T(8,128)S(1)} %copy.383, f32[4,4,128]{2,1,0:T(4,128)S(1)} %get-tuple-element.388, f32[4,4,5,128]{3,2,1,0:T(8,128)S(1)} %copy.385, ...), kind=kLoop, calls=%fused_computation.30.clone.1 | loop fusion | flops 62912508 | bytes 4087824 | tf_op jit(solution)/shard_map/while/body/eval_jaxpr/vmap()/reduce_sum | solution.py:102
  73.5 17.0 %fusion.213 = f32[4,4,1,128,1]{3,2,4,1,0:T(1,128)S(1)} fusion(f32[4,5,128,128]{3,2,1,0:T(8,128)S(1)} %get-tuple-element.383, f32[4,5,128,128]{3,2,1,0:T(8,128)S(1)} %get-tuple-element.384, f32[4,4,5,128]{3,2,1,0:T(8,128)S(1)} %copy.383, f32[4,4,128]{2,1,0:T(4,128)S(1)} %get-tuple-element.388, f32[4,4,5,128]{3,2,1,0:T(8,128)S(1)} %copy.385, ...), kind=kOutput, calls=%fused_computation.29.clone.1 | convolution fusion | flops 70778880 | bytes 2818048 | tf_op jit(solution)/shard_map/while/body/eval_jaxpr/vmap(skij,skj->si)/dot_general | solution.py:105
  90.4 16.9 %fusion.214 = f32[4,4,1,128,1]{3,2,4,1,0:T(1,128)S(1)} fusion(f32[4,5,128,128]{3,2,1,0:T(8,128)S(1)} %get-tuple-element.383, f32[4,5,128,128]{3,2,1,0:T(8,128)S(1)} %get-tuple-element.384, f32[4,4,5,128]{3,2,1,0:T(8,128)S(1)} %copy.383, f32[4,4,128]{2,1,0:T(4,128)S(1)} %get-tuple-element.388, f32[4,4,5,128]{3,2,1,0:T(8,128)S(1)} %copy.385, ...), kind=kOutput, calls=%fused_computation.27.clone.1 | convolution fusion | flops 70778880 | bytes 2818048 | tf_op jit(solution)/shard_map/while/body/eval_jaxpr/vmap(skij,skj->si)/dot_general | solution.py:105
  107.4 16.9 %fusion.215 = f32[4,4,1,128,1]{3,2,4,1,0:T(1,128)S(1)} fusion(f32[4,5,128,128]{3,2,1,0:T(8,128)S(1)} %get-tuple-element.383, f32[4,5,128,128]{3,2,1,0:T(8,128)S(1)} %get-tuple-element.384, f32[4,4,5,128]{3,2,1,0:T(8,128)S(1)} %copy.383, f32[4,4,128]{2,1,0:T(4,128)S(1)} %get-tuple-element.388, f32[4,4,5,128]{3,2,1,0:T(8,128)S(1)} %copy.385, ...), kind=kOutput, calls=%fused_computation.28.clone.1 | convolution fusion | flops 70778880 | bytes 2818048 | tf_op jit(solution)/shard_map/while/body/eval_jaxpr/vmap(skij,skj->si)/dot_general | solution.py:105
  127.3 3.3 select_multiply_fusion.2
  131.5 14.9 %fusion.211 = (f32[4,4,128]{2,1,0:T(4,128)S(1)}, f32[4]{0:T(128)S(1)}) fusion(f32[4,5,128,128]{3,2,1,0:T(8,128)S(1)} %get-tuple-element.383, f32[4,5,128,128]{3,2,1,0:T(8,128)S(1)} %get-tuple-element.384, f32[4,4,5,128]{3,2,1,0:T(8,128)S(1)} %copy.383, f32[4,4,128]{2,1,0:T(4,128)S(1)} %get-tuple-element.388, f32[4,4,5,128]{3,2,1,0:T(8,128)S(1)} %copy.385, ...), kind=kLoop, calls=%fused_computation.30.clone.1 | loop fusion | flops 62912508 | bytes 4087824 | tf_op jit(solution)/shard_map/while/body/eval_jaxpr/vmap()/reduce_sum | solution.py:102
  146.4 17.0 %fusion.213 = f32[4,4,1,128,1]{3,2,4,1,0:T(1,128)S(1)} fusion(f32[4,5,128,128]{3,2,1,0:T(8,128)S(1)} %get-tuple-element.383, f32[4,5,128,128]{3,2,1,0:T(8,128)S(1)} %get-tuple-element.384, f32[4,4,5,128]{3,2,1,0:T(8,128)S(1)} %copy.383, f32[4,4,128]{2,1,0:T(4,128)S(1)} %get-tuple-element.388, f32[4,4,5,128]{3,2,1,0:T(8,128)S(1)} %copy.385, ...), kind=kOutput, calls=%fused_computation.29.clone.1 | convolution fusion | flops 70778880 | bytes 2818048 | tf_op jit(solution)/shard_map/while/body/eval_jaxpr/vmap(skij,skj->si)/dot_general | solution.py:105
  163.4 16.9 %fusion.214 = f32[4,4,1,128,1]{3,2,4,1,0:T(1,128)S(1)} fusion(f32[4,5,128,128]{3,2,1,0:T(8,128)S(1)} %get-tuple-element.383, f32[4,5,128,128]{3,2,1,0:T(8,128)S(1)} %get-tuple-element.384, f32[4,4,5,128]{3,2,1,0:T(8,128)S(1)} %copy.383, f32[4,4,128]{2,1,0:T(4,128)S(1)} %get-tuple-element.388, f32[4,4,5,128]{3,2,1,0:T(8,128)S(1)} %copy.385, ...), kind=kOutput, calls=%fused_computation.27.clone.1 | convolution fusion | flops 70778880 | bytes 2818048 | tf_op jit(solution)/shard_map/while/body/eval_jaxpr/vmap(skij,skj->si)/dot_general | solution.py:105
  180.3 16.9 %fusion.215 = f32[4,4,1,128,1]{3,2,4,1,0:T(1,128)S(1)} fusion(f32[4,5,128,128]{3,2,1,0:T(8,128)S(1)} %get-tuple-element.383, f32[4,5,128,128]{3,2,1,0:T(8,128)S(1)} %get-tuple-element.384, f32[4,4,5,128]{3,2,1,0:T(8,128)S(1)} %copy.383, f32[4,4,128]{2,1,0:T(4,128)S(1)} %get-tuple-element.388, f32[4,4,5,128]{3,2,1,0:T(8,128)S(1)} %copy.385, ...), kind=kOutput, calls=%fused_computation.28.clone.1 | convolution fusion | flops 70778880 | bytes 2818048 | tf_op jit(solution)/shard_map/while/body/eval_jaxpr/vmap(skij,skj->si)/dot_general | solution.py:105
  204.4 14.9 %fusion.211 = (f32[4,4,128]{2,1,0:T(4,128)S(1)}, f32[4]{0:T(128)S(1)}) fusion(f32[4,5,128,128]{3,2,1,0:T(8,128)S(1)} %get-tuple-element.383, f32[4,5,128,128]{3,2,1,0:T(8,128)S(1)} %get-tuple-element.384, f32[4,4,5,128]{3,2,1,0:T(8,128)S(1)} %copy.383, f32[4,4,128]{2,1,0:T(4,128)S(1)} %get-tuple-element.388, f32[4,4,5,128]{3,2,1,0:T(8,128)S(1)} %copy.385, ...), kind=kLoop, calls=%fused_computation.30.clone.1 | loop fusion | flops 62912508 | bytes 4087824 | tf_op jit(solution)/shard_map/while/body/eval_jaxpr/vmap()/reduce_sum | solution.py:102
  219.4 17.0 %fusion.213 = f32[4,4,1,128,1]{3,2,4,1,0:T(1,128)S(1)} fusion(f32[4,5,128,128]{3,2,1,0:T(8,128)S(1)} %get-tuple-element.383, f32[4,5,128,128]{3,2,1,0:T(8,128)S(1)} %get-tuple-element.384, f32[4,4,5,128]{3,2,1,0:T(8,128)S(1)} %copy.383, f32[4,4,128]{2,1,0:T(4,128)S(1)} %get-tuple-element.388, f32[4,4,5,128]{3,2,1,0:T(8,128)S(1)} %copy.385, ...), kind=kOutput, calls=%fused_computation.29.clone.1 | convolution fusion | flops 70778880 | bytes 2818048 | tf_op jit(solution)/shard_map/while/body/eval_jaxpr/vmap(skij,skj->si)/dot_general | solution.py:105
  236.3 16.9 %fusion.214 = f32[4,4,1,128,1]{3,2,4,1,0:T(1,128)S(1)} fusion(f32[4,5,128,128]{3,2,1,0:T(8,128)S(1)} %get-tuple-element.383, f32[4,5,128,128]{3,2,1,0:T(8,128)S(1)} %get-tuple-element.384, f32[4,4,5,128]{3,2,1,0:T(8,128)S(1)} %copy.383, f32[4,4,128]{2,1,0:T(4,128)S(1)} %get-tuple-element.388, f32[4,4,5,128]{3,2,1,0:T(8,128)S(1)} %copy.385, ...), kind=kOutput, calls=%fused_computation.27.clone.1 | convolution fusion | flops 70778880 | bytes 2818048 | tf_op jit(solution)/shard_map/while/body/eval_jaxpr/vmap(skij,skj->si)/dot_general | solution.py:105
  253.3 16.9 %fusion.215 = f32[4,4,1,128,1]{3,2,4,1,0:T(1,128)S(1)} fusion(f32[4,5,128,128]{3,2,1,0:T(8,128)S(1)} %get-tuple-element.383, f32[4,5,128,128]{3,2,1,0:T(8,128)S(1)} %get-tuple-element.384, f32[4,4,5,128]{3,2,1,0:T(8,128)S(1)} %copy.383, f32[4,4,128]{2,1,0:T(4,128)S(1)} %get-tuple-element.388, f32[4,4,5,128]{3,2,1,0:T(8,128)S(1)} %copy.385, ...), kind=kOutput, calls=%fused_computation.28.clone.1 | convolution fusion | flops 70778880 | bytes 2818048 | tf_op jit(solution)/shard_map/while/body/eval_jaxpr/vmap(skij,skj->si)/dot_general | solution.py:105
  277.4 14.9 %fusion.211 = (f32[4,4,128]{2,1,0:T(4,128)S(1)}, f32[4]{0:T(128)S(1)}) fusion(f32[4,5,128,128]{3,2,1,0:T(8,128)S(1)} %get-tuple-element.383, f32[4,5,128,128]{3,2,1,0:T(8,128)S(1)} %get-tuple-element.384, f32[4,4,5,128]{3,2,1,0:T(8,128)S(1)} %copy.383, f32[4,4,128]{2,1,0:T(4,128)S(1)} %get-tuple-element.388, f32[4,4,5,128]{3,2,1,0:T(8,128)S(1)} %copy.385, ...), kind=kLoop, calls=%fused_computation.30.clone.1 | loop fusion | flops 62912508 | bytes 4087824 | tf_op jit(solution)/shard_map/while/body/eval_jaxpr/vmap()/reduce_sum | solution.py:102
  292.4 17.0 %fusion.213 = f32[4,4,1,128,1]{3,2,4,1,0:T(1,128)S(1)} fusion(f32[4,5,128,128]{3,2,1,0:T(8,128)S(1)} %get-tuple-element.383, f32[4,5,128,128]{3,2,1,0:T(8,128)S(1)} %get-tuple-element.384, f32[4,4,5,128]{3,2,1,0:T(8,128)S(1)} %copy.383, f32[4,4,128]{2,1,0:T(4,128)S(1)} %get-tuple-element.388, f32[4,4,5,128]{3,2,1,0:T(8,128)S(1)} %copy.385, ...), kind=kOutput, calls=%fused_computation.29.clone.1 | convolution fusion | flops 70778880 | bytes 2818048 | tf_op jit(solution)/shard_map/while/body/eval_jaxpr/vmap(skij,skj->si)/dot_general | solution.py:105
  309.3 16.9 %fusion.214 = f32[4,4,1,128,1]{3,2,4,1,0:T(1,128)S(1)} fusion(f32[4,5,128,128]{3,2,1,0:T(8,128)S(1)} %get-tuple-element.383, f32[4,5,128,128]{3,2,1,0:T(8,128)S(1)} %get-tuple-element.384, f32[4,4,5,128]{3,2,1,0:T(8,128)S(1)} %copy.383, f32[4,4,128]{2,1,0:T(4,128)S(1)} %get-tuple-element.388, f32[4,4,5,128]{3,2,1,0:T(8,128)S(1)} %copy.385, ...), kind=kOutput, calls=%fused_computation.27.clone.1 | convolution fusion | flops 70778880 | bytes 2818048 | tf_op jit(solution)/shard_map/while/body/eval_jaxpr/vmap(skij,skj->si)/dot_general | solution.py:105
  326.3 16.9 %fusion.215 = f32[4,4,1,128,1]{3,2,4,1,0:T(1,128)S(1)} fusion(f32[4,5,128,128]{3,2,1,0:T(8,128)S(1)} %get-tuple-element.383, f32[4,5,128,128]{3,2,1,0:T(8,128)S(1)} %get-tuple-element.384, f32[4,4,5,128]{3,2,1,0:T(8,128)S(1)} %copy.383, f32[4,4,128]{2,1,0:T(4,128)S(1)} %get-tuple-element.388, f32[4,4,5,128]{3,2,1,0:T(8,128)S(1)} %copy.385, ...), kind=kOutput, calls=%fused_computation.28.clone.1 | convolution fusion | flops 70778880 | bytes 2818048 | tf_op jit(solution)/shard_map/while/body/eval_jaxpr/vmap(skij,skj->si)/dot_general | solution.py:105
  346.2 3.3 select_multiply_fusion.2
  350.4 14.9 %fusion.211 = (f32[4,4,128]{2,1,0:T(4,128)S(1)}, f32[4]{0:T(128)S(1)}) fusion(f32[4,5,128,128]{3,2,1,0:T(8,128)S(1)} %get-tuple-element.383, f32[4,5,128,128]{3,2,1,0:T(8,128)S(1)} %get-tuple-element.384, f32[4,4,5,128]{3,2,1,0:T(8,128)S(1)} %copy.383, f32[4,4,128]{2,1,0:T(4,128)S(1)} %get-tuple-element.388, f32[4,4,5,128]{3,2,1,0:T(8,128)S(1)} %copy.385, ...), kind=kLoop, calls=%fused_computation.30.clone.1 | loop fusion | flops 62912508 | bytes 4087824 | tf_op jit(solution)/shard_map/while/body/eval_jaxpr/vmap()/reduce_sum | solution.py:102
  365.3 17.0 %fusion.213 = f32[4,4,1,128,1]{3,2,4,1,0:T(1,128)S(1)} fusion(f32[4,5,128,128]{3,2,1,0:T(8,128)S(1)} %get-tuple-element.383, f32[4,5,128,128]{3,2,1,0:T(8,128)S(1)} %get-tuple-element.384, f32[4,4,5,128]{3,2,1,0:T(8,128)S(1)} %copy.383, f32[4,4,128]{2,1,0:T(4,128)S(1)} %get-tuple-element.388, f32[4,4,5,128]{3,2,1,0:T(8,128)S(1)} %copy.385, ...), kind=kOutput, calls=%fused_computation.29.clone.1 | convolution fusion | flops 70778880 | bytes 2818048 | tf_op jit(solution)/shard_map/while/body/eval_jaxpr/vmap(skij,skj->si)/dot_general | solution.py:105
  382.3 16.9 %fusion.214 = f32[4,4,1,128,1]{3,2,4,1,0:T(1,128)S(1)} fusion(f32[4,5,128,128]{3,2,1,0:T(8,128)S(1)} %get-tuple-element.383, f32[4,5,128,128]{3,2,1,0:T(8,128)S(1)} %get-tuple-element.384, f32[4,4,5,128]{3,2,1,0:T(8,128)S(1)} %copy.383, f32[4,4,128]{2,1,0:T(4,128)S(1)} %get-tuple-element.388, f32[4,4,5,128]{3,2,1,0:T(8,128)S(1)} %copy.385, ...), kind=kOutput, calls=%fused_computation.27.clone.1 | convolution fusion | flops 70778880 | bytes 2818048 | tf_op jit(solution)/shard_map/while/body/eval_jaxpr/vmap(skij,skj->si)/dot_general | solution.py:105
  399.2 16.9 %fusion.215 = f32[4,4,1,128,1]{3,2,4,1,0:T(1,128)S(1)} fusion(f32[4,5,128,128]{3,2,1,0:T(8,128)S(1)} %get-tuple-element.383, f32[4,5,128,128]{3,2,1,0:T(8,128)S(1)} %get-tuple-element.384, f32[4,4,5,128]{3,2,1,0:T(8,128)S(1)} %copy.383, f32[4,4,128]{2,1,0:T(4,128)S(1)} %get-tuple-element.388, f32[4,4,5,128]{3,2,1,0:T(8,128)S(1)} %copy.385, ...), kind=kOutput, calls=%fused_computation.28.clone.1 | convolution fusion | flops 70778880 | bytes 2818048 | tf_op jit(solution)/shard_map/while/body/eval_jaxpr/vmap(skij,skj->si)/dot_general | solution.py:105
  423.3 14.9 %fusion.211 = (f32[4,4,128]{2,1,0:T(4,128)S(1)}, f32[4]{0:T(128)S(1)}) fusion(f32[4,5,128,128]{3,2,1,0:T(8,128)S(1)} %get-tuple-element.383, f32[4,5,128,128]{3,2,1,0:T(8,128)S(1)} %get-tuple-element.384, f32[4,4,5,128]{3,2,1,0:T(8,128)S(1)} %copy.383, f32[4,4,128]{2,1,0:T(4,128)S(1)} %get-tuple-element.388, f32[4,4,5,128]{3,2,1,0:T(8,128)S(1)} %copy.385, ...), kind=kLoop, calls=%fused_computation.30.clone.1 | loop fusion | flops 62912508 | bytes 4087824 | tf_op jit(solution)/shard_map/while/body/eval_jaxpr/vmap()/reduce_sum | solution.py:102
  438.3 17.0 %fusion.213 = f32[4,4,1,128,1]{3,2,4,1,0:T(1,128)S(1)} fusion(f32[4,5,128,128]{3,2,1,0:T(8,128)S(1)} %get-tuple-element.383, f32[4,5,128,128]{3,2,1,0:T(8,128)S(1)} %get-tuple-element.384, f32[4,4,5,128]{3,2,1,0:T(8,128)S(1)} %copy.383, f32[4,4,128]{2,1,0:T(4,128)S(1)} %get-tuple-element.388, f32[4,4,5,128]{3,2,1,0:T(8,128)S(1)} %copy.385, ...), kind=kOutput, calls=%fused_computation.29.clone.1 | convolution fusion | flops 70778880 | bytes 2818048 | tf_op jit(solution)/shard_map/while/body/eval_jaxpr/vmap(skij,skj->si)/dot_general | solution.py:105
  455.2 16.9 %fusion.214 = f32[4,4,1,128,1]{3,2,4,1,0:T(1,128)S(1)} fusion(f32[4,5,128,128]{3,2,1,0:T(8,128)S(1)} %get-tuple-element.383, f32[4,5,128,128]{3,2,1,0:T(8,128)S(1)} %get-tuple-element.384, f32[4,4,5,128]{3,2,1,0:T(8,128)S(1)} %copy.383, f32[4,4,128]{2,1,0:T(4,128)S(1)} %get-tuple-element.388, f32[4,4,5,128]{3,2,1,0:T(8,128)S(1)} %copy.385, ...), kind=kOutput, calls=%fused_computation.27.clone.1 | convolution fusion | flops 70778880 | bytes 2818048 | tf_op jit(solution)/shard_map/while/body/eval_jaxpr/vmap(skij,skj->si)/dot_general | solution.py:105
  472.2 16.9 %fusion.215 = f32[4,4,1,128,1]{3,2,4,1,0:T(1,128)S(1)} fusion(f32[4,5,128,128]{3,2,1,0:T(8,128)S(1)} %get-tuple-element.383, f32[4,5,128,128]{3,2,1,0:T(8,128)S(1)} %get-tuple-element.384, f32[4,4,5,128]{3,2,1,0:T(8,128)S(1)} %copy.383, f32[4,4,128]{2,1,0:T(4,128)S(1)} %get-tuple-element.388, f32[4,4,5,128]{3,2,1,0:T(8,128)S(1)} %copy.385, ...), kind=kOutput, calls=%fused_computation.28.clone.1 | convolution fusion | flops 70778880 | bytes 2818048 | tf_op jit(solution)/shard_map/while/body/eval_jaxpr/vmap(skij,skj->si)/dot_general | solution.py:105
  489.8 18.3 %all-reduce = (f32[4]{0:T(128)S(1)}, f32[4]{0:T(128)S(1)}, f32[]{:T(128)}) all-reduce(f32[4]{0:T(128)S(1)} %get-tuple-element.121, f32[4]{0:T(128)S(1)} %copy-done.7, f32[]{:T(128)} %get-tuple-element.122), channel_id=1, replica_groups=mesh['res'=8,'samp'=4] {'res'}, use_global_device_ids=true, to_apply=%region_13.14 | all-reduce | flops 9 | bytes 72 | tf_op jit(solution)/shard_map/psum | solution.py:157
  510.0 6.3 %psum.63 = f32[]{:T(128)} all-reduce(f32[]{:T(128)} %get-tuple-element.228), channel_id=1, replica_groups=mesh['res'=8,'samp'=4] {'samp'}, use_global_device_ids=true, to_apply=%region_16.17 | all-reduce | flops 1 | bytes 8 | tf_op jit(solution)/shard_map/psum | solution.py:163
  (362 shorter events, 55.6 us)
Async XLA Ops:
  0.6 10.1 %copy-start.1 = (f32[4,3,3072]{2,0,1:T(4,128)S(1)}, f32[4,3,3072]{2,0,1:T(4,128)}, u32[]{:S(2)}) copy-start(f32[4,3,3072]{2,0,1:T(4,128)} %param.7) | copy-start | bytes 442372
  0.6 10.1 %copy-start = (f32[3,3072]{1,0:T(4,128)S(1)}, f32[3,3072]{1,0:T(4,128)}, u32[]{:S(2)}) copy-start(f32[3,3072]{1,0:T(4,128)} %param.8) | copy-start | bytes 110596
  3.8 47.9 %collective-permute-start.1 = (f32[16,256]{1,0:T(8,128)S(1)}, f32[16,256]{1,0:T(8,128)S(1)}, u32[]{:S(2)}, u32[]{:S(2)}) collective-permute-start(f32[16,256]{1,0:T(8,128)S(1)} %get-tuple-element.264), channel_id=1, source_target_pairs={{4,0},{8,4},{12,8},{16,12},{20,16},{24,20},{28,24},{5,1},{9,5},{13... | collective-permute-start | bytes 49160 | tf_op jit(solution)/shard_map/ppermute | solution.py:24
  5.1 46.6 %collective-permute-start = (f32[16,256]{1,0:T(8,128)S(1)}, f32[16,256]{1,0:T(8,128)S(1)}, u32[]{:S(2)}, u32[]{:S(2)}) collective-permute-start(f32[16,256]{1,0:T(8,128)S(1)} %get-tuple-element.263), channel_id=1, source_target_pairs={{0,4},{4,8},{8,12},{12,16},{16,20},{20,24},{24,28},{1,5},{5,9},{9,... | collective-permute-start | bytes 49160 | tf_op jit(solution)/shard_map/ppermute | solution.py:21
  10.7 37.0 %copy-start.6 = (f32[4]{0:T(128)S(1)}, f32[4]{0:T(128)}, u32[]{:S(2)}) copy-start(f32[4]{0:T(128)} %param.11) | copy-start | bytes 52
  37.6 13.3 %copy-start.4 = (s32[24,5]{0,1:T(8,128)S(1)}, s32[24,5]{0,1:T(8,128)}, u32[]{:S(2)}) copy-start(s32[24,5]{0,1:T(8,128)} %param.10) | copy-start | bytes 1444
  51.8 438.0 %copy-start.7 = (f32[4]{0:T(128)S(1)}, f32[4]{0:T(128)}, u32[]{:S(2)}) copy-start(f32[4]{0:T(128)} %get-tuple-element.269) | copy-start | bytes 52
  51.8 456.4 %copy-start.5 = (f32[4]{0:T(128)S(1)}, f32[4]{0:T(128)}, u32[]{:S(2)}) copy-start(f32[4]{0:T(128)} %get-tuple-element.227) | copy-start | bytes 52
  51.8 466.7 %copy-start.2 = (f32[4,3072]{1,0:T(4,128)S(1)}, f32[4,3072]{1,0:T(4,128)}, u32[]{:S(2)}) copy-start(f32[4,3072]{1,0:T(4,128)} %broadcast_multiply_fusion) | copy-start | bytes 147460
  489.8 28.7 %copy-start.3 = (f32[4,3,3072]{2,0,1:T(4,128)S(1)}, f32[4,3,3072]{2,0,1:T(4,128)}, u32[]{:S(2)}) copy-start(f32[4,3,3072]{2,0,1:T(4,128)} %get-tuple-element.270) | copy-start | bytes 442372
where the time goes:
time: 521 us; the launch traced here: 520 us
  matrix products  316 us (61%)
  other arithmetic  125 us (24%)
  blocking collectives  46.1 us (9%)
  local copies, waits for them, and re-layouts  17.8 us (3%)
  starting transfers between devices  6.76 us (1%)
    dot_general x18, matrix products, pair_terms(): jnp.einsum('skij,skj->si', factor, far_pred[:, component], precision=prec...  305 us
    reduce_sum x6, other arithmetic, pair_terms(): weight_row = jnp.sum(factor, axis=(1, 3))  89.6 us
    psum x1, blocking collectives, shards(): lax.psum((weight_sum, pred_sum, true_sum, cross), 'res')  21.5 us
    mul x6, other arithmetic, pair_terms(): score_sum = jnp.sum(mask_fwd * pair_score, axis=(1, 2, 3))  20.1 us
    psum x1, blocking collectives, shards(): lax.psum((square_local, score_local, pair_local), 'res')  18.3 us
  transfers between devices with their start and end apart: 2, of which 0 were waited for; matrix products, arithmetic and copies ran while one was open for 4% of the time, Pallas kernels for 0%

commit v1 on v0

v1 whole, which is shorter than its diff:
```python
import functools

import jax
import jax.numpy as jnp
from jax import lax
from jax.experimental import pallas as pl
from jax.experimental.pallas import tpu as pltpu
from jax.sharding import PartitionSpec as P

LANES = 128
BAND = 2
SWEEPS = 20
SIGMA = 16.0
HALF_THRESHOLDS = (0.25, 0.5, 1.0, 2.0)
EPS = 0.25e-6
F32 = jnp.float32


def roll(x, shift, axis=1):
    return pltpu.roll(x, shift, axis)


def two_sum(a, b):
    s = a + b
    t = s - a
    return s, (a - (s - t)) + (b - t)


def two_prod(a, b):
    def halves(x):
        t = x * 4097.0
        h = t - (t - x)
        return h, x - h

    p = a * b
    ah, al = halves(a)
    bh, bl = halves(b)
    return p, ((ah * bh - p) + ah * bl + al * bh) + al * bl


def pair_add(x, y):
    s, e = two_sum(x[0], y[0])
    return two_sum(s, e + (x[1] + y[1]))


def pair_neg(x):
    return -x[0], -x[1]


def pair_mul(x, y):
    p, e = two_prod(x[0], y[0])
    return two_sum(p, e + (x[0] * y[1] + x[1] * y[0]))


def pair_div(x, w):
    q = x[0] / w
    p, e = two_prod(q, w)
    return two_sum(q, (((x[0] - p) - e) + x[1]) / w)


def pair_kernel(base_ref, part_ref, pred_ref, true_ref, kind_ref, lo_ref, hi_ref, pull_ref, stat_ref,
                x_ref, xr_ref, s_ref, td_ref, w_ref, pi_ref, aj_ref, sc_ref, cn_ref, *, copies, tiles):
    base = base_ref[0]
    rows = 3 * copies
    window = tiles + 2 * BAND
    for q in range(BAND):
        x_ref[q] = lo_ref[:, q * LANES:(q + 1) * LANES]
        x_ref[window - BAND + q] = hi_ref[:, q * LANES:(q + 1) * LANES]

    @pl.loop(0, tiles)
    def _(t):
        sl = pl.ds(pl.multiple_of(t * LANES, LANES), LANES)
        kind = kind_ref[:, sl]
        for s in range(copies):
            x_ref[t + BAND, 3 * s:3 * s + 3, :] = pred_ref[s, :, sl] * 0.5
        x_ref[t + BAND, rows:rows + 3, :] = true_ref[:, sl] * 0.5
        x_ref[t + BAND, rows + 3:rows + 4, :] = jnp.where(kind == 1, 15.0, 7.5)

    @pl.loop(0, window)
    def _(t):
        x = x_ref[t]
        for b in range(16):
            xr_ref[t, b] = roll(x, 127 - 8 * b)
        pi_ref[t] = jnp.zeros(pi_ref.shape[1:], F32)

    sc_ref[...] = jnp.zeros_like(sc_ref)
    cn_ref[...] = jnp.zeros_like(cn_ref)
    row = lax.broadcasted_iota(jnp.int32, (8, LANES), 0)

    zero = jnp.zeros((16, LANES), F32)

    def add_tile(t, carry):
        acc, total = carry
        x = x_ref[t + BAND]
        kind = kind_ref[:, pl.ds(pl.multiple_of(t * LANES, LANES), LANES)]
        weight = jnp.where(kind == 1, 5.0, jnp.where(kind == 2, 10.0, 1.0))
        wx = x * weight
        terms = [wx * x[rows + c:rows + c + 1] for c in range(3)] + [wx, wx * x]
        out = []
        for (high, low), term in zip(acc, terms):
            s, e = two_sum(high, term)
            out.append((s, low + e))
        return tuple(out), total + weight

    acc, total = lax.fori_loop(0, tiles, add_tile, (tuple((zero, zero) for _ in range(5)), jnp.zeros((1, LANES), F32)))
    lane = lax.broadcasted_iota(jnp.int32, (16, LANES), 1)
    row16 = lax.broadcasted_iota(jnp.int32, (16, LANES), 0)
    for k in (64, 32, 16, 8, 4, 2, 1):
        acc = tuple(pair_add(a, (roll(a[0], k), roll(a[1], k))) for a in acc)
    high, low = zero, zero
    for q in range(5):
        high = jnp.where(lane == q, acc[q][0], high)
        low = jnp.where(lane == q, acc[q][1], low)

    def body(g, blocks, share):
        st = [s_ref[rows + c] for c in range(3)]
        cut_j = s_ref[rows + 3]
        count = jnp.zeros((8, LANES), F32)
        for b in range(blocks):
            d2 = None
            for c in range(3):
                gap = xr_ref[g, b, rows + c:rows + c + 1, :] - st[c]
                d2 = gap * gap if d2 is None else d2 + gap * gap
            d2 = d2 + EPS
            td = d2 * lax.rsqrt(d2)
            cut_i = xr_ref[g, b, rows + 3:rows + 4, :]
            w = jnp.where(td < cut_j, 0.0625, 0.0) + jnp.where(td < cut_i, 0.0625, 0.0)
            if blocks == 8 and b == 7:
                w = jnp.where(row == 7, w * 0.5, w)
            td_ref[b] = td
            w_ref[b] = w
            count = count + w
        cn_ref[...] += count * share
        for s in range(copies):
            sj = [s_ref[3 * s + c] for c in range(3)]
            to_i = [jnp.zeros((8, LANES), F32) for _ in range(3)]
            to_j = [jnp.zeros((8, LANES), F32) for _ in range(3)]
            score = jnp.zeros((8, LANES), F32)
            for b in range(blocks):
                gap = [xr_ref[g, b, 3 * s + c:3 * s + c + 1, :] - sj[c] for c in range(3)]
                d2 = gap[0] * gap[0] + gap[1] * gap[1] + gap[2] * gap[2] + EPS
                r = lax.rsqrt(d2)
                diff = d2 * r - td_ref[b]
                spread = jnp.abs(diff)
                u = [jnp.tanh(t - spread) for t in HALF_THRESHOLDS]
                w = w_ref[b]
                score = score + w * ((u[0] + u[1]) + (u[2] + u[3]))
                slope = ((u[0] * u[0] + u[1] * u[1]) + (u[2] * u[2] + u[3] * u[3])) - 4.0
                sign = jnp.maximum(jnp.minimum(diff * 1e30, w), -w)
                f = slope * r * sign
                for c in range(3):
                    h = f * gap[c]
                    to_j[c] = to_j[c] + h
                    to_i[c] = to_i[c] + roll(h, 8 * b + 1)
            sc_ref[s] += score * share
            for c in range(3):
                pi_ref[g, 3 * s + c] += to_i[c]
                aj_ref[3 * s + c] -= to_j[c]

    @pl.loop(0, tiles + BAND)
    def _(t):
        j = t + BAND
        aj_ref[...] = jnp.zeros_like(aj_ref)
        for m in range(rows + 4):
            s_ref[m] = pltpu.roll(jnp.broadcast_to(x_ref[j, m:m + 1, :], (8, LANES)), 0, 1, stride=1, stride_axis=0)

        @pl.when(t < tiles)
        def _():
            body(j, 8, 1.0)

        @pl.loop(1, BAND + 1)
        def _(o):
            g = t - o
            owner = jnp.clip(jnp.where(t < tiles, t, g), 0, tiles - 1)
            other = base + jnp.where(t < tiles, g, t)
            hit = jnp.bool_(False)
            for k in range(1, part_ref.shape[1]):
                hit = hit | (part_ref[owner, k] == other)

            @pl.when(hit & ((t < tiles) | (g < tiles)))
            def _():
                body(j - o, 16, jnp.where((t >= tiles) | (g < 0), 0.5, 1.0))

        for m in range(rows):
            a = aj_ref[m]
            for k in (4, 2, 1):
                a = a + roll(roll(a, 8 - k, 0), LANES - k, 1)
            pi_ref[j, m] += jnp.where(row == 0, a, 0.0)

    @pl.loop(0, tiles)
    def _(t):
        sl = pl.ds(pl.multiple_of(t * LANES, LANES), LANES)
        for s in range(copies):
            for c in range(3):
                pull_ref[s, c:c + 1, sl] = jnp.sum(pi_ref[t + BAND, 3 * s + c], axis=0, keepdims=True)

    sums = [jnp.sum(sc_ref[s], keepdims=True) for s in range(copies)]
    sums += [jnp.sum(cn_ref[...], keepdims=True), jnp.sum(total, keepdims=True)]
    column = zero
    for i, value in enumerate(sums):
        column = jnp.where(row16 == i, value, column)
    stat_ref[0] = jnp.where(lane == 5, column, high)
    stat_ref[1] = low


def finish_kernel(stat_ref, noise_ref, pred_ref, true_ref, kind_ref, pull_ref, loss_ref, grad_ref, m_ref, k_ref, *, copies, tiles, atoms):
    rows = 3 * copies
    stats = [stat_ref[0], stat_ref[1]]

    def per_copy(c, q, scale):
        return tuple(stat_ref[part, pl.ds(c, copies, stride=3), :][:, q:q + 1] * scale for part in range(2))

    def shared(r, q, scale):
        return tuple(stats[part][r:r + 1, q:q + 1] * scale for part in range(2))

    def wide(x):
        return tuple(jnp.broadcast_to(v, (copies, LANES)) for v in x)

    weight_sum = jnp.broadcast_to(stats[0][copies + 1:copies + 2, 5:6], (copies, LANES))
    count = jnp.broadcast_to(stats[0][copies:copies + 1, 5:6], (copies, LANES)) * 16.0
    score = jnp.broadcast_to(stats[0][0:copies, 5:6], (copies, LANES)) * 2.0 + 0.5 * count
    pred_sum = [wide(per_copy(c, 3, 2.0)) for c in range(3)]
    true_sum = [wide(shared(rows + c, 3, 2.0)) for c in range(3)]
    pred_mean = [pair_div(x, weight_sum) for x in pred_sum]
    true_mean = [pair_div(x, weight_sum) for x in true_sum]
    cov = [[pair_add(wide(per_copy(c, d, 4.0)), pair_neg(pair_mul(pred_sum[c], true_mean[d]))) for d in range(3)] for c in range(3)]
    ct = {}
    for d in range(3):
        for e in range(d + 1):
            ct[d, e] = pair_add(wide(shared(rows + d, e, 4.0)), pair_neg(pair_mul(true_sum[d], true_mean[e])))
    var = None
    for c in range(3):
        term = pair_add(wide(per_copy(c, 4, 4.0)), pair_neg(pair_mul(pred_sum[c], pred_mean[c])))
        var = term if var is None else pair_add(var, term)

    x = [[cov[c][d][0] for d in range(3)] for c in range(3)]
    frobenius = jnp.sqrt(sum(x[c][d] * x[c][d] for c in range(3) for d in range(3)))
    x = [[x[c][d] / frobenius for d in range(3)] for c in range(3)]

    def sweep(_, flat):
        x = [flat[0:3], flat[3:6], flat[6:9]]
        gram = {}
        for a in range(3):
            for b in range(a + 1):
                gram[a, b] = gram[b, a] = x[a][0] * x[b][0] + x[a][1] * x[b][1] + x[a][2] * x[b][2]
        return tuple(1.5 * x[a][d] - 0.5 * (gram[a, 0] * x[0][d] + gram[a, 1] * x[1][d] + gram[a, 2] * x[2][d])
                     for a in range(3) for d in range(3))

    flat = lax.fori_loop(0, SWEEPS, sweep, tuple(v for line in x for v in line))
    x = [flat[0:3], flat[3:6], flat[6:9]]

    square = var
    nothing = jnp.zeros((copies, LANES), F32)
    for c in range(3):
        for d in range(3):
            square = pair_add(square, pair_mul((-2.0 * x[c][d], nothing), cov[c][d]))
    for d in range(3):
        for e in range(d + 1):
            gram = None
            for c in range(3):
                term = two_prod(x[c][d], x[c][e])
                gram = term if gram is None else pair_add(gram, term)
            if d != e:
                gram = (2.0 * gram[0], 2.0 * gram[1])
            square = pair_add(square, pair_mul(gram, ct[d, e]))

    row = lax.broadcasted_iota(jnp.int32, (copies, LANES), 0)
    noise = nothing
    for s in range(copies):
        noise = jnp.where(row == s, noise_ref[s], noise)
    loss_weight = (noise * noise + SIGMA * SIGMA) / (noise * SIGMA * (noise * SIGMA))
    mean_square = (square[0] + square[1]) / (3.0 * weight_sum)
    loss_ref[...] = loss_weight * mean_square + 1.0 - score / count

    grad_scale = 16.0 * atoms
    for c in range(3):
        for d in range(3):
            m_ref[d, pl.ds(c, copies, stride=3), :] = x[c][d]
        m_ref[3, pl.ds(c, copies, stride=3), :] = pred_mean[c][0]
        m_ref[4, pl.ds(c, copies, stride=3), :] = grad_scale * 2.0 * loss_weight / (3.0 * weight_sum)
        m_ref[5, pl.ds(c, copies, stride=3), :] = grad_scale / count
        k_ref[c:c + 1, :] = true_mean[c][0][0:1]

    @pl.loop(0, tiles)
    def _(t):
        sl = pl.ds(pl.multiple_of(t * LANES, LANES), LANES)
        kind = kind_ref[:, sl]
        weight = jnp.where(kind == 1, 5.0, jnp.where(kind == 2, 10.0, 1.0))
        centred = true_ref[:, sl] - k_ref[0:3, :]
        for s in range(copies):
            r = slice(3 * s, 3 * s + 3)
            target = m_ref[0, r, :] * centred[0:1] + m_ref[1, r, :] * centred[1:2] + m_ref[2, r, :] * centred[2:3] + m_ref[3, r, :]
            deviation = pred_ref[s, :, sl] - target
            grad_ref[s, :, sl] = m_ref[4, r, :] * weight * deviation - m_ref[5, r, :] * pull_ref[s, :, sl]


VMEM = pl.BlockSpec(memory_space=pltpu.VMEM)
SMEM = pl.BlockSpec(memory_space=pltpu.SMEM)


def swap(x, axis, step):
    return lax.ppermute(x, axis, [(i, i ^ step) for i in range(lax.axis_size(axis))])


def shards(coords_pred, coords_true, atom_kind, partners, noise_level):
    copies, _, local = coords_pred.shape
    tiles = partners.shape[0]
    rows = 3 * copies
    window = tiles + 2 * BAND
    size = lax.axis_size("res")
    kind = atom_kind[None]
    base = (lax.axis_index("res") * tiles)[None].astype(jnp.int32)

    def edge(start):
        take = lambda a: lax.slice_in_dim(a, start, start + BAND * LANES, axis=a.ndim - 1)
        cut = jnp.where(take(atom_kind) == 1, 15.0, 7.5).astype(F32)
        return jnp.concatenate([take(coords_pred).reshape(rows, -1) * 0.5, take(coords_true) * 0.5, cut[None]], axis=0)

    forward = [(i, i + 1) for i in range(size - 1)]
    low = lax.ppermute(edge(local - BAND * LANES), "res", forward)
    high = lax.ppermute(edge(0), "res", [(b, a) for a, b in forward])

    pull, stats = pl.pallas_call(
        functools.partial(pair_kernel, copies=copies, tiles=tiles),
        in_specs=[SMEM, SMEM] + [VMEM] * 5,
        out_specs=[VMEM, VMEM],
        out_shape=[jax.ShapeDtypeStruct((copies, 3, local), F32), jax.ShapeDtypeStruct((2, 16, LANES), F32)],
        scratch_shapes=[
            pltpu.VMEM((window, 16, LANES), F32),
            pltpu.VMEM((window, 16, 16, LANES), F32),
            pltpu.VMEM((16, 8, LANES), F32),
            pltpu.VMEM((16, 8, LANES), F32),
            pltpu.VMEM((16, 8, LANES), F32),
            pltpu.VMEM((window, rows, 8, LANES), F32),
            pltpu.VMEM((rows, 8, LANES), F32),
            pltpu.VMEM((copies, 8, LANES), F32),
            pltpu.VMEM((8, LANES), F32),
        ],
        compiler_params=pltpu.CompilerParams(vmem_limit_bytes=40 * 2**20),
        name="pairs",
    )(base, partners, coords_pred, coords_true, kind, low, high)

    step = 1
    while step < size:
        other = swap(stats, "res", step)
        total, error = two_sum(stats[0], other[0])
        stats = jnp.stack([total, (stats[1] + other[1]) + error])
        step *= 2

    loss, grad = pl.pallas_call(
        functools.partial(finish_kernel, copies=copies, tiles=tiles, atoms=local * size),
        in_specs=[VMEM, SMEM] + [VMEM] * 4,
        out_specs=[VMEM, VMEM],
        out_shape=[jax.ShapeDtypeStruct((copies, LANES), F32), jax.ShapeDtypeStruct((copies, 3, local), F32)],
        scratch_shapes=[pltpu.VMEM((6, rows, LANES), F32), pltpu.VMEM((8, LANES), F32)],
        compiler_params=pltpu.CompilerParams(vmem_limit_bytes=40 * 2**20),
        name="finish",
    )(stats, noise_level, coords_pred, coords_true, kind, pull)
    copy_loss = loss[:, 0]
    total = jnp.sum(copy_loss)[None]
    step = 1
    while step < lax.axis_size("samp"):
        total = total + swap(total, "samp", step)
        step *= 2
    mean_loss = total[0] / (copies * lax.axis_size("samp"))
    return copy_loss, mean_loss, grad


def solution(mesh):
    in_specs = (P("samp", None, "res"), P(None, "res"), P("res"), P("res", None), P("samp"))
    out_specs = (P("samp"), P(), P("samp", None, "res"))
    return jax.shard_map(shards, mesh=mesh, in_specs=in_specs, out_specs=out_specs, check_vma=False)
```

time: 521 us -> 74 us (0.14)
  matrix products: 316 us -> 0 us
  other arithmetic: 125 us -> 2.9 us
  blocking collectives: 46.1 us -> 0 us
  Pallas kernels: 0 us -> 33.6 us
  starting transfers between devices: 6.76 us -> 22.8 us
  local copies, waits for them, and re-layouts: 17.8 us -> 2.31 us
  waiting for transfers between devices: 0.01 us -> 9.72 us
    dot_general x62 -> x0, matrix products: 316 us -> none  [the longest x18 305 us: pair_terms(): jnp.einsum('skij,skj->si', factor, far_pred[:, component], precision=prec...]
    reduce_sum x9 -> x1, other arithmetic: 92.9 us -> 0.65 us  [shards(): total = jnp.sum(copy_loss)[None]]
    psum x3 -> x0, blocking collectives: 46.1 us -> none  [the longest x1 21.5 us: shards(): lax.psum((weight_sum, pred_sum, true_sum, cross), 'res')]
    pallas_call x0 -> x2, Pallas kernels: none -> 33.6 us  [the longest x1 31.9 us: shards(): pl.pallas_call(functools.partial(pair_kernel, copies=copies, tiles=tiles)...]
    mul x9 -> x2, other arithmetic: 22.1 us -> 1.44 us  [the longest x1 0.73 us: edge(): take(coords_pred).reshape(rows, -1) * 0.5]
    ppermute x2 -> x7, starting transfers between devices: 6.76 us -> 22.8 us  [the longest x5 16.6 us: swap(): lax.ppermute(x, axis, [(i, i ^ step) for i in range(lax.axis_size(axis))])]
    gather x18 -> x0, local copies, waits for them, and re-layouts: 10.1 us -> none  [the longest x6 3.42 us: visit_group(): jnp.take(far_tiles, partner_tiles - first_tile, axis=1)]
    ppermute x2 -> x7, waiting for transfers between devices: 0.01 us -> 9.72 us  [the longest x5 6.3 us: swap(): lax.ppermute(x, axis, [(i, i ^ step) for i in range(lax.axis_size(axis))])]
  transfers between devices with their start and end apart: 2 -> 7, of which waited for: 0 -> 6; matrix products, arithmetic and copies ran while one was open for 4% -> 1% of each run, Pallas kernels for 0% -> 0%
where the time goes in v1:
time: 74 us; the launch traced here: 75 us
  Pallas kernels  33.6 us (45%)
  starting transfers between devices  22.8 us (31%)
  waiting for transfers between devices  9.72 us (13%)
  between operations  3.8 us (5%)
  other arithmetic  2.9 us (4%)
  local copies, waits for them, and re-layouts  2.31 us (3%)
    pallas_call x1, Pallas kernels, shards(): pl.pallas_call(functools.partial(pair_kernel, copies=copies, tiles=tiles)...  31.9 us
    ppermute x5, starting transfers between devices, swap(): lax.ppermute(x, axis, [(i, i ^ step) for i in range(lax.axis_size(axis))])  16.6 us
    ppermute x5, waiting for transfers between devices, swap(): lax.ppermute(x, axis, [(i, i ^ step) for i in range(lax.axis_size(axis))])  6.3 us
    ppermute x1, starting transfers between devices, shards(): low = lax.ppermute(edge(local - BAND * LANES), 'res', forward)  4.84 us
    ppermute x1, waiting for transfers between devices, shards(): high = lax.ppermute(edge(0), 'res', [(b, a) for a, b in forward])  3.42 us
    unnamed x13, local copies, waits for them, and re-layouts  2.28 us
    pallas_call x1, Pallas kernels, shards(): pl.pallas_call(functools.partial(finish_kernel, copies=copies, tiles=tile...  1.63 us
  transfers between devices with their start and end apart: 7, of which 6 were waited for; matrix products, arithmetic and copies ran while one was open for 1% of the time, Pallas kernels for 0%

profile of v1, /device:TPU:0, one launch (start us, length us, event | category | flops | bytes accessed | tf_op | source)
XLA Modules:
  0.0 75.0 jit_solution(18086337518860202869)
XLA Ops:
  0.6 0.0 copy-start.3
  0.6 0.7 compare_select_fusion
  1.4 0.7 slice_multiply_fusion.2
  2.1 0.7 slice_multiply_fusion
  2.9 4.8 %collective-permute-start = (f32[16,256]{1,0:T(8,128)S(1)}, f32[16,256]{1,0:T(8,128)S(1)}, u32[]{:S(2)}, u32[]{:S(2)}) collective-permute-start(f32[16,256]{1,0:T(8,128)S(1)} %pad_maximum_fusion), channel_id=1, source_target_pairs={{0,4},{4,8},{8,12},{12,16},{16,20},{20,24},{24,28},{1,5},{5,9},{9,... | collective-permute-start | bytes 49160 | tf_op jit(solution)/shard_map/ppermute | solution.py:320
  7.8 1.3 %collective-permute-start.1 = (f32[16,256]{1,0:T(8,128)S(1)}, f32[16,256]{1,0:T(8,128)S(1)}, u32[]{:S(2)}, u32[]{:S(2)}) collective-permute-start(f32[16,256]{1,0:T(8,128)S(1)} %pad_maximum_fusion.1), channel_id=1, source_target_pairs={{4,0},{8,4},{12,8},{16,12},{20,16},{24,20},{28,24},{5,1},{9,5},{13... | collective-permute-start | bytes 49160 | tf_op jit(solution)/shard_map/ppermute | solution.py:321
  9.1 0.0 copy-done.3
  9.1 0.0 copy-start
  9.1 0.1 copy.17.pred_ref
  9.2 0.0 copy-start.4
  9.2 0.0 copy-start.1
  9.2 0.7 copy-done.4
  9.9 0.1 copy.16.part_ref
  10.0 0.0 collective-permute-done.lo_ref
  10.0 3.4 %collective-permute-done.1.hi_ref = f32[16,256]{1,0:T(8,128)S(1)} collective-permute-done((f32[16,256]{1,0:T(8,128)S(1)}, f32[16,256]{1,0:T(8,128)S(1)}, u32[]{:S(2)}, u32[]{:S(2)}) %collective-permute-start.1) | collective-permute-done | bytes 16416 | tf_op jit(solution)/shard_map/ppermute | solution.py:321
  13.4 0.0 copy-done
  13.4 0.0 copy-done.1
  13.4 31.9 %pairs.1 = (f32[4,3,3072]{2,1,0:T(4,128)S(1)}, f32[2,16,128]{2,1,0:T(8,128)S(1)}) custom-call(s32[1]{0:T(128)} %bitcast.base_ref, s32[24,5]{1,0:T(8,128)S(1)} %copy.16.part_ref, f32[4,3,3072]{2,1,0:T(4,128)S(1)} %copy.17.pred_ref, f32[3,3072]{1,0:T(4,128)S(1)} %copy-done, s32[1,3072]{1,0:T(1,128)S(1)} %bitcast.6, f32[16,256]{1,0:T(8,128)S(1)} %collective-permute-done.lo_ref, ...), custom_call_target="tpu_custom_call" | custom-call | tf_op jit(solution)/shard_map/pairs/pallas_call | solution.py:323
  45.3 4.0 %collective-permute-start.2 = (f32[2,16,128]{2,1,0:T(8,128)S(1)}, f32[2,16,128]{2,1,0:T(8,128)S(1)}, u32[]{:S(2)}, u32[]{:S(2)}) collective-permute-start(f32[2,16,128]{2,1,0:T(8,128)S(1)} %get-tuple-element.7), channel_id=1, source_target_pairs={{0,4},{4,0},{8,12},{12,8},{16,20},{20,16},{24,28},{28,24},{1,5},{5... | collective-permute-start | bytes 49160 | tf_op jit(solution)/shard_map/ppermute | solution.py:302
  49.4 1.7 %collective-permute-done.2 = f32[2,16,128]{2,1,0:T(8,128)S(1)} collective-permute-done((f32[2,16,128]{2,1,0:T(8,128)S(1)}, f32[2,16,128]{2,1,0:T(8,128)S(1)}, u32[]{:S(2)}, u32[]{:S(2)}) %collective-permute-start.2) | collective-permute-done | bytes 16416 | tf_op jit(solution)/shard_map/ppermute | solution.py:302
  51.1 2.8 %collective-permute-start.3 = (f32[2,16,128]{2,1,0:T(8,128)S(1)}, f32[2,16,128]{2,1,0:T(8,128)S(1)}, u32[]{:S(2)}, u32[]{:S(2)}) collective-permute-start(f32[2,16,128]{2,1,0:T(8,128)S(1)} %pad_maximum_fusion.2), channel_id=1, source_target_pairs={{0,8},{4,12},{8,0},{12,4},{16,24},{20,28},{24,16},{28,20},{1,9},{5... | collective-permute-start | bytes 49160 | tf_op jit(solution)/shard_map/ppermute | solution.py:302
  53.9 1.7 %collective-permute-done.3 = f32[2,16,128]{2,1,0:T(8,128)S(1)} collective-permute-done((f32[2,16,128]{2,1,0:T(8,128)S(1)}, f32[2,16,128]{2,1,0:T(8,128)S(1)}, u32[]{:S(2)}, u32[]{:S(2)}) %collective-permute-start.3) | collective-permute-done | bytes 16416 | tf_op jit(solution)/shard_map/ppermute | solution.py:302
  55.7 6.8 %collective-permute-start.4 = (f32[2,16,128]{2,1,0:T(8,128)S(1)}, f32[2,16,128]{2,1,0:T(8,128)S(1)}, u32[]{:S(2)}, u32[]{:S(2)}) collective-permute-start(f32[2,16,128]{2,1,0:T(8,128)S(1)} %pad_maximum_fusion.3), channel_id=1, source_target_pairs={{0,16},{4,20},{8,24},{12,28},{16,0},{20,4},{24,8},{28,12},{1,17},{... | collective-permute-start | bytes 49160 | tf_op jit(solution)/shard_map/ppermute | solution.py:302
  62.5 1.7 %collective-permute-done.4 = f32[2,16,128]{2,1,0:T(8,128)S(1)} collective-permute-done((f32[2,16,128]{2,1,0:T(8,128)S(1)}, f32[2,16,128]{2,1,0:T(8,128)S(1)}, u32[]{:S(2)}, u32[]{:S(2)}) %collective-permute-start.4) | collective-permute-done | bytes 16416 | tf_op jit(solution)/shard_map/ppermute | solution.py:302
  64.3 0.6 copy-done.2
  64.9 1.6 %finish.1 = (f32[4,128]{1,0:T(4,128)S(1)}, f32[4,3,3072]{2,1,0:T(4,128)S(1)}) custom-call(f32[2,16,128]{2,1,0:T(8,128)S(1)} %pad_maximum_fusion.4.stat_ref, f32[4]{0:T(128)S(1)} %copy-done.2, f32[4,3,3072]{2,1,0:T(4,128)S(1)} %copy.17.pred_ref, f32[3,3072]{1,0:T(4,128)S(1)} %copy-done, s32[1,3072]{1,0:T(1,128)S(1)} %bitcast.7, ...), custom_call_target="tpu_custom_call" | custom-call | tf_op jit(solution)/shard_map/finish/pallas_call | solution.py:350
  66.6 0.7 slice_reduce_fusion
  67.2 0.0 collective-permute-start.5
  67.2 0.8 %copy.19 = f32[4,3,3072]{2,0,1:T(4,128)} copy(f32[4,3,3072]{2,1,0:T(4,128)S(1)} %get-tuple-element.16) | data formatting | bytes 294912
  68.0 0.5 collective-permute-done.5
  69.7 2.9 %collective-permute-start.6 = (f32[1]{0:T(128)}, f32[1]{0:T(128)}, u32[]{:S(2)}, u32[]{:S(2)}) collective-permute-start(f32[1]{0:T(128)} %add.84), channel_id=1, source_target_pairs={{0,2},{1,3},{2,0},{3,1},{4,6},{5,7},{6,4},{7,5},{8,10},{9,11},{10,... | collective-permute-start | bytes 20 | tf_op jit(solution)/shard_map/ppermute | solution.py:302
  72.6 0.7 collective-permute-done.6
  (13 shorter events, 0.1 us)
Async XLA Ops:
  0.6 8.4 %copy-start.3 = (f32[4,3,3072]{2,0,1:T(4,128)S(1)}, f32[4,3,3072]{2,0,1:T(4,128)}, u32[]{:S(2)}) copy-start(f32[4,3,3072]{2,0,1:T(4,128)} %param.5) | copy-start | bytes 442372
  2.9 7.1 %collective-permute-start = (f32[16,256]{1,0:T(8,128)S(1)}, f32[16,256]{1,0:T(8,128)S(1)}, u32[]{:S(2)}, u32[]{:S(2)}) collective-permute-start(f32[16,256]{1,0:T(8,128)S(1)} %pad_maximum_fusion), channel_id=1, source_target_pairs={{0,4},{4,8},{8,12},{12,16},{16,20},{20,24},{24,28},{1,5},{5,9},{9,... | collective-permute-start | bytes 49160 | tf_op jit(solution)/shard_map/ppermute | solution.py:320
  7.8 5.6 %collective-permute-start.1 = (f32[16,256]{1,0:T(8,128)S(1)}, f32[16,256]{1,0:T(8,128)S(1)}, u32[]{:S(2)}, u32[]{:S(2)}) collective-permute-start(f32[16,256]{1,0:T(8,128)S(1)} %pad_maximum_fusion.1), channel_id=1, source_target_pairs={{4,0},{8,4},{12,8},{16,12},{20,16},{24,20},{28,24},{5,1},{9,5},{13... | collective-permute-start | bytes 49160 | tf_op jit(solution)/shard_map/ppermute | solution.py:321
  9.1 4.3 %copy-start = (f32[3,3072]{1,0:T(4,128)S(1)}, f32[3,3072]{1,0:T(4,128)}, u32[]{:S(2)}) copy-start(f32[3,3072]{1,0:T(4,128)} %true_ref.3) | copy-start | bytes 110596
  9.2 0.7 copy-start.4
  9.2 4.2 %copy-start.1 = (s32[3072]{0:T(1024)S(1)}, s32[3072]{0:T(1024)}, u32[]{:S(2)}) copy-start(s32[3072]{0:T(1024)} %param.7) | copy-start | bytes 36868
  45.3 5.8 %collective-permute-start.2 = (f32[2,16,128]{2,1,0:T(8,128)S(1)}, f32[2,16,128]{2,1,0:T(8,128)S(1)}, u32[]{:S(2)}, u32[]{:S(2)}) collective-permute-start(f32[2,16,128]{2,1,0:T(8,128)S(1)} %get-tuple-element.7), channel_id=1, source_target_pairs={{0,4},{4,0},{8,12},{12,8},{16,20},{20,16},{24,28},{28,24},{1,5},{5... | collective-permute-start | bytes 49160 | tf_op jit(solution)/shard_map/ppermute | solution.py:302
  51.1 4.6 %collective-permute-start.3 = (f32[2,16,128]{2,1,0:T(8,128)S(1)}, f32[2,16,128]{2,1,0:T(8,128)S(1)}, u32[]{:S(2)}, u32[]{:S(2)}) collective-permute-start(f32[2,16,128]{2,1,0:T(8,128)S(1)} %pad_maximum_fusion.2), channel_id=1, source_target_pairs={{0,8},{4,12},{8,0},{12,4},{16,24},{20,28},{24,16},{28,20},{1,9},{5... | collective-permute-start | bytes 49160 | tf_op jit(solution)/shard_map/ppermute | solution.py:302
  55.7 8.6 %collective-permute-start.4 = (f32[2,16,128]{2,1,0:T(8,128)S(1)}, f32[2,16,128]{2,1,0:T(8,128)S(1)}, u32[]{:S(2)}, u32[]{:S(2)}) collective-permute-start(f32[2,16,128]{2,1,0:T(8,128)S(1)} %pad_maximum_fusion.3), channel_id=1, source_target_pairs={{0,16},{4,20},{8,24},{12,28},{16,0},{20,4},{24,8},{28,12},{1,17},{... | collective-permute-start | bytes 49160 | tf_op jit(solution)/shard_map/ppermute | solution.py:302
  64.3 0.7 copy-start.2
  67.2 1.2 %collective-permute-start.5 = (f32[1]{0:T(128)}, f32[1]{0:T(128)}, u32[]{:S(2)}, u32[]{:S(2)}) collective-permute-start(f32[1]{0:T(128)} %bitcast.4), channel_id=1, source_target_pairs={{0,1},{1,0},{2,3},{3,2},{4,5},{5,4},{6,7},{7,6},{8,9},{9,8},{10,11... | collective-permute-start | bytes 20 | tf_op jit(solution)/shard_map/ppermute | solution.py:302
  69.7 3.6 %collective-permute-start.6 = (f32[1]{0:T(128)}, f32[1]{0:T(128)}, u32[]{:S(2)}, u32[]{:S(2)}) collective-permute-start(f32[1]{0:T(128)} %add.84), channel_id=1, source_target_pairs={{0,2},{1,3},{2,0},{3,1},{4,6},{5,7},{6,4},{7,5},{8,10},{9,11},{10,... | collective-permute-start | bytes 20 | tf_op jit(solution)/shard_map/ppermute | solution.py:302

commit v2 on v1

v2 whole, which is shorter than its diff:
```python
import functools

import jax
import jax.numpy as jnp
from jax import lax
from jax.experimental import pallas as pl
from jax.experimental.pallas import tpu as pltpu
from jax.sharding import PartitionSpec as P

LANES = 128
BAND = 2
SWEEPS = 20
SIGMA = 16.0
HALF_THRESHOLDS = (0.25, 0.5, 1.0, 2.0)
EPS = 0.25e-6
F32 = jnp.float32
BF16 = jnp.bfloat16


def roll(x, shift, axis=1):
    return pltpu.roll(x, shift, axis)


def two_sum(a, b):
    s = a + b
    t = s - a
    return s, (a - (s - t)) + (b - t)


def two_prod(a, b):
    def halves(x):
        t = x * 4097.0
        h = t - (t - x)
        return h, x - h

    p = a * b
    ah, al = halves(a)
    bh, bl = halves(b)
    return p, ((ah * bh - p) + ah * bl + al * bh) + al * bl


def pair_add(x, y):
    s, e = two_sum(x[0], y[0])
    return two_sum(s, e + (x[1] + y[1]))


def pair_neg(x):
    return -x[0], -x[1]


def pair_mul(x, y):
    p, e = two_prod(x[0], y[0])
    return two_sum(p, e + (x[0] * y[1] + x[1] * y[0]))


def pair_div(x, w):
    q = x[0] / w
    p, e = two_prod(q, w)
    return two_sum(q, (((x[0] - p) - e) + x[1]) / w)


def dot(a, b):
    return jnp.dot(a, b, preferred_element_type=F32)


def dot_nt(a, b):
    return lax.dot_general(a, b, (((1,), (1,)), ((), ())), preferred_element_type=F32)


def split3(x):
    a = x.astype(BF16).astype(F32)
    rest = x - a
    b = rest.astype(BF16).astype(F32)
    return a, b, (rest - b).astype(BF16).astype(F32)


def stack(a, b, axis):
    return jnp.concatenate([a, b], axis=axis)


def listed(part_ref, owner, other):
    hit = jnp.bool_(False)
    for k in range(1, part_ref.shape[1]):
        hit = hit | (part_ref[owner, k] == other)
    return hit


class Engine:
    names = ("v", "cut", "centre", "left", "point", "right", "true", "weight", "d", "f", "acc", "score", "count", "tri", "items")

    def __init__(self, copies, refs):
        self.copies = copies
        self.twos = copies // 2
        for name, ref in zip(self.names, refs):
            setattr(self, name, ref)

    @staticmethod
    def scratch(tiles, copies, items):
        n, twos = tiles + 1, copies // 2
        return [
            pltpu.VMEM((n, copies + 1, 8, LANES), F32),
            pltpu.VMEM((n, 1, LANES), F32),
            pltpu.VMEM((n, copies + 1, 8, LANES), F32),
            pltpu.VMEM((n, twos + 1, LANES, LANES), BF16),
            pltpu.VMEM((n, twos, 64, 2 * LANES), BF16),
            [pltpu.VMEM((2, twos + 1, LANES, 2 * LANES), BF16)] * 2,
            [pltpu.VMEM((LANES, LANES), F32)] * 2,
            [pltpu.VMEM((LANES, LANES), F32)] * 2,
            [pltpu.VMEM((twos + 1, LANES, 2 * LANES), F32)] * 2,
            [pltpu.VMEM((twos, 2 * LANES, 2 * LANES), BF16)] * 2,
            pltpu.VMEM((n, copies, 8, LANES), F32),
            pltpu.VMEM((copies, 8, LANES), F32),
            pltpu.VMEM((8, LANES), F32),
            pltpu.VMEM((2, LANES, LANES), BF16),
            pltpu.SMEM((4, items + 2), jnp.int32),
        ]

    def begin(self, tiles):
        for ref in [self.v, self.acc, self.score, self.count, *self.right, *self.f]:
            ref[...] = jnp.zeros_like(ref)
        self.cut[tiles] = jnp.zeros((1, LANES), F32)
        row = lax.broadcasted_iota(jnp.int32, (LANES, LANES), 0)
        lane = lax.broadcasted_iota(jnp.int32, (LANES, LANES), 1)
        self.tri[0] = jnp.where(lane > row, 1.0, 0.0).astype(BF16)
        self.tri[1] = jnp.where(lane < row, 1.0, 0.0).astype(BF16)
        pick = jnp.where(row == 7, 1.0, 0.0).astype(BF16)
        for ref in self.right:
            for k in range(2):
                ref[k, self.twos, :, LANES:] = pick

    @staticmethod
    def unit(k):
        return jnp.where(lax.broadcasted_iota(jnp.int32, (8, LANES), 0) == k, 1.0, 0.0)

    def prep(self, t):
        groups = []
        for s in range(self.copies + 1):
            v = self.v[t, s]
            centre = jnp.broadcast_to(jnp.sum(v, axis=1, keepdims=True) * (1.0 / LANES), (8, LANES))
            self.centre[t, s] = centre
            y = v - centre
            norm = jnp.sum(y * y, axis=0, keepdims=True)
            x = y + (self.unit(4) + EPS * self.unit(5)) + norm * self.unit(3)
            if s == self.copies:
                x = x + self.unit(7) * self.cut[t]
            a, b, c = split3(x)
            groups.append(jnp.concatenate([a, a, b, a, b, c, b, c], axis=0))
            if s < self.copies:
                a, b, c = split3(v + self.unit(3))
                p = jnp.concatenate([a, b, c, jnp.zeros_like(a)], axis=0).astype(BF16)
                q = 32 * (s % 2)
                self.point[t, s // 2, q:q + 32, :LANES] = p
                self.point[t, s // 2, q:q + 32, LANES:] = p
        groups.append(jnp.zeros((64, LANES), F32))
        for h in range(self.twos + 1):
            self.left[t, h] = stack(groups[2 * h], groups[2 * h + 1], 0).T.astype(BF16)

    def build(self, slot, k, g, j):
        for s in range(self.copies + 1):
            y = self.v[j, s] - self.centre[g, s]
            norm = jnp.sum(y * y, axis=0, keepdims=True)
            a, b, c = split3((self.unit(3) + self.unit(5)) - 2.0 * y + norm * self.unit(4))
            q, m = 64 * (s % 2), LANES * (s % 2)
            self.right[slot][k, s // 2, q:q + 64, m:m + LANES] = jnp.concatenate([a, b, a, c, b, a, c, b], axis=0).astype(BF16)

    def squares(self, slot, k, g, h):
        return dot(self.left[g, h], self.right[slot][k, h])

    def weigh(self, slot, cut_j, live, share):
        total = jnp.zeros((8, LANES), F32)
        for b in range(16):
            k = slice(8 * b, 8 * b + 8)
            d2 = jnp.maximum(self.d[slot][self.twos, k, :LANES], EPS)
            dist = d2 * lax.rsqrt(d2)
            w = jnp.where(dist < cut_j(k), 0.0625, 0.0) + jnp.where(dist < self.d[slot][self.twos, k, LANES:], 0.0625, 0.0)
            if live is not None:
                w = w * live(k)
            self.true[slot][k, :] = dist
            self.weight[slot][k, :] = w
            total = total + w
        self.count[...] += total * share

    def factor(self, slot, share):
        for s in range(self.copies):
            h, m = s // 2, LANES * (s % 2)
            score = jnp.zeros((8, LANES), F32)
            for q in range(8):
                k = slice(16 * q, 16 * q + 16)
                d2 = jnp.maximum(self.d[slot][h, k, m:m + LANES], EPS)
                r = lax.rsqrt(d2)
                diff = d2 * r - self.true[slot][k, :]
                spread = jnp.abs(diff)
                u = [jnp.tanh(t - spread) for t in HALF_THRESHOLDS]
                w = self.weight[slot][k, :]
                z = w * ((u[0] + u[1]) + (u[2] + u[3]))
                score = score + z[:8] + z[8:]
                slope = ((u[0] * u[0] + u[1] * u[1]) + (u[2] * u[2] + u[3] * u[3])) - 4.0
                f = slope * r * jnp.maximum(jnp.minimum(diff * 1e30, w), -w)
                high = f.astype(BF16)
                self.f[slot][h, k, m:m + LANES] = high
                self.f[slot][h, LANES + 16 * q:LANES + 16 * q + 16, m:m + LANES] = (f - high.astype(F32)).astype(BF16)
            self.score[s] += score * share

    @staticmethod
    def fold(z):
        return [z[k:k + 8, m:m + LANES] + z[k + 8:k + 16, m:m + LANES] + z[k + 16:k + 24, m:m + LANES] for k, m in ((0, 0), (32, LANES))]

    def along_j(self, p, f):
        return self.fold(dot(p, f))

    def along_i(self, p, f):
        one = stack(f[:LANES, :LANES], f[LANES:, :LANES], 1)
        two = stack(f[:LANES, LANES:], f[LANES:, LANES:], 1)
        return self.fold(dot_nt(p, stack(one, two, 0)))

    def cross_build(self, item, slot):
        self.build(slot, 0, item[0], item[1])

    def cross_measure(self, item, slot):
        for h in [self.twos, *range(self.twos)]:
            self.d[slot][h] = self.squares(slot, 0, item[0], h)

    def cross_factor(self, item, slot):
        share = item[2].astype(F32) * 0.5
        cut = self.cut[item[1]]
        self.weigh(slot, lambda k: cut, None, share)
        self.factor(slot, share)

    def cross_collect(self, item, slot):
        g, j = item[0], item[1]
        for h in range(self.twos):
            f = self.f[slot][h]
            x = self.along_j(self.point[g, h], f)
            y = self.along_i(self.point[j, h], f)
            for k in range(2):
                self.acc[j, 2 * h + k] += x[k]
                self.acc[g, 2 * h + k] += y[k]

    def self_build(self, item, slot):
        for k in range(2):
            self.build(slot, k, item[k], item[k])

    def self_measure(self, item, slot):
        row = lax.broadcasted_iota(jnp.int32, (LANES, 2 * LANES), 0)
        lane = lax.broadcasted_iota(jnp.int32, (LANES, 2 * LANES), 1) % LANES
        for h in [self.twos, *range(self.twos)]:
            self.d[slot][h] = jnp.where(lane > row, self.squares(slot, 0, item[0], h), self.squares(slot, 1, item[1], h))

    def self_factor(self, item, slot):
        row = lax.broadcasted_iota(jnp.int32, (8, LANES), 0)
        lane = lax.broadcasted_iota(jnp.int32, (8, LANES), 1)
        cut = [self.cut[item[0]], self.cut[item[1]]]
        self.weigh(slot, lambda k: jnp.where(lane > row + k.start, cut[0], cut[1]), lambda k: jnp.where(lane == row + k.start, 0.0, 1.0), 1.0)
        self.factor(slot, 1.0)

    def self_collect(self, item, slot):
        for h in range(self.twos):
            f = self.f[slot][h]
            for k in range(2):
                mask = stack(self.tri[k], self.tri[k], 0)
                part = f * stack(mask, mask, 1)
                x = self.along_j(self.point[item[k], h], part)
                y = self.along_i(self.point[item[k], h], part)
                for q in range(2):
                    self.acc[item[k], 2 * h + q] += x[q] + y[q]

    def half(self, kind, items, slot):
        last, now, soon, later = items
        getattr(self, kind + "_collect")(last, 1 - slot)
        getattr(self, kind + "_measure")(soon, 1 - slot)
        getattr(self, kind + "_build")(later, slot)
        getattr(self, kind + "_factor")(now, slot)

    def begin_list(self, kind, item, n):
        getattr(self, kind + "_build")(item(0), 0)
        getattr(self, kind + "_measure")(item(0), 0)
        getattr(self, kind + "_build")(item(jnp.minimum(1, n - 1)), 1)

    def pairs_of_items(self, kind, item, n, dummy):
        def at(p):
            return tuple(jnp.where(p < 0, dummy, z) for z in item(jnp.clip(p, 0, n - 1)))

        @pl.loop(0, n // 2)
        def _(i):
            p = 2 * i
            for slot in range(2):
                self.half(kind, [at(p + slot - 1), at(p + slot), at(p + slot + 1), at(p + slot + 2)], slot)

    def pull(self, t, s):
        a = self.acc[t, s]
        return (self.v[t, s] * a[3:4] - a)[0:3]

    def scores(self, weight_total):
        rows = [jnp.sum(self.score[s], axis=0, keepdims=True) for s in range(self.copies)]
        rows += [jnp.sum(self.count[...], axis=0, keepdims=True), weight_total]
        total = jnp.zeros((8, LANES), F32)
        for k, x in enumerate(rows):
            total = total + x * self.unit(k)
        return jnp.broadcast_to(jnp.sum(total, axis=1, keepdims=True), (8, LANES))


def finish_list(e, item, n, dummy):
    @pl.when(n % 2 == 1)
    def _():
        before = tuple(jnp.where(n > 1, z, dummy) for z in item(jnp.maximum(n - 2, 0)))
        e.cross_collect(before, 1)
        e.cross_factor(item(n - 1), 0)
        e.cross_collect(item(n - 1), 0)

    @pl.when(n % 2 == 0)
    def _():
        e.cross_collect(item(n - 1), 1)


def interior_kernel(base_ref, part_ref, pred_ref, true_ref, kind_ref, pull_ref, stat_ref, x_ref, mom_ref, *scratch, copies, tiles):
    e = Engine(copies, scratch)
    base = base_ref[0]
    rows = 3 * copies
    e.begin(tiles)
    x_ref[...] = jnp.zeros_like(x_ref)
    mom_ref[...] = jnp.zeros_like(mom_ref)

    def scan(t, n):
        for o in range(1, BAND + 1):
            hit = listed(part_ref, t, base + t - o) & (t >= o)

            @pl.when(hit)
            def _(n=n, o=o):
                e.items[0, n] = t - o
                e.items[1, n] = t
                e.items[2, n] = 2

            n = n + jnp.where(hit, 1, 0)
        return n

    n = lax.fori_loop(0, tiles, scan, jnp.int32(0))
    unroll = next(u for u in (6, 4, 3, 2, 1) if tiles % u == 0)

    @pl.loop(0, tiles // unroll)
    def _(m):
        for q in range(unroll):
            t = m * unroll + q
            sl = pl.ds(pl.multiple_of(t * LANES, LANES), LANES)
            kind = kind_ref[:, sl]
            weight = jnp.where(kind == 1, 5.0, jnp.where(kind == 2, 10.0, 1.0))
            for s in range(copies):
                v = pred_ref[s, :, sl] * 0.5
                e.v[t, s, 0:3, :] = v
                x_ref[q, 3 * s:3 * s + 3, :] = v
            v = true_ref[:, sl] * 0.5
            e.v[t, copies, 0:3, :] = v
            x_ref[q, rows:rows + 3, :] = v
            e.cut[t] = jnp.where(kind == 1, 15.0, 7.5)
            x = x_ref[q]
            wx = x * weight
            terms = [wx * x[rows + c:rows + c + 1] for c in range(3)] + [wx, wx * x]
            for i, term in enumerate(terms):
                total, error = two_sum(mom_ref[0, i], term)
                mom_ref[0, i] = total
                mom_ref[1, i] += error
            mom_ref[0, 5, 0:1, :] += weight
            e.prep(t)

    e.prep(tiles)

    blank = jnp.zeros((LANES - 80, LANES), F32)
    high, low = (jnp.concatenate([mom_ref[part, i] for i in range(5)] + [blank], axis=0).T for part in range(2))
    sums = [(high[8 * k:8 * k + 8], low[8 * k:8 * k + 8]) for k in range(16)]
    while len(sums) > 1:
        sums = [pair_add(a, b) for a, b in zip(sums[::2], sums[1::2])]
    sums = sums[0]
    for k in (4, 2, 1):
        sums = pair_add(sums, (roll(sums[0], k, 0), roll(sums[1], k, 0)))
    stat_ref[0] = sums[0] * e.unit(0) + sums[1] * e.unit(1)

    def twin(i):
        return 2 * i, 2 * i + 1

    half = tiles // 2
    e.begin_list("self", twin, half)
    e.pairs_of_items("self", twin, half, tiles)

    def item(i):
        return e.items[0, i], e.items[1, i], e.items[2, i]

    @pl.when(n == 0)
    def _():
        for k, z in enumerate((tiles, tiles, 0)):
            e.items[k, 0] = z

    n = jnp.maximum(n, 1)
    e.begin_list("cross", item, n)
    e.self_collect(twin(half - 1), 1)
    e.pairs_of_items("cross", item, n, tiles)
    finish_list(e, item, n, tiles)

    @pl.loop(0, tiles)
    def _(t):
        sl = pl.ds(pl.multiple_of(t * LANES, LANES), LANES)
        for s in range(copies):
            pull_ref[s, :, sl] = e.pull(t, s)

    stat_ref[1] = e.scores(mom_ref[0, 5, 0:1, :])


def edge_kernel(base_ref, part_ref, pred_ref, true_ref, kind_ref, low_ref, high_ref, stat_ref, pull_ref, out_ref, *scratch, copies, tiles):
    e = Engine(copies, scratch)
    base = base_ref[0]
    span = BAND * LANES
    local = tiles * LANES
    window = 4 * BAND
    e.begin(window)
    for q in range(BAND):
        sl = slice(q * LANES, q * LANES + LANES)
        for ref, t in ((low_ref, q), (high_ref, 3 * BAND + q)):
            for s in range(copies + 1):
                e.v[t, s, 0:3, :] = ref[3 * s:3 * s + 3, sl]
            e.cut[t] = ref[3 * copies + 3:3 * copies + 4, sl]
        for start, t in ((0, BAND + q), (local - span, 2 * BAND + q)):
            sl = slice(start + q * LANES, start + q * LANES + LANES)
            for s in range(copies):
                e.v[t, s, 0:3, :] = pred_ref[s, :, sl] * 0.5
            e.v[t, copies, 0:3, :] = true_ref[:, sl] * 0.5
            e.cut[t] = jnp.where(kind_ref[:, sl] == 1, 15.0, 7.5)
    n = jnp.int32(0)
    for o in range(1, BAND + 1):
        for k in range(o):
            for owner, other, g, j in ((k, k - o, BAND + k - o, BAND + k), (tiles - 1 - k, tiles - 1 - k + o, 3 * BAND - 1 - k, 3 * BAND - 1 - k + o)):
                hit = listed(part_ref, owner, base + other)

                @pl.when(hit)
                def _(n=n, g=g, j=j):
                    e.items[0, n] = g
                    e.items[1, n] = j
                    e.items[2, n] = 1

                n = n + jnp.where(hit, 1, 0)

    def item(i):
        return e.items[0, i], e.items[1, i], e.items[2, i]

    @pl.when(n > 0)
    def _():
        for t in range(window + 1):
            e.prep(t)
        e.begin_list("cross", item, n)
        e.pairs_of_items("cross", item, n, window)
        finish_list(e, item, n, window)

    for t in range(2 * BAND):
        for s in range(copies):
            pull_ref[s, :, t * LANES:(t + 1) * LANES] = e.pull(BAND + t, s)
    out_ref[0] = stat_ref[0]
    out_ref[1] = stat_ref[1] + e.scores(jnp.zeros((1, LANES), F32))


def finish_kernel(stat_ref, noise_ref, pred_ref, true_ref, kind_ref, pull_ref, edge_ref, loss_ref, grad_ref, m_ref, k_ref, s_ref, *, copies, tiles, atoms):
    rows = 3 * copies
    column = stack(stat_ref[0], jnp.zeros((LANES - 8, LANES), F32), 0).T
    for part in range(2):
        s_ref[part] = jnp.broadcast_to(column[:, part:part + 1], (LANES, LANES))

    def per_copy(c, q, scale):
        return tuple(s_ref[part, pl.ds(16 * q + c, copies, stride=3), :] * scale for part in range(2))

    def shared(r, q, scale):
        return tuple(s_ref[part, 16 * q + r:16 * q + r + 1, :] * scale for part in range(2))

    def wide(x):
        return tuple(jnp.broadcast_to(v, (copies, LANES)) for v in x)

    weight_sum = jnp.broadcast_to(stat_ref[1, copies + 1:copies + 2, :], (copies, LANES))
    count = jnp.broadcast_to(stat_ref[1, copies:copies + 1, :], (copies, LANES)) * 16.0
    score = stat_ref[1, 0:copies, :] * 2.0 + 0.5 * count
    pred_sum = [wide(per_copy(c, 3, 2.0)) for c in range(3)]
    true_sum = [wide(shared(rows + c, 3, 2.0)) for c in range(3)]
    pred_mean = [pair_div(x, weight_sum) for x in pred_sum]
    true_mean = [pair_div(x, weight_sum) for x in true_sum]
    cov = [[pair_add(wide(per_copy(c, d, 4.0)), pair_neg(pair_mul(pred_sum[c], true_mean[d]))) for d in range(3)] for c in range(3)]
    ct = {}
    for d in range(3):
        for e in range(d + 1):
            ct[d, e] = pair_add(wide(shared(rows + d, e, 4.0)), pair_neg(pair_mul(true_sum[d], true_mean[e])))
    var = None
    for c in range(3):
        term = pair_add(wide(per_copy(c, 4, 4.0)), pair_neg(pair_mul(pred_sum[c], pred_mean[c])))
        var = term if var is None else pair_add(var, term)

    x = [[cov[c][d][0] for d in range(3)] for c in range(3)]
    frobenius = jnp.sqrt(sum(x[c][d] * x[c][d] for c in range(3) for d in range(3)))
    x = [[x[c][d] / frobenius for d in range(3)] for c in range(3)]

    def sweep(_, flat):
        x = [flat[0:3], flat[3:6], flat[6:9]]
        gram = {}
        for a in range(3):
            for b in range(a + 1):
                gram[a, b] = gram[b, a] = x[a][0] * x[b][0] + x[a][1] * x[b][1] + x[a][2] * x[b][2]
        return tuple(1.5 * x[a][d] - 0.5 * (gram[a, 0] * x[0][d] + gram[a, 1] * x[1][d] + gram[a, 2] * x[2][d])
                     for a in range(3) for d in range(3))

    flat = lax.fori_loop(0, SWEEPS, sweep, tuple(v for line in x for v in line))
    x = [flat[0:3], flat[3:6], flat[6:9]]

    square = var
    nothing = jnp.zeros((copies, LANES), F32)
    for c in range(3):
        for d in range(3):
            square = pair_add(square, pair_mul((-2.0 * x[c][d], nothing), cov[c][d]))
    for d in range(3):
        for e in range(d + 1):
            gram = None
            for c in range(3):
                term = two_prod(x[c][d], x[c][e])
                gram = term if gram is None else pair_add(gram, term)
            if d != e:
                gram = (2.0 * gram[0], 2.0 * gram[1])
            square = pair_add(square, pair_mul(gram, ct[d, e]))

    row = lax.broadcasted_iota(jnp.int32, (copies, LANES), 0)
    noise = nothing
    for s in range(copies):
        noise = jnp.where(row == s, noise_ref[s], noise)
    loss_weight = (noise * noise + SIGMA * SIGMA) / (noise * SIGMA * (noise * SIGMA))
    mean_square = (square[0] + square[1]) / (3.0 * weight_sum)
    loss_ref[...] = loss_weight * mean_square + 1.0 - score / count

    grad_scale = 16.0 * atoms
    for c in range(3):
        for d in range(3):
            m_ref[d, pl.ds(c, copies, stride=3), :] = x[c][d]
        m_ref[3, pl.ds(c, copies, stride=3), :] = pred_mean[c][0]
        m_ref[4, pl.ds(c, copies, stride=3), :] = grad_scale * 2.0 * loss_weight / (3.0 * weight_sum)
        m_ref[5, pl.ds(c, copies, stride=3), :] = grad_scale / count
        k_ref[c:c + 1, :] = true_mean[c][0][0:1]

    @pl.loop(0, tiles)
    def _(t):
        sl = pl.ds(pl.multiple_of(t * LANES, LANES), LANES)
        kind = kind_ref[:, sl]
        weight = jnp.where(kind == 1, 5.0, jnp.where(kind == 2, 10.0, 1.0))
        centred = true_ref[:, sl] - k_ref[0:3, :]
        for s in range(copies):
            r = slice(3 * s, 3 * s + 3)
            target = m_ref[0, r, :] * centred[0:1] + m_ref[1, r, :] * centred[1:2] + m_ref[2, r, :] * centred[2:3] + m_ref[3, r, :]
            deviation = pred_ref[s, :, sl] - target
            grad_ref[s, :, sl] = m_ref[4, r, :] * weight * deviation - m_ref[5, r, :] * pull_ref[s, :, sl]

    for t in range(2 * BAND):
        start = t * LANES if t < BAND else (tiles - 2 * BAND + t) * LANES
        for s in range(copies):
            grad_ref[s, :, start:start + LANES] -= m_ref[5, 3 * s:3 * s + 3, :] * edge_ref[s, :, t * LANES:(t + 1) * LANES]


VMEM = pl.BlockSpec(memory_space=pltpu.VMEM)
SMEM = pl.BlockSpec(memory_space=pltpu.SMEM)
PARAMS = pltpu.CompilerParams(vmem_limit_bytes=40 * 2**20)


def swap(x, axis, step):
    return lax.ppermute(x, axis, [(i, i ^ step) for i in range(lax.axis_size(axis))])


def shards(coords_pred, coords_true, atom_kind, partners, noise_level):
    copies, _, local = coords_pred.shape
    tiles = partners.shape[0]
    rows = 3 * copies
    size = lax.axis_size("res")
    kind = atom_kind[None]
    base = (lax.axis_index("res") * tiles)[None].astype(jnp.int32)
    stats_shape = jax.ShapeDtypeStruct((2, 8, LANES), F32)

    def edge(start):
        take = lambda a: lax.slice_in_dim(a, start, start + BAND * LANES, axis=a.ndim - 1)
        cut = jnp.where(take(atom_kind) == 1, 15.0, 7.5).astype(F32)
        return jnp.concatenate([take(coords_pred).reshape(rows, -1) * 0.5, take(coords_true) * 0.5, cut[None]], axis=0)

    forward = [(i, i + 1) for i in range(size - 1)]
    low = lax.ppermute(edge(local - BAND * LANES), "res", forward)
    high = lax.ppermute(edge(0), "res", [(b, a) for a, b in forward])

    pull, stats = pl.pallas_call(
        functools.partial(interior_kernel, copies=copies, tiles=tiles),
        in_specs=[SMEM, SMEM] + [VMEM] * 3,
        out_specs=[VMEM, VMEM],
        out_shape=[jax.ShapeDtypeStruct((copies, 3, local), F32), stats_shape],
        scratch_shapes=[pltpu.VMEM((6, 16, LANES), F32), pltpu.VMEM((2, 6, 16, LANES), F32)] + Engine.scratch(tiles, copies, BAND * tiles),
        compiler_params=PARAMS,
        cost_estimate=pl.CostEstimate(flops=10**8, bytes_accessed=10**6, transcendentals=10**7),
        name="interior",
    )(base, partners, coords_pred, coords_true, kind)
    edge_pull, stats = pl.pallas_call(
        functools.partial(edge_kernel, copies=copies, tiles=tiles),
        in_specs=[SMEM, SMEM] + [VMEM] * 6,
        out_specs=[VMEM, VMEM],
        out_shape=[jax.ShapeDtypeStruct((copies, 3, 2 * BAND * LANES), F32), stats_shape],
        scratch_shapes=Engine.scratch(4 * BAND, copies, BAND * (BAND + 1)),
        compiler_params=PARAMS,
        name="edges",
    )(base, partners, coords_pred, coords_true, kind, low, high, stats)

    step = 1
    while step < size:
        other = swap(stats, "res", step)
        total, error = two_sum(stats[0, 0], other[0, 0])
        moments = jnp.stack([total, (stats[0, 1] + other[0, 1]) + error] + [jnp.zeros((LANES,), F32)] * 6)
        stats = jnp.stack([moments, stats[1] + other[1]])
        step *= 2

    loss, grad = pl.pallas_call(
        functools.partial(finish_kernel, copies=copies, tiles=tiles, atoms=local * size),
        in_specs=[VMEM, SMEM] + [VMEM] * 5,
        out_specs=[VMEM, VMEM],
        out_shape=[jax.ShapeDtypeStruct((copies, LANES), F32), jax.ShapeDtypeStruct((copies, 3, local), F32)],
        scratch_shapes=[pltpu.VMEM((6, rows, LANES), F32), pltpu.VMEM((8, LANES), F32), pltpu.VMEM((2, LANES, LANES), F32)],
        compiler_params=PARAMS,
        name="finish",
    )(stats, noise_level, coords_pred, coords_true, kind, pull, edge_pull)
    copy_loss = loss[:, 0]
    total = jnp.sum(copy_loss)[None]
    step = 1
    while step < lax.axis_size("samp"):
        total = total + swap(total, "samp", step)
        step *= 2
    mean_loss = total[0] / (copies * lax.axis_size("samp"))
    return copy_loss, mean_loss, grad


def solution(mesh):
    in_specs = (P("samp", None, "res"), P(None, "res"), P("res"), P("res", None), P("samp"))
    out_specs = (P("samp"), P(), P("samp", None, "res"))
    return jax.shard_map(shards, mesh=mesh, in_specs=in_specs, out_specs=out_specs, check_vma=False)
```

time: 74 us -> 62 us (0.84)
  Pallas kernels: 33.6 us -> 26.2 us
  waiting for transfers between devices: 9.72 us -> 6.38 us
  starting transfers between devices: 22.8 us -> 20.5 us
    pallas_call x1 -> x2, Pallas kernels: 31.9 us -> 24.5 us  [the longest x1 21.3 us: shards(): pl.pallas_call(functools.partial(interior_kernel, copies=copies, tiles=ti...]
    ppermute x1, waiting for transfers between devices: 3.42 us -> 0.01 us  [shards(): high = lax.ppermute(edge(0), 'res', [(b, a) for a, b in forward])]
    ppermute x5, starting transfers between devices: 16.6 us -> 14.3 us  [swap(): lax.ppermute(x, axis, [(i, i ^ step) for i in range(lax.axis_size(axis))])]
  transfers between devices with their start and end apart: 7 -> 7, of which waited for: 6 -> 5; matrix products, arithmetic and copies ran while one was open for 1% -> 2% of each run, Pallas kernels for 0% -> 34%
where the time goes in v2:
time: 62 us; the launch traced here: 62.5 us
  Pallas kernels  26.2 us (42%)
  starting transfers between devices  20.5 us (33%)
  waiting for transfers between devices  6.38 us (10%)
  between operations  3.81 us (6%)
  other arithmetic  3.13 us (5%)
  local copies, waits for them, and re-layouts  2.48 us (4%)
    pallas_call x1, Pallas kernels, shards(): pl.pallas_call(functools.partial(interior_kernel, copies=copies, tiles=ti...  21.3 us
    ppermute x5, starting transfers between devices, swap(): lax.ppermute(x, axis, [(i, i ^ step) for i in range(lax.axis_size(axis))])  14.3 us
    ppermute x5, waiting for transfers between devices, swap(): lax.ppermute(x, axis, [(i, i ^ step) for i in range(lax.axis_size(axis))])  6.37 us
    ppermute x1, starting transfers between devices, shards(): low = lax.ppermute(edge(local - BAND * LANES), 'res', forward)  4.84 us
    pallas_call x1, Pallas kernels, shards(): pl.pallas_call(functools.partial(edge_kernel, copies=copies, tiles=tiles)...  3.17 us
    unnamed x13, local copies, waits for them, and re-layouts  2.29 us
    pallas_call x1, Pallas kernels, shards(): pl.pallas_call(functools.partial(finish_kernel, copies=copies, tiles=tile...  1.71 us
    ppermute x1, starting transfers between devices, shards(): high = lax.ppermute(edge(0), 'res', [(b, a) for a, b in forward])  1.29 us
  transfers between devices with their start and end apart: 7, of which 5 were waited for; matrix products, arithmetic and copies ran while one was open for 2% of the time, Pallas kernels for 34%

profile of v2, /device:TPU:0, one launch (start us, length us, event | category | flops | bytes accessed | tf_op | source)
XLA Modules:
  0.0 62.5 jit_solution(11653333505262882289)
XLA Ops:
  0.6 0.0 copy-start.3
  0.6 0.7 %compare_select_fusion = (f32[256]{0:T(256)S(1)}, f32[256]{0:T(256)S(1)}) fusion(s32[3072]{0:T(1024)} %param.7), kind=kLoop, calls=%fused_computation.15 | loop fusion | flops 1024 | bytes 4096 | tf_op jit(solution)/shard_map/jit(_where)/select_n | solution.py:575
  1.4 0.7 %slice_multiply_fusion.2 = (f32[3,256]{1,0:T(4,128)S(1)}, f32[3,256]{1,0:T(4,128)S(1)}) fusion(f32[3,3072]{1,0:T(4,128)} %true_ref.5), kind=kLoop, calls=%fused_computation.13 | loop fusion | flops 1536 | bytes 12288 | tf_op jit(solution)/shard_map/mul | solution.py:576
  2.1 0.7 %slice_multiply_fusion = (f32[4,3,256]{2,0,1:T(4,128)S(1)}, f32[4,3,256]{2,0,1:T(4,128)S(1)}) fusion(f32[4,3,3072]{2,0,1:T(4,128)} %param.5), kind=kLoop, calls=%fused_computation.2 | loop fusion | flops 6144 | bytes 49152 | tf_op jit(solution)/shard_map/mul | solution.py:576
  2.9 4.8 %collective-permute-start = (f32[16,256]{1,0:T(8,128)S(1)}, f32[16,256]{1,0:T(8,128)S(1)}, u32[]{:S(2)}, u32[]{:S(2)}) collective-permute-start(f32[16,256]{1,0:T(8,128)S(1)} %pad_maximum_fusion), channel_id=1, source_target_pairs={{0,4},{4,8},{8,12},{12,16},{16,20},{20,24},{24,28},{1,5},{5,9},{9,... | collective-permute-start | bytes 49160 | tf_op jit(solution)/shard_map/ppermute | solution.py:579
  7.8 1.3 %collective-permute-start.1 = (f32[16,256]{1,0:T(8,128)S(1)}, f32[16,256]{1,0:T(8,128)S(1)}, u32[]{:S(2)}, u32[]{:S(2)}) collective-permute-start(f32[16,256]{1,0:T(8,128)S(1)} %pad_maximum_fusion.1), channel_id=1, source_target_pairs={{4,0},{8,4},{12,8},{16,12},{20,16},{24,20},{28,24},{5,1},{9,5},{13... | collective-permute-start | bytes 49160 | tf_op jit(solution)/shard_map/ppermute | solution.py:580
  9.1 0.0 copy-start
  9.1 0.1 copy.21.pred_ref
  9.2 0.0 copy-start.4
  9.2 0.0 copy-start.1
  9.2 0.7 %copy-done.4 = s32[24,5]{0,1:T(8,128)S(1)} copy-done((s32[24,5]{0,1:T(8,128)S(1)}, s32[24,5]{0,1:T(8,128)}, u32[]{:S(2)}) %copy-start.4) | copy-done | bytes 504
  9.9 0.1 copy.20.part_ref
  10.0 21.3 %interior.1 = (f32[4,3,3072]{2,1,0:T(4,128)S(1)}, f32[2,8,128]{2,1,0:T(8,128)S(1)}) custom-call(s32[1]{0:T(128)} %bitcast.base_ref, s32[24,5]{1,0:T(8,128)S(1)} %copy.20.part_ref, f32[4,3,3072]{2,1,0:T(4,128)S(1)} %copy.21.pred_ref, f32[3,3072]{1,0:T(4,128)S(1)} %copy-done, s32[1,3072]{1,0:T(1,128)S(1)} %bitcast.78), custom_call_target="tpu_custom_call" | custom-call | flops 100000000 | bytes 1000000 | tf_op jit(solution)/shard_map/interior/pallas_call | solution.py:582
  31.3 3.2 %edges.1 = (f32[4,3,512]{2,1,0:T(4,128)S(1)}, f32[2,8,128]{2,1,0:T(8,128)S(1)}) custom-call(s32[1]{0:T(128)} %bitcast.base_ref, s32[24,5]{1,0:T(8,128)S(1)} %copy.20.part_ref, f32[4,3,3072]{2,1,0:T(4,128)S(1)} %copy.21.pred_ref, f32[3,3072]{1,0:T(4,128)S(1)} %copy-done, s32[1,3072]{1,0:T(1,128)S(1)} %bitcast.79, f32[16,256]{1,0:T(8,128)S(1)} %collective-permute-done.low_ref, ...), custom_call_target="tpu_custom_call" | custom-call | tf_op jit(solution)/shard_map/edges/pallas_call | solution.py:592
  34.5 6.5 %collective-permute-start.2 = (f32[2,8,128]{2,1,0:T(8,128)S(1)}, f32[2,8,128]{2,1,0:T(8,128)S(1)}, u32[]{:S(2)}, u32[]{:S(2)}) collective-permute-start(f32[2,8,128]{2,1,0:T(8,128)S(1)} %get-tuple-element.10), channel_id=1, source_target_pairs={{0,4},{4,0},{8,12},{12,8},{16,20},{20,16},{24,28},{28,24},{1,5},{5... | collective-permute-start | bytes 24584 | tf_op jit(solution)/shard_map/ppermute | solution.py:561
  41.0 0.1 pad.17.clone
  41.1 0.1 pad.16.clone
  41.2 1.5 %collective-permute-done.2 = f32[2,8,128]{2,1,0:T(8,128)S(1)} collective-permute-done((f32[2,8,128]{2,1,0:T(8,128)S(1)}, f32[2,8,128]{2,1,0:T(8,128)S(1)}, u32[]{:S(2)}, u32[]{:S(2)}) %collective-permute-start.2) | collective-permute-done | bytes 8224 | tf_op jit(solution)/shard_map/ppermute | solution.py:561
  42.7 0.1 maximum_bitcast_fusion
  42.7 2.2 %collective-permute-start.3 = (f32[2,8,128]{2,1,0:T(8,128)S(1)}, f32[2,8,128]{2,1,0:T(8,128)S(1)}, u32[]{:S(2)}, u32[]{:S(2)}) collective-permute-start(f32[2,8,128]{2,1,0:T(8,128)S(1)} %pad_maximum_fusion.2), channel_id=1, source_target_pairs={{0,8},{4,12},{8,0},{12,4},{16,24},{20,28},{24,16},{28,20},{1,9},{5... | collective-permute-start | bytes 24584 | tf_op jit(solution)/shard_map/ppermute | solution.py:561
  44.9 1.6 %collective-permute-done.3 = f32[2,8,128]{2,1,0:T(8,128)S(1)} collective-permute-done((f32[2,8,128]{2,1,0:T(8,128)S(1)}, f32[2,8,128]{2,1,0:T(8,128)S(1)}, u32[]{:S(2)}, u32[]{:S(2)}) %collective-permute-start.3) | collective-permute-done | bytes 8224 | tf_op jit(solution)/shard_map/ppermute | solution.py:561
  46.5 0.1 maximum_bitcast_fusion.1
  46.6 2.8 %collective-permute-start.4 = (f32[2,8,128]{2,1,0:T(8,128)S(1)}, f32[2,8,128]{2,1,0:T(8,128)S(1)}, u32[]{:S(2)}, u32[]{:S(2)}) collective-permute-start(f32[2,8,128]{2,1,0:T(8,128)S(1)} %pad_maximum_fusion.3), channel_id=1, source_target_pairs={{0,16},{4,20},{8,24},{12,28},{16,0},{20,4},{24,8},{28,12},{1,17},{... | collective-permute-start | bytes 24584 | tf_op jit(solution)/shard_map/ppermute | solution.py:561
  49.4 1.8 %collective-permute-done.4 = f32[2,8,128]{2,1,0:T(8,128)S(1)} collective-permute-done((f32[2,8,128]{2,1,0:T(8,128)S(1)}, f32[2,8,128]{2,1,0:T(8,128)S(1)}, u32[]{:S(2)}, u32[]{:S(2)}) %collective-permute-start.4) | collective-permute-done | bytes 8224 | tf_op jit(solution)/shard_map/ppermute | solution.py:561
  51.2 0.1 maximum_bitcast_fusion.2
  51.3 0.7 %copy-done.2 = f32[4]{0:T(128)S(1)} copy-done((f32[4]{0:T(128)S(1)}, f32[4]{0:T(128)}, u32[]{:S(2)}) %copy-start.2) | copy-done | bytes 40
  52.0 1.7 %finish.1 = (f32[4,128]{1,0:T(4,128)S(1)}, f32[4,3,3072]{2,1,0:T(4,128)S(1)}) custom-call(f32[2,8,128]{2,1,0:T(8,128)S(1)} %pad_maximum_fusion.4.stat_ref, f32[4]{0:T(128)S(1)} %copy-done.2, f32[4,3,3072]{2,1,0:T(4,128)S(1)} %copy.21.pred_ref, f32[3,3072]{1,0:T(4,128)S(1)} %copy-done, s32[1,3072]{1,0:T(1,128)S(1)} %bitcast.80, ...), custom_call_target="tpu_custom_call" | custom-call | tf_op jit(solution)/shard_map/finish/pallas_call | solution.py:610
  53.7 0.7 %slice_reduce_fusion = (f32[]{:T(128)}, f32[4]{0:T(128)}) fusion(f32[4,128]{1,0:T(4,128)S(1)} %get-tuple-element.13), kind=kLoop, calls=%fused_computation.17 | loop fusion | flops 3 | bytes 36 | tf_op jit(solution)/shard_map/reduce_sum | solution.py:620
  54.3 0.8 %copy.23 = f32[4,3,3072]{2,0,1:T(4,128)} copy(f32[4,3,3072]{2,1,0:T(4,128)S(1)} %get-tuple-element.20) | data formatting | bytes 294912
  55.1 0.6 %collective-permute-done.5 = f32[1]{0:T(128)} collective-permute-done((f32[1]{0:T(128)}, f32[1]{0:T(128)}, u32[]{:S(2)}, u32[]{:S(2)}) %collective-permute-start.5) | collective-permute-done | bytes 36 | tf_op jit(solution)/shard_map/ppermute | solution.py:561
  57.0 2.9 %collective-permute-start.6 = (f32[1]{0:T(128)}, f32[1]{0:T(128)}, u32[]{:S(2)}, u32[]{:S(2)}) collective-permute-start(f32[1]{0:T(128)} %add.180), channel_id=1, source_target_pairs={{0,2},{1,3},{2,0},{3,1},{4,6},{5,7},{6,4},{7,5},{8,10},{9,11},{10,... | collective-permute-start | bytes 20 | tf_op jit(solution)/shard_map/ppermute | solution.py:561
  59.9 0.8 %collective-permute-done.6 = f32[1]{0:T(128)} collective-permute-done((f32[1]{0:T(128)}, f32[1]{0:T(128)}, u32[]{:S(2)}, u32[]{:S(2)}) %collective-permute-start.6) | collective-permute-done | bytes 36 | tf_op jit(solution)/shard_map/ppermute | solution.py:561
  (24 shorter events, 0.1 us)
Async XLA Ops:
  0.6 8.4 %copy-start.3 = (f32[4,3,3072]{2,0,1:T(4,128)S(1)}, f32[4,3,3072]{2,0,1:T(4,128)}, u32[]{:S(2)}) copy-start(f32[4,3,3072]{2,0,1:T(4,128)} %param.5) | copy-start | bytes 442372
  2.9 28.5 %collective-permute-start = (f32[16,256]{1,0:T(8,128)S(1)}, f32[16,256]{1,0:T(8,128)S(1)}, u32[]{:S(2)}, u32[]{:S(2)}) collective-permute-start(f32[16,256]{1,0:T(8,128)S(1)} %pad_maximum_fusion), channel_id=1, source_target_pairs={{0,4},{4,8},{8,12},{12,16},{16,20},{20,24},{24,28},{1,5},{5,9},{9,... | collective-permute-start | bytes 49160 | tf_op jit(solution)/shard_map/ppermute | solution.py:579
  7.8 23.6 %collective-permute-start.1 = (f32[16,256]{1,0:T(8,128)S(1)}, f32[16,256]{1,0:T(8,128)S(1)}, u32[]{:S(2)}, u32[]{:S(2)}) collective-permute-start(f32[16,256]{1,0:T(8,128)S(1)} %pad_maximum_fusion.1), channel_id=1, source_target_pairs={{4,0},{8,4},{12,8},{16,12},{20,16},{24,20},{28,24},{5,1},{9,5},{13... | collective-permute-start | bytes 49160 | tf_op jit(solution)/shard_map/ppermute | solution.py:580
  9.1 0.9 %copy-start = (f32[3,3072]{1,0:T(4,128)S(1)}, f32[3,3072]{1,0:T(4,128)}, u32[]{:S(2)}) copy-start(f32[3,3072]{1,0:T(4,128)} %true_ref.5) | copy-start | bytes 110596
  9.2 0.7 %copy-start.4 = (s32[24,5]{0,1:T(8,128)S(1)}, s32[24,5]{0,1:T(8,128)}, u32[]{:S(2)}) copy-start(s32[24,5]{0,1:T(8,128)} %param.8) | copy-start | bytes 1444
  9.2 0.8 %copy-start.1 = (s32[3072]{0:T(1024)S(1)}, s32[3072]{0:T(1024)}, u32[]{:S(2)}) copy-start(s32[3072]{0:T(1024)} %param.7) | copy-start | bytes 36868
  34.5 8.2 %collective-permute-start.2 = (f32[2,8,128]{2,1,0:T(8,128)S(1)}, f32[2,8,128]{2,1,0:T(8,128)S(1)}, u32[]{:S(2)}, u32[]{:S(2)}) collective-permute-start(f32[2,8,128]{2,1,0:T(8,128)S(1)} %get-tuple-element.10), channel_id=1, source_target_pairs={{0,4},{4,0},{8,12},{12,8},{16,20},{20,16},{24,28},{28,24},{1,5},{5... | collective-permute-start | bytes 24584 | tf_op jit(solution)/shard_map/ppermute | solution.py:561
  42.7 3.8 %collective-permute-start.3 = (f32[2,8,128]{2,1,0:T(8,128)S(1)}, f32[2,8,128]{2,1,0:T(8,128)S(1)}, u32[]{:S(2)}, u32[]{:S(2)}) collective-permute-start(f32[2,8,128]{2,1,0:T(8,128)S(1)} %pad_maximum_fusion.2), channel_id=1, source_target_pairs={{0,8},{4,12},{8,0},{12,4},{16,24},{20,28},{24,16},{28,20},{1,9},{5... | collective-permute-start | bytes 24584 | tf_op jit(solution)/shard_map/ppermute | solution.py:561
  46.6 4.6 %collective-permute-start.4 = (f32[2,8,128]{2,1,0:T(8,128)S(1)}, f32[2,8,128]{2,1,0:T(8,128)S(1)}, u32[]{:S(2)}, u32[]{:S(2)}) collective-permute-start(f32[2,8,128]{2,1,0:T(8,128)S(1)} %pad_maximum_fusion.3), channel_id=1, source_target_pairs={{0,16},{4,20},{8,24},{12,28},{16,0},{20,4},{24,8},{28,12},{1,17},{... | collective-permute-start | bytes 24584 | tf_op jit(solution)/shard_map/ppermute | solution.py:561
  51.3 0.7 %copy-start.2 = (f32[4]{0:T(128)S(1)}, f32[4]{0:T(128)}, u32[]{:S(2)}) copy-start(f32[4]{0:T(128)} %noise_ref.1) | copy-start | bytes 52
  54.3 1.4 %collective-permute-start.5 = (f32[1]{0:T(128)}, f32[1]{0:T(128)}, u32[]{:S(2)}, u32[]{:S(2)}) collective-permute-start(f32[1]{0:T(128)} %bitcast.16), channel_id=1, source_target_pairs={{0,1},{1,0},{2,3},{3,2},{4,5},{5,4},{6,7},{7,6},{8,9},{9,8},{10,11... | collective-permute-start | bytes 20 | tf_op jit(solution)/shard_map/ppermute | solution.py:561
  57.0 3.7 %collective-permute-start.6 = (f32[1]{0:T(128)}, f32[1]{0:T(128)}, u32[]{:S(2)}, u32[]{:S(2)}) collective-permute-start(f32[1]{0:T(128)} %add.180), channel_id=1, source_target_pairs={{0,2},{1,3},{2,0},{3,1},{4,6},{5,7},{6,4},{7,5},{8,10},{9,11},{10,... | collective-permute-start | bytes 20 | tf_op jit(solution)/shard_map/ppermute | solution.py:561

commit v3 on v2

v3 whole, which is shorter than its diff:
```python
import functools

import jax
import jax.numpy as jnp
from jax import lax
from jax.experimental import pallas as pl
from jax.experimental.pallas import tpu as pltpu
from jax.sharding import PartitionSpec as P

LANES = 128
BAND = 2
SWEEPS = 20
SIGMA = 16.0
HALF_THRESHOLDS = (0.25, 0.5, 1.0, 2.0)
EPS = 0.25e-6
F32 = jnp.float32
BF16 = jnp.bfloat16


def roll(x, shift, axis=1):
    return pltpu.roll(x, shift, axis)


def two_sum(a, b):
    s = a + b
    t = s - a
    return s, (a - (s - t)) + (b - t)


def two_prod(a, b):
    def halves(x):
        t = x * 4097.0
        h = t - (t - x)
        return h, x - h

    p = a * b
    ah, al = halves(a)
    bh, bl = halves(b)
    return p, ((ah * bh - p) + ah * bl + al * bh) + al * bl


def pair_add(x, y):
    s, e = two_sum(x[0], y[0])
    return two_sum(s, e + (x[1] + y[1]))


def pair_neg(x):
    return -x[0], -x[1]


def pair_mul(x, y):
    p, e = two_prod(x[0], y[0])
    return two_sum(p, e + (x[0] * y[1] + x[1] * y[0]))


def pair_div(x, w):
    q = x[0] / w
    p, e = two_prod(q, w)
    return two_sum(q, (((x[0] - p) - e) + x[1]) / w)


def dot(a, b):
    return jnp.dot(a, b, preferred_element_type=F32)


def dot_nt(a, b):
    return lax.dot_general(a, b, (((1,), (1,)), ((), ())), preferred_element_type=F32)


def split3(x):
    a = x.astype(BF16).astype(F32)
    rest = x - a
    b = rest.astype(BF16).astype(F32)
    return a, b, (rest - b).astype(BF16).astype(F32)


def stack(a, b, axis):
    return jnp.concatenate([a, b], axis=axis)


def listed(part_ref, owner, other):
    hit = jnp.bool_(False)
    for k in range(1, part_ref.shape[1]):
        hit = hit | (part_ref[owner, k] == other)
    return hit


class Engine:
    names = ("v", "cut", "centre", "left", "point", "right", "true", "weight", "minus", "d", "f", "acc", "score", "count", "tri", "items")

    def __init__(self, copies, refs):
        self.copies = copies
        self.twos = copies // 2
        for name, ref in zip(self.names, refs):
            setattr(self, name, ref)

    @staticmethod
    def scratch(tiles, copies, items):
        n, twos = tiles + 1, copies // 2
        return [
            pltpu.VMEM((n, copies + 1, 8, LANES), F32),
            pltpu.VMEM((n, 1, LANES), F32),
            pltpu.VMEM((n, copies + 1, 8, LANES), F32),
            pltpu.VMEM((n, twos + 1, LANES, LANES), BF16),
            pltpu.VMEM((n, twos, 64, 2 * LANES), BF16),
            [pltpu.VMEM((1, twos + 1, LANES, 2 * LANES), BF16)] * 2,
            [pltpu.VMEM((LANES, LANES), F32)] * 2,
            [pltpu.VMEM((LANES, LANES), F32)] * 2,
            [pltpu.VMEM((LANES, LANES), F32)] * 2,
            [pltpu.VMEM((1, twos + 1, LANES, 2 * LANES), F32)] * 2,
            [pltpu.VMEM((1, twos, 2 * LANES, 2 * LANES), BF16)] * 2,
            pltpu.VMEM((n, copies, 8, LANES), F32),
            pltpu.VMEM((copies, 8, LANES), F32),
            pltpu.VMEM((8, LANES), F32),
            pltpu.VMEM((2, LANES, LANES), BF16),
            pltpu.SMEM((4, items + 2), jnp.int32),
        ]

    @staticmethod
    def self_scratch(copies):
        twos = copies // 2
        return [
            [pltpu.VMEM((2, twos + 1, LANES, 2 * LANES), BF16)] * 2,
            [pltpu.VMEM((2, twos + 1, LANES, 2 * LANES), F32)] * 2,
            [pltpu.VMEM((2, twos, 2 * LANES, 2 * LANES), BF16)] * 2,
        ]

    def for_self(self, refs):
        other = Engine(self.copies, [])
        other.__dict__.update(self.__dict__)
        other.right, other.d, other.f = refs
        return other

    def begin(self, tiles):
        for ref in [self.acc, self.score, self.count, *self.f, self.v.at[tiles], self.cut.at[tiles], self.centre.at[tiles], self.left.at[tiles], self.point.at[tiles]]:
            ref[...] = jnp.zeros_like(ref)
        row = lax.broadcasted_iota(jnp.int32, (LANES, LANES), 0)
        lane = lax.broadcasted_iota(jnp.int32, (LANES, LANES), 1)
        self.tri[0] = jnp.where(lane > row, 1.0, 0.0).astype(BF16)
        self.tri[1] = jnp.where(lane < row, 1.0, 0.0).astype(BF16)
        self.begin_right()

    def begin_right(self):
        pick = jnp.where(lax.broadcasted_iota(jnp.int32, (LANES, LANES), 0) == 7, 1.0, 0.0).astype(BF16)
        for ref in self.right:
            ref[...] = jnp.zeros_like(ref)
            for k in range(ref.shape[0]):
                ref[k, self.twos, :, LANES:] = pick

    def place(self, t, ref):
        blank = jnp.zeros((5, LANES), F32)
        for s in range(self.copies):
            self.v[t, s] = stack(ref[pl.ds(s, 3, stride=self.copies), :], blank, 0)
        self.v[t, self.copies] = stack(ref[3 * self.copies:3 * self.copies + 3, :], blank, 0)

    @staticmethod
    def unit(k):
        return jnp.where(lax.broadcasted_iota(jnp.int32, (8, LANES), 0) == k, 1.0, 0.0)

    def prep(self, t):
        groups = []
        for s in range(self.copies + 1):
            v = self.v[t, s]
            centre = jnp.broadcast_to(jnp.sum(v, axis=1, keepdims=True) * (1.0 / LANES), (8, LANES))
            self.centre[t, s] = centre
            y = v - centre
            norm = jnp.sum(y * y, axis=0, keepdims=True)
            x = y + (self.unit(4) + EPS * self.unit(5)) + norm * self.unit(3)
            if s == self.copies:
                x = x + self.unit(7) * self.cut[t]
            a, b, c = split3(x)
            groups.append(jnp.concatenate([a, a, b, a, b, c, b, c], axis=0))
            if s < self.copies:
                a, b, c = split3(v + self.unit(3))
                p = jnp.concatenate([a, b, c, jnp.zeros_like(a)], axis=0).astype(BF16)
                q = 32 * (s % 2)
                self.point[t, s // 2, q:q + 32, :LANES] = p
                self.point[t, s // 2, q:q + 32, LANES:] = p
        groups.append(jnp.zeros((64, LANES), F32))
        for h in range(self.twos + 1):
            self.left[t, h] = stack(groups[2 * h], groups[2 * h + 1], 0).T.astype(BF16)

    def build(self, slot, k, g, j):
        for s in range(self.copies + 1):
            y = self.v[j, s] - self.centre[g, s]
            norm = jnp.sum(y * y, axis=0, keepdims=True)
            a, b, c = split3((self.unit(3) + self.unit(5)) - 2.0 * y + norm * self.unit(4))
            q, m = 64 * (s % 2), LANES * (s % 2)
            self.right[slot][k, s // 2, q:q + 64, m:m + LANES] = jnp.concatenate([a, b, a, c, b, a, c, b], axis=0).astype(BF16)

    def squares(self, slot, k, g, h):
        return dot(self.left[g, h], self.right[slot][k, h])

    def get(self, slot, h, k, lanes, shared):
        one = self.d[slot][0, h, k, lanes]
        if not shared:
            return one
        return jnp.where(self.upper(k), one, self.d[slot][1, h, k, lanes])

    @staticmethod
    def upper(k):
        shape = (k.stop - k.start, LANES)
        return lax.broadcasted_iota(jnp.int32, shape, 1) > lax.broadcasted_iota(jnp.int32, shape, 0) + k.start

    def weigh(self, slot, cuts, share, shared):
        total = jnp.zeros((8, LANES), F32)
        for b in range(16):
            k = slice(8 * b, 8 * b + 8)
            d2 = jnp.maximum(self.get(slot, self.twos, k, slice(0, LANES), shared), EPS)
            dist = d2 * lax.rsqrt(d2)
            cut_j = jnp.where(self.upper(k), cuts[0], cuts[1]) if shared else cuts[0]
            cut_i = self.get(slot, self.twos, k, slice(LANES, 2 * LANES), shared)
            w = jnp.where(dist < cut_j, 0.0625, 0.0) + jnp.where(dist < cut_i, 0.0625, 0.0)
            if shared:
                row = lax.broadcasted_iota(jnp.int32, (8, LANES), 0) + 8 * b
                w = jnp.where(lax.broadcasted_iota(jnp.int32, (8, LANES), 1) == row, 0.0, w)
            self.true[slot][k, :] = dist
            self.weight[slot][k, :] = w
            self.minus[slot][k, :] = -w
            total = total + w
        self.count[...] += total * share

    def factor(self, slot, share, shared):
        for s in range(self.copies):
            h, m = s // 2, LANES * (s % 2)
            score = jnp.zeros((8, LANES), F32)
            for q in range(8):
                k = slice(16 * q, 16 * q + 16)
                d2 = jnp.maximum(self.get(slot, h, k, slice(m, m + LANES), shared), EPS)
                r = lax.rsqrt(d2)
                diff = d2 * r - self.true[slot][k, :]
                spread = jnp.abs(diff)
                u = [jnp.tanh(t - spread) for t in HALF_THRESHOLDS]
                w = self.weight[slot][k, :]
                z = w * ((u[0] + u[1]) + (u[2] + u[3]))
                score = score + z[:8] + z[8:]
                slope = ((u[0] * u[0] + u[1] * u[1]) + (u[2] * u[2] + u[3] * u[3])) - 4.0
                f = slope * r * jnp.maximum(jnp.minimum(diff * 1e30, w), self.minus[slot][k, :])
                high = f.astype(BF16)
                low = (f - high.astype(F32)).astype(BF16)
                for i in range(1 + shared):
                    part = (high * self.tri[i, k, :], low * self.tri[i, k, :]) if shared else (high, low)
                    for x, start in zip(part, (16 * q, LANES + 16 * q)):
                        self.f[slot][i, h, start:start + 16, m:m + LANES] = x
            self.score[s] += score * share

    @staticmethod
    def fold(z):
        return [z[k:k + 8, m:m + LANES] + z[k + 8:k + 16, m:m + LANES] + z[k + 16:k + 24, m:m + LANES] for k, m in ((0, 0), (32, LANES))]

    def along_j(self, p, f):
        return self.fold(dot(p, f))

    def along_i(self, p, f):
        one = stack(f[:LANES, :LANES], f[LANES:, :LANES], 1)
        two = stack(f[:LANES, LANES:], f[LANES:, LANES:], 1)
        return self.fold(dot_nt(p, stack(one, two, 0)))

    def cross_build(self, item, slot):
        self.build(slot, 0, item[0], item[1])

    def cross_measure(self, item, slot):
        for h in [self.twos, *range(self.twos)]:
            self.d[slot][0, h] = self.squares(slot, 0, item[0], h)

    def cross_factor(self, item, slot):
        share = item[2].astype(F32) * 0.5
        self.weigh(slot, [self.cut[item[1]]], share, False)
        self.factor(slot, share, False)

    def cross_collect(self, item, slot):
        g, j = item[0], item[1]
        for h in range(self.twos):
            f = self.f[slot][0, h]
            x = self.along_j(self.point[g, h], f)
            y = self.along_i(self.point[j, h], f)
            for k in range(2):
                self.acc[j, 2 * h + k] += x[k]
                self.acc[g, 2 * h + k] += y[k]

    def self_build(self, item, slot):
        for k in range(2):
            self.build(slot, k, item[k], item[k])

    def self_measure(self, item, slot):
        for h in [self.twos, *range(self.twos)]:
            for k in range(2):
                self.d[slot][k, h] = self.squares(slot, k, item[k], h)

    def self_factor(self, item, slot):
        self.weigh(slot, [self.cut[item[0]], self.cut[item[1]]], 1.0, True)
        self.factor(slot, 1.0, True)

    def self_collect(self, item, slot):
        for h in range(self.twos):
            for k in range(2):
                f = self.f[slot][k, h]
                x = self.along_j(self.point[item[k], h], f)
                y = self.along_i(self.point[item[k], h], f)
                for q in range(2):
                    self.acc[item[k], 2 * h + q] += x[q] + y[q]

    def half(self, kind, items, slot):
        last, now, soon, later = items
        getattr(self, kind + "_collect")(last, 1 - slot)
        getattr(self, kind + "_measure")(soon, 1 - slot)
        getattr(self, kind + "_build")(later, 1 - slot)
        getattr(self, kind + "_factor")(now, slot)

    def begin_list(self, kind, item, n):
        getattr(self, kind + "_build")(item(0), 0)
        getattr(self, kind + "_measure")(item(0), 0)
        for i in (1, 2):
            getattr(self, kind + "_build")(item(jnp.minimum(i, n - 1)), i % 2)

    def run_list(self, kind, item, n, dummy):
        def at(p):
            return tuple(jnp.where(p < 0, dummy, z) for z in item(jnp.clip(p, 0, n - 1)))

        @pl.loop(0, n // 2)
        def _(i):
            p = 2 * i
            for slot in range(2):
                self.half(kind, [at(p + slot - 1), at(p + slot), at(p + slot + 1), at(p + slot + 3)], slot)

    def pull(self, t, s):
        a = self.acc[t, s]
        return (self.v[t, s] * a[3:4] - a)[0:3]

    def scores(self, weight_total):
        rows = [jnp.sum(self.score[s], axis=0, keepdims=True) for s in range(self.copies)]
        rows += [jnp.sum(self.count[...], axis=0, keepdims=True), weight_total]
        total = jnp.zeros((8, LANES), F32)
        for k, x in enumerate(rows):
            total = total + x * self.unit(2 + k)
        return jnp.broadcast_to(jnp.sum(total, axis=1, keepdims=True), (8, LANES))


def finish_list(e, item, n, dummy, also=lambda: None):
    @pl.when(n % 2 == 1)
    def _():
        before = tuple(jnp.where(n > 1, z, dummy) for z in item(jnp.maximum(n - 2, 0)))
        also()
        e.cross_collect(before, 1)
        e.cross_factor(item(n - 1), 0)
        e.cross_collect(item(n - 1), 0)

    @pl.when(n % 2 == 0)
    def _():
        also()
        e.cross_collect(item(n - 1), 1)


def interior_kernel(base_ref, part_ref, pred_ref, true_ref, kind_ref, pull_ref, stat_ref, x_ref, mom_ref, self_refs, *scratch, copies, tiles):
    e = Engine(copies, scratch)
    own = e.for_self(self_refs)
    base = base_ref[0]
    rows = 3 * copies
    e.begin(tiles)
    own.begin_right()
    x_ref[...] = jnp.zeros_like(x_ref)
    mom_ref[...] = jnp.zeros_like(mom_ref)

    unroll = next(u for u in (6, 4, 3, 2, 1) if tiles % u == 0)

    def prepare(m, n):
        for q in range(unroll):
            t = m * unroll + q
            for o in range(1, BAND + 1):
                e.items[0, n] = t - o
                e.items[1, n] = t
                e.items[2, n] = 2
                n = n + jnp.where(listed(part_ref, t, base + t - o) & (t >= o), 1, 0)
            sl = pl.ds(pl.multiple_of(t * LANES, LANES), LANES)
            kind = kind_ref[:, sl]
            weight = jnp.where(kind == 1, 5.0, jnp.where(kind == 2, 10.0, 1.0))
            for c in range(3):
                x_ref[q, c * copies:(c + 1) * copies, :] = pred_ref[c, :, sl] * 0.5
            x_ref[q, rows:rows + 3, :] = true_ref[:, sl] * 0.5
            e.place(t, x_ref.at[q])
            e.cut[t] = jnp.where(kind == 1, 15.0, 7.5)
            x = x_ref[q]
            wx = x * weight
            terms = [wx * x[rows + c:rows + c + 1] for c in range(3)] + [wx, wx * x]
            for i, term in enumerate(terms):
                total, error = two_sum(mom_ref[0, i], term)
                mom_ref[0, i] = total
                mom_ref[1, i] += error
            mom_ref[0, 5, 0:1, :] += weight
            e.prep(t)
        return n

    n = lax.fori_loop(0, tiles // unroll, prepare, jnp.int32(0))

    blank = jnp.zeros((LANES - 80, LANES), F32)
    high, low = (jnp.concatenate([mom_ref[part, i] for i in range(5)] + [blank], axis=0).T for part in range(2))
    sums = [(high[8 * k:8 * k + 8], low[8 * k:8 * k + 8]) for k in range(16)]
    while len(sums) > 1:
        sums = [pair_add(a, b) for a, b in zip(sums[::2], sums[1::2])]
    sums = sums[0]
    for k in (4, 2, 1):
        sums = pair_add(sums, (roll(sums[0], k, 0), roll(sums[1], k, 0)))
    moments = [x * e.unit(0) for x in sums]

    def twin(i):
        return 2 * i, 2 * i + 1

    def item(i):
        return e.items[0, i], e.items[1, i], e.items[2, i]

    for k, z in enumerate((tiles, tiles, 0)):
        e.items[k, 0] = jnp.where(n == 0, z, e.items[k, 0])
    n = jnp.maximum(n, 1)
    half = tiles // 2
    own.begin_list("self", twin, half)
    e.begin_list("cross", item, n)
    own.run_list("self", twin, half, tiles)
    e.run_list("cross", item, n, tiles)
    finish_list(e, item, n, tiles, lambda: own.self_collect(twin(half - 1), 1))

    @pl.loop(0, tiles // unroll)
    def _(m):
        for q in range(unroll):
            t = m * unroll + q
            sl = pl.ds(pl.multiple_of(t * LANES, LANES), LANES)
            for s in range(copies):
                pull = e.pull(t, s)
                for c in range(3):
                    pull_ref[c, s:s + 1, sl] = pull[c:c + 1]

    stat_ref[0] = moments[0] + e.scores(mom_ref[0, 5, 0:1, :])
    stat_ref[1] = moments[1]


def edge_kernel(base_ref, part_ref, pred_ref, true_ref, kind_ref, low_ref, high_ref, stat_ref, pull_ref, out_ref, x_ref, *scratch, copies, tiles):
    e = Engine(copies, scratch)
    base = base_ref[0]
    span = BAND * LANES
    local = tiles * LANES
    window = 4 * BAND
    e.begin(window)
    rows = 3 * copies
    for q in range(BAND):
        sl = slice(q * LANES, q * LANES + LANES)
        for ref, t in ((low_ref, q), (high_ref, 3 * BAND + q)):
            x_ref[t] = ref[:, sl]
        for start, t in ((0, BAND + q), (local - span, 2 * BAND + q)):
            sl = slice(start + q * LANES, start + q * LANES + LANES)
            for c in range(3):
                x_ref[t, c * copies:(c + 1) * copies, :] = pred_ref[c, :, sl] * 0.5
            x_ref[t, rows:rows + 3, :] = true_ref[:, sl] * 0.5
            x_ref[t, rows + 3:rows + 4, :] = jnp.where(kind_ref[:, sl] == 1, 15.0, 7.5)
    for t in range(window):
        e.place(t, x_ref.at[t])
        e.cut[t] = x_ref[t, rows + 3:rows + 4, :]
    n = jnp.int32(0)
    for o in range(1, BAND + 1):
        for k in range(o):
            for owner, other, g, j in ((k, k - o, BAND + k - o, BAND + k), (tiles - 1 - k, tiles - 1 - k + o, 3 * BAND - 1 - k, 3 * BAND - 1 - k + o)):
                e.items[0, n] = g
                e.items[1, n] = j
                e.items[2, n] = 1
                n = n + jnp.where(listed(part_ref, owner, base + other), 1, 0)

    def item(i):
        return e.items[0, i], e.items[1, i], e.items[2, i]

    @pl.when(n > 0)
    def _():
        for t in range(window):
            e.prep(t)
        e.begin_list("cross", item, n)
        e.run_list("cross", item, n, window)
        finish_list(e, item, n, window)

    for t in range(2 * BAND):
        for s in range(copies):
            pull = e.pull(BAND + t, s)
            for c in range(3):
                pull_ref[c, s:s + 1, t * LANES:(t + 1) * LANES] = pull[c:c + 1]
    out_ref[0] = stat_ref[0] + e.scores(jnp.zeros((1, LANES), F32))
    out_ref[1] = stat_ref[1]


def solve_kernel(stat_ref, noise_ref, loss_ref, sum_ref, m_ref, k_ref, s_ref, *, copies, atoms):
    rows = 3 * copies
    for part in range(2):
        column = jnp.broadcast_to(stat_ref[part, 0:1, :], (LANES, LANES)).T
        s_ref[part] = column

    def per_copy(c, q, scale):
        return tuple(s_ref[part, 16 * q + c * copies:16 * q + (c + 1) * copies, :] * scale for part in range(2))

    def shared(r, q, scale):
        return tuple(s_ref[part, 16 * q + r:16 * q + r + 1, :] * scale for part in range(2))

    def wide(x):
        return tuple(jnp.broadcast_to(v, (copies, LANES)) for v in x)

    weight_sum = jnp.broadcast_to(stat_ref[0, copies + 3:copies + 4, :], (copies, LANES))
    count = jnp.broadcast_to(stat_ref[0, copies + 2:copies + 3, :], (copies, LANES)) * 16.0
    score = stat_ref[0, 2:copies + 2, :] * 2.0 + 0.5 * count
    pred_sum = [wide(per_copy(c, 3, 2.0)) for c in range(3)]
    true_sum = [wide(shared(rows + c, 3, 2.0)) for c in range(3)]
    pred_mean = [pair_div(x, weight_sum) for x in pred_sum]
    true_mean = [pair_div(x, weight_sum) for x in true_sum]
    cov = [[pair_add(wide(per_copy(c, d, 4.0)), pair_neg(pair_mul(pred_sum[c], true_mean[d]))) for d in range(3)] for c in range(3)]
    ct = {}
    for d in range(3):
        for e in range(d + 1):
            ct[d, e] = pair_add(wide(shared(rows + d, e, 4.0)), pair_neg(pair_mul(true_sum[d], true_mean[e])))
    var = None
    for c in range(3):
        term = pair_add(wide(per_copy(c, 4, 4.0)), pair_neg(pair_mul(pred_sum[c], pred_mean[c])))
        var = term if var is None else pair_add(var, term)

    x = [[cov[c][d][0] for d in range(3)] for c in range(3)]
    frobenius = jnp.sqrt(sum(x[c][d] * x[c][d] for c in range(3) for d in range(3)))
    x = [[x[c][d] / frobenius for d in range(3)] for c in range(3)]

    def sweep(_, flat):
        x = [flat[0:3], flat[3:6], flat[6:9]]
        gram = {}
        for a in range(3):
            for b in range(a + 1):
                gram[a, b] = gram[b, a] = x[a][0] * x[b][0] + x[a][1] * x[b][1] + x[a][2] * x[b][2]
        return tuple(1.5 * x[a][d] - 0.5 * (gram[a, 0] * x[0][d] + gram[a, 1] * x[1][d] + gram[a, 2] * x[2][d])
                     for a in range(3) for d in range(3))

    flat = lax.fori_loop(0, SWEEPS, sweep, tuple(v for line in x for v in line))
    x = [flat[0:3], flat[3:6], flat[6:9]]

    square = var
    nothing = jnp.zeros((copies, LANES), F32)
    for c in range(3):
        for d in range(3):
            square = pair_add(square, pair_mul((-2.0 * x[c][d], nothing), cov[c][d]))
    for d in range(3):
        for e in range(d + 1):
            gram = None
            for c in range(3):
                term = two_prod(x[c][d], x[c][e])
                gram = term if gram is None else pair_add(gram, term)
            if d != e:
                gram = (2.0 * gram[0], 2.0 * gram[1])
            square = pair_add(square, pair_mul(gram, ct[d, e]))

    row = lax.broadcasted_iota(jnp.int32, (copies, LANES), 0)
    noise = nothing
    for s in range(copies):
        noise = jnp.where(row == s, noise_ref[s], noise)
    loss_weight = (noise * noise + SIGMA * SIGMA) / (noise * SIGMA * (noise * SIGMA))
    mean_square = (square[0] + square[1]) / (3.0 * weight_sum)
    loss = loss_weight * mean_square + 1.0 - score / count
    for s in range(copies):
        loss_ref[s] = loss[s, 0]
    sum_ref[...] = jnp.broadcast_to(jnp.sum(loss, axis=0, keepdims=True), (8, LANES))

    grad_scale = 16.0 * atoms
    for c in range(3):
        for d in range(3):
            m_ref[3 * c + d] = x[c][d]
        m_ref[9 + c] = pred_mean[c][0]
        k_ref[c:c + 1, :] = true_mean[c][0][0:1]
    m_ref[12] = grad_scale * 2.0 * loss_weight / (3.0 * weight_sum)
    m_ref[13] = grad_scale / count


def gradient_kernel(m_ref, k_ref, pred_ref, true_ref, kind_ref, pull_ref, edge_ref, grad_ref, *, copies, tiles):
    for t in range(tiles):
        sl = slice(t * LANES, (t + 1) * LANES)
        kind = kind_ref[:, sl]
        weight = jnp.where(kind == 1, 5.0, jnp.where(kind == 2, 10.0, 1.0))
        centred = true_ref[:, sl] - k_ref[0:3, :]
        for c in range(3):
            target = m_ref[3 * c] * centred[0:1] + m_ref[3 * c + 1] * centred[1:2] + m_ref[3 * c + 2] * centred[2:3] + m_ref[9 + c]
            deviation = pred_ref[c, :, sl] - target
            grad_ref[c, :, sl] = m_ref[12] * weight * deviation - m_ref[13] * pull_ref[c, :, sl]

    for t in range(2 * BAND):
        start = t * LANES if t < BAND else (tiles - 2 * BAND + t) * LANES
        for c in range(3):
            grad_ref[c, :, start:start + LANES] -= m_ref[13] * edge_ref[c, :, t * LANES:(t + 1) * LANES]


def pack_kernel(part_ref, noise_ref, pred_ref, true_ref, kind_ref, first_ref, last_ref, *, copies, tiles):
    span = BAND * LANES
    for ref, start in ((first_ref, 0), (last_ref, tiles * LANES - span)):
        sl = slice(start, start + span)
        for c in range(3):
            ref[c * copies:(c + 1) * copies, :] = pred_ref[c, :, sl] * 0.5
        ref[3 * copies:3 * copies + 3, :] = true_ref[:, sl] * 0.5
        ref[3 * copies + 3:3 * copies + 4, :] = jnp.where(kind_ref[:, sl] == 1, 15.0, 7.5)


VMEM = pl.BlockSpec(memory_space=pltpu.VMEM)
SMEM = pl.BlockSpec(memory_space=pltpu.SMEM)
PARAMS = pltpu.CompilerParams(vmem_limit_bytes=40 * 2**20)


def swap(x, axis, step):
    return lax.ppermute(x, axis, [(i, i ^ step) for i in range(lax.axis_size(axis))])


def shards(coords_pred, coords_true, atom_kind, partners, noise_level):
    copies, _, local = coords_pred.shape
    tiles = partners.shape[0]
    rows = 3 * copies
    size = lax.axis_size("res")
    kind = atom_kind[None]
    coords_pred = jnp.transpose(coords_pred, (1, 0, 2))
    base = (lax.axis_index("res") * tiles)[None].astype(jnp.int32)
    stats_shape = jax.ShapeDtypeStruct((2, 8, LANES), F32)

    block = jax.ShapeDtypeStruct((rows + 4, BAND * LANES), F32)
    first, last = pl.pallas_call(
        functools.partial(pack_kernel, copies=copies, tiles=tiles),
        in_specs=[SMEM, SMEM] + [VMEM] * 3,
        out_specs=[VMEM, VMEM],
        out_shape=[block, block],
        name="pack",
    )(partners, noise_level, coords_pred, coords_true, kind)
    forward = [(i, i + 1) for i in range(size - 1)]
    low = lax.ppermute(last, "res", forward)
    high = lax.ppermute(first, "res", [(b, a) for a, b in forward])

    pull, stats = pl.pallas_call(
        functools.partial(interior_kernel, copies=copies, tiles=tiles),
        in_specs=[SMEM, SMEM] + [VMEM] * 3,
        out_specs=[VMEM, VMEM],
        out_shape=[jax.ShapeDtypeStruct((3, copies, local), F32), stats_shape],
        scratch_shapes=[pltpu.VMEM((6, 16, LANES), F32), pltpu.VMEM((2, 6, 16, LANES), F32), Engine.self_scratch(copies)] + Engine.scratch(tiles, copies, BAND * tiles),
        compiler_params=PARAMS,
        cost_estimate=pl.CostEstimate(flops=10**8, bytes_accessed=10**6, transcendentals=10**7),
        name="interior",
    )(base, partners, coords_pred, coords_true, kind)
    edge_pull, stats = pl.pallas_call(
        functools.partial(edge_kernel, copies=copies, tiles=tiles),
        in_specs=[SMEM, SMEM] + [VMEM] * 6,
        out_specs=[VMEM, VMEM],
        out_shape=[jax.ShapeDtypeStruct((3, copies, 2 * BAND * LANES), F32), stats_shape],
        scratch_shapes=[pltpu.VMEM((4 * BAND, 16, LANES), F32)] + Engine.scratch(4 * BAND, copies, BAND * (BAND + 1)),
        compiler_params=PARAMS,
        name="edges",
    )(base, partners, coords_pred, coords_true, kind, low, high, stats)

    step = 1
    while step < size:
        other = swap(stats, "res", step)
        total, error = two_sum(stats[0], other[0])
        stats = jnp.stack([total, (stats[1] + other[1]) + error])
        step *= 2

    copy_loss, total, maps, centre = pl.pallas_call(
        functools.partial(solve_kernel, copies=copies, atoms=local * size),
        in_specs=[VMEM, SMEM],
        out_specs=[SMEM] + [VMEM] * 3,
        out_shape=[
            jax.ShapeDtypeStruct((copies,), F32),
            jax.ShapeDtypeStruct((8, LANES), F32),
            jax.ShapeDtypeStruct((14, copies, LANES), F32),
            jax.ShapeDtypeStruct((8, LANES), F32),
        ],
        scratch_shapes=[pltpu.VMEM((2, LANES, LANES), F32)],
        name="solve",
    )(stats, noise_level)
    step = 1
    while step < lax.axis_size("samp"):
        total = total + swap(total, "samp", step)
        step *= 2
    mean_loss = total[0, 0] / (copies * lax.axis_size("samp"))
    grad = pl.pallas_call(
        functools.partial(gradient_kernel, copies=copies, tiles=tiles),
        in_specs=[VMEM] * 7,
        out_specs=VMEM,
        out_shape=jax.ShapeDtypeStruct((3, copies, local), F32),
        cost_estimate=pl.CostEstimate(flops=10**6, bytes_accessed=10**6, transcendentals=0),
        name="gradient",
    )(maps, centre, coords_pred, coords_true, kind, pull, edge_pull)
    return copy_loss, mean_loss, jnp.transpose(grad, (1, 0, 2))


def solution(mesh):
    in_specs = (P("samp", None, "res"), P(None, "res"), P("res"), P("res", None), P("samp"))
    out_specs = (P("samp"), P(), P("samp", None, "res"))
    return jax.shard_map(shards, mesh=mesh, in_specs=in_specs, out_specs=out_specs, check_vma=False)
```

time: 62 us -> 61.6 us (level); the launches traced: 62.5 us -> 60.9 us
  Pallas kernels: 26.2 us -> 28.1 us
  other arithmetic: 3.13 us -> 1.33 us
  between operations: 3.81 us -> 2.51 us
  starting transfers between devices: 20.5 us -> 19.8 us
    pallas_call x1 -> x3, Pallas kernels: 1.71 us -> 5.6 us  [the longest x1 2.14 us: shards(): pl.pallas_call(functools.partial(solve_kernel, copies=copies, atoms=local...]
    pallas_call x1, Pallas kernels: 3.17 us -> 0.97 us  [shards(): pl.pallas_call(functools.partial(edge_kernel, copies=copies, tiles=tiles)...]
    mul x2 -> x0, other arithmetic: 1.44 us -> none  [the longest x1 0.73 us: edge(): take(coords_pred).reshape(rows, -1) * 0.5]
    select_n x1 -> x0, other arithmetic: 0.75 us -> none  [edge(): cut = jnp.where(take(atom_kind) == 1, 15.0, 7.5).astype(F32)]
    ppermute x5, starting transfers between devices: 14.3 us -> 13.6 us  [swap(): lax.ppermute(x, axis, [(i, i ^ step) for i in range(lax.axis_size(axis))])]
    add x6 -> x5, other arithmetic: 0.04 us -> 0.71 us  [the longest x2 0.69 us: shards(): total = total + swap(total, 'samp', step)]
    reduce_sum x1 -> x0, other arithmetic: 0.65 us -> none  [shards(): total = jnp.sum(copy_loss)[None]]
  transfers between devices with their start and end apart: 7 -> 7, of which waited for: 5 -> 5; matrix products, arithmetic and copies ran while one was open for 2% -> 0% of each run, Pallas kernels for 34% -> 38%
where the time goes in v3:
time: 61.6 us; the launch traced here: 60.9 us
  Pallas kernels  28.1 us (46%)
  starting transfers between devices  19.8 us (32%)
  waiting for transfers between devices  6.51 us (11%)
  local copies, waits for them, and re-layouts  2.59 us (4%)
  between operations  2.51 us (4%)
  other arithmetic  1.33 us (2%)
    pallas_call x1, Pallas kernels, shards(): pl.pallas_call(functools.partial(interior_kernel, copies=copies, tiles=ti...  21.5 us
    ppermute x5, starting transfers between devices, swap(): lax.ppermute(x, axis, [(i, i ^ step) for i in range(lax.axis_size(axis))])  13.6 us
    ppermute x5, waiting for transfers between devices, swap(): lax.ppermute(x, axis, [(i, i ^ step) for i in range(lax.axis_size(axis))])  6.5 us
    ppermute x1, starting transfers between devices, shards(): low = lax.ppermute(last, 'res', forward)  4.96 us
    pallas_call x1, Pallas kernels, shards(): pl.pallas_call(functools.partial(solve_kernel, copies=copies, atoms=local...  2.14 us
    unnamed x13, local copies, waits for them, and re-layouts  2.07 us
    pallas_call x1, Pallas kernels, shards(): pl.pallas_call(functools.partial(gradient_kernel, copies=copies, tiles=ti...  1.84 us
    pallas_call x1, Pallas kernels, shards(): pl.pallas_call(functools.partial(pack_kernel, copies=copies, tiles=tiles)...  1.61 us
  transfers between devices with their start and end apart: 7, of which 5 were waited for; matrix products, arithmetic and copies ran while one was open for 0% of the time, Pallas kernels for 38%

profile of v3, /device:TPU:0, one launch (start us, length us, event | category | flops | bytes accessed | tf_op | source)
XLA Modules:
  0.0 60.9 jit_solution(12374408618365971854)
XLA Ops:
  0.6 0.0 copy-start
  0.6 1.4 %copy.10.part_ref = s32[24,5]{1,0:T(8,128)} copy(s32[24,5]{0,1:T(8,128)} %param.8) | data formatting | bytes 960 | tf_op args[3]
  2.0 0.0 copy-start.1
  2.0 0.0 copy-start.4
  2.0 1.6 %pack.1 = (f32[16,256]{1,0:T(8,128)}, f32[16,256]{1,0:T(8,128)}) custom-call(s32[24,5]{1,0:T(8,128)} %copy.10.part_ref, f32[4]{0:T(128)} %noise_ref.3, f32[3,4,3072]{2,1,0:T(4,128)} %bitcast.5, f32[3,3072]{1,0:T(4,128)} %true_ref.7, s32[1,3072]{1,0:T(1,128)} %bitcast.9), custom_call_target="tpu_custom_call" | custom-call | tf_op jit(solution)/shard_map/pack/pallas_call | solution.py:616
  3.7 5.0 %collective-permute-start = (f32[16,256]{1,0:T(8,128)}, f32[16,256]{1,0:T(8,128)S(1)}, u32[]{:S(2)}, u32[]{:S(2)}) collective-permute-start(f32[16,256]{1,0:T(8,128)} %get-tuple-element.13), channel_id=1, source_target_pairs={{0,4},{4,8},{8,12},{12,16},{16,20},{20,24},{24,28},{1,5},{5,9},{9,... | collective-permute-start | bytes 49160 | tf_op jit(solution)/shard_map/ppermute | solution.py:624
  8.6 1.3 %collective-permute-start.1 = (f32[16,256]{1,0:T(8,128)}, f32[16,256]{1,0:T(8,128)S(1)}, u32[]{:S(2)}, u32[]{:S(2)}) collective-permute-start(f32[16,256]{1,0:T(8,128)} %get-tuple-element.14), channel_id=1, source_target_pairs={{4,0},{8,4},{12,8},{16,12},{20,16},{24,20},{28,24},{5,1},{9,5},{13... | collective-permute-start | bytes 49160 | tf_op jit(solution)/shard_map/ppermute | solution.py:625
  9.9 0.0 copy-done
  9.9 0.0 copy-done.1
  10.0 0.0 copy-done.4
  10.0 0.0 copy-done.3
  10.0 21.5 %interior.1 = (f32[3,4,3072]{2,1,0:T(4,128)S(1)}, f32[2,8,128]{2,1,0:T(8,128)S(1)}) custom-call(s32[1]{0:T(128)} %bitcast.base_ref, s32[24,5]{1,0:T(8,128)S(1)} %copy-done.3, f32[3,4,3072]{2,1,0:T(4,128)S(1)} %bitcast.7, f32[3,3072]{1,0:T(4,128)S(1)} %copy-done.1, s32[1,3072]{1,0:T(1,128)S(1)} %bitcast.11), custom_call_target="tpu_custom_call" | custom-call | flops 100000000 | bytes 1000000 | tf_op jit(solution)/shard_map/interior/pallas_call | solution.py:627
  31.5 0.7 %copy-done.2 = f32[3,4,3072]{2,1,0:T(4,128)} copy-done((f32[3,4,3072]{2,1,0:T(4,128)}, f32[3,4,3072]{2,1,0:T(4,128)S(1)}, u32[]{:S(2)}) %copy-start.2) | copy-done | bytes 147480
  32.1 0.0 collective-permute-done.low_ref
  32.2 0.0 collective-permute-done.1.high_ref
  32.2 1.0 %edges.1 = (f32[3,4,512]{2,1,0:T(4,128)S(1)}, f32[2,8,128]{2,1,0:T(8,128)S(1)}) custom-call(s32[1]{0:T(128)} %bitcast.base_ref, s32[24,5]{1,0:T(8,128)S(1)} %copy-done.3, f32[3,4,3072]{2,1,0:T(4,128)S(1)} %bitcast.8, f32[3,3072]{1,0:T(4,128)S(1)} %copy-done.1, s32[1,3072]{1,0:T(1,128)S(1)} %bitcast.12, f32[16,256]{1,0:T(8,128)S(1)} %collective-permute-done.low_ref, ...), custom_call_target="tpu_custom_call" | custom-call | tf_op jit(solution)/shard_map/edges/pallas_call | solution.py:637
  33.1 2.3 %collective-permute-start.2 = (f32[2,8,128]{2,1,0:T(8,128)S(1)}, f32[2,8,128]{2,1,0:T(8,128)S(1)}, u32[]{:S(2)}, u32[]{:S(2)}) collective-permute-start(f32[2,8,128]{2,1,0:T(8,128)S(1)} %get-tuple-element.16), channel_id=1, source_target_pairs={{0,4},{4,0},{8,12},{12,8},{16,20},{20,16},{24,28},{28,24},{1,5},{5... | collective-permute-start | bytes 24584 | tf_op jit(solution)/shard_map/ppermute | solution.py:602
  35.4 1.6 %collective-permute-done.2 = f32[2,8,128]{2,1,0:T(8,128)S(1)} collective-permute-done((f32[2,8,128]{2,1,0:T(8,128)S(1)}, f32[2,8,128]{2,1,0:T(8,128)S(1)}, u32[]{:S(2)}, u32[]{:S(2)}) %collective-permute-start.2) | collective-permute-done | bytes 8224 | tf_op jit(solution)/shard_map/ppermute | solution.py:602
  37.1 6.5 %collective-permute-start.3 = (f32[2,8,128]{2,1,0:T(8,128)S(1)}, f32[2,8,128]{2,1,0:T(8,128)S(1)}, u32[]{:S(2)}, u32[]{:S(2)}) collective-permute-start(f32[2,8,128]{2,1,0:T(8,128)S(1)} %pad_maximum_fusion), channel_id=1, source_target_pairs={{0,8},{4,12},{8,0},{12,4},{16,24},{20,28},{24,16},{28,20},{1,9},{5... | collective-permute-start | bytes 24584 | tf_op jit(solution)/shard_map/ppermute | solution.py:602
  43.5 1.6 %collective-permute-done.3 = f32[2,8,128]{2,1,0:T(8,128)S(1)} collective-permute-done((f32[2,8,128]{2,1,0:T(8,128)S(1)}, f32[2,8,128]{2,1,0:T(8,128)S(1)}, u32[]{:S(2)}, u32[]{:S(2)}) %collective-permute-start.3) | collective-permute-done | bytes 8224 | tf_op jit(solution)/shard_map/ppermute | solution.py:602
  45.2 0.0 copy-done.5
  45.2 3.2 %collective-permute-start.4 = (f32[2,8,128]{2,1,0:T(8,128)S(1)}, f32[2,8,128]{2,1,0:T(8,128)S(1)}, u32[]{:S(2)}, u32[]{:S(2)}) collective-permute-start(f32[2,8,128]{2,1,0:T(8,128)S(1)} %pad_maximum_fusion.1), channel_id=1, source_target_pairs={{0,16},{4,20},{8,24},{12,28},{16,0},{20,4},{24,8},{28,12},{1,17},{... | collective-permute-start | bytes 24584 | tf_op jit(solution)/shard_map/ppermute | solution.py:602
  48.4 1.6 %collective-permute-done.4 = f32[2,8,128]{2,1,0:T(8,128)S(1)} collective-permute-done((f32[2,8,128]{2,1,0:T(8,128)S(1)}, f32[2,8,128]{2,1,0:T(8,128)S(1)}, u32[]{:S(2)}, u32[]{:S(2)}) %collective-permute-start.4) | collective-permute-done | bytes 8224 | tf_op jit(solution)/shard_map/ppermute | solution.py:602
  50.1 0.6 pad_maximum_fusion.2.stat_ref
  50.7 2.1 %solve.1 = (f32[4]{0:T(128)}, f32[8,128]{1,0:T(8,128)}, f32[14,4,128]{2,1,0:T(4,128)}, f32[8,128]{1,0:T(8,128)}) custom-call(f32[2,8,128]{2,1,0:T(8,128)} %pad_maximum_fusion.2.stat_ref, f32[4]{0:T(128)} %noise_ref.3), custom_call_target="tpu_custom_call" | custom-call | tf_op jit(solution)/shard_map/solve/pallas_call | solution.py:654
  52.8 0.1 collective-permute-start.5
  52.9 1.4 %collective-permute-done.5 = f32[8,128]{1,0:T(8,128)S(1)} collective-permute-done((f32[8,128]{1,0:T(8,128)}, f32[8,128]{1,0:T(8,128)S(1)}, u32[]{:S(2)}, u32[]{:S(2)}) %collective-permute-start.5) | collective-permute-done | bytes 4128 | tf_op jit(solution)/shard_map/ppermute | solution.py:602
  54.3 0.7 %add.84 = f32[8,128]{1,0:T(8,128)S(1)} add(f32[8,128]{1,0:T(8,128)} %get-tuple-element.18, f32[8,128]{1,0:T(8,128)S(1)} %collective-permute-done.5) | non-fusion elementwise | flops 1024 | bytes 12288 | tf_op jit(solution)/shard_map/add | solution.py:669
  54.9 1.5 %collective-permute-start.6 = (f32[8,128]{1,0:T(8,128)S(1)}, f32[8,128]{1,0:T(8,128)S(1)}, u32[]{:S(2)}, u32[]{:S(2)}) collective-permute-start(f32[8,128]{1,0:T(8,128)S(1)} %add.84), channel_id=1, source_target_pairs={{0,2},{1,3},{2,0},{3,1},{4,6},{5,7},{6,4},{7,5},{8,10},{9,11},{10,... | collective-permute-start | bytes 12296 | tf_op jit(solution)/shard_map/ppermute | solution.py:602
  56.5 1.8 %gradient.1 = f32[3,4,3072]{2,1,0:T(4,128)} custom-call(f32[14,4,128]{2,1,0:T(4,128)} %get-tuple-element.19.m_ref, f32[8,128]{1,0:T(8,128)} %get-tuple-element.20.k_ref, f32[3,4,3072]{2,1,0:T(4,128)} %bitcast.6, f32[3,3072]{1,0:T(4,128)} %true_ref.7, s32[1,3072]{1,0:T(1,128)} %bitcast.10, f32[3,4,3072]{2,1,0:T(4,128)} %copy-done.2, f32[3,4,512]{2,1,0:T(4,128)} %copy-done.5), custom_call_target="tpu_custom_call" | custom-call | flops 1000000 | bytes 1000000 | tf_op jit(solution)/shard_map/gradient/pallas_call | solution.py:672
  58.3 0.2 collective-permute-done.6
  58.6 0.5 slice.35
  (9 shorter events, 0.0 us)
Async XLA Ops:
  0.6 9.3 %copy-start = (f32[4,3,3072]{2,0,1:T(4,128)S(1)}, f32[4,3,3072]{2,0,1:T(4,128)}, u32[]{:S(2)}) copy-start(f32[4,3,3072]{2,0,1:T(4,128)} %param.5) | copy-start | bytes 442372
  2.0 7.9 %copy-start.1 = (f32[3,3072]{1,0:T(4,128)S(1)}, f32[3,3072]{1,0:T(4,128)}, u32[]{:S(2)}) copy-start(f32[3,3072]{1,0:T(4,128)} %true_ref.7) | copy-start | bytes 110596
  2.0 7.9 %copy-start.4 = (s32[3072]{0:T(1024)S(1)}, s32[3072]{0:T(1024)}, u32[]{:S(2)}) copy-start(s32[3072]{0:T(1024)} %param.7) | copy-start | bytes 36868
  3.7 6.3 %copy-start.3 = (s32[24,5]{1,0:T(8,128)S(1)}, s32[24,5]{1,0:T(8,128)}, u32[]{:S(2)}) copy-start(s32[24,5]{1,0:T(8,128)} %copy.10.part_ref) | copy-start | bytes 1444
  3.7 28.5 %collective-permute-start = (f32[16,256]{1,0:T(8,128)}, f32[16,256]{1,0:T(8,128)S(1)}, u32[]{:S(2)}, u32[]{:S(2)}) collective-permute-start(f32[16,256]{1,0:T(8,128)} %get-tuple-element.13), channel_id=1, source_target_pairs={{0,4},{4,8},{8,12},{12,16},{16,20},{20,24},{24,28},{1,5},{5,9},{9,... | collective-permute-start | bytes 49160 | tf_op jit(solution)/shard_map/ppermute | solution.py:624
  8.6 23.5 %collective-permute-start.1 = (f32[16,256]{1,0:T(8,128)}, f32[16,256]{1,0:T(8,128)S(1)}, u32[]{:S(2)}, u32[]{:S(2)}) collective-permute-start(f32[16,256]{1,0:T(8,128)} %get-tuple-element.14), channel_id=1, source_target_pairs={{4,0},{8,4},{12,8},{16,12},{20,16},{24,20},{28,24},{5,1},{9,5},{13... | collective-permute-start | bytes 49160 | tf_op jit(solution)/shard_map/ppermute | solution.py:625
  31.5 0.7 %copy-start.2 = (f32[3,4,3072]{2,1,0:T(4,128)}, f32[3,4,3072]{2,1,0:T(4,128)S(1)}, u32[]{:S(2)}) copy-start(f32[3,4,3072]{2,1,0:T(4,128)S(1)} %get-tuple-element.21.pull_ref) | copy-start | bytes 442372
  33.1 12.1 %copy-start.5 = (f32[3,4,512]{2,1,0:T(4,128)}, f32[3,4,512]{2,1,0:T(4,128)S(1)}, u32[]{:S(2)}) copy-start(f32[3,4,512]{2,1,0:T(4,128)S(1)} %get-tuple-element.22.edge_ref) | copy-start | bytes 73732
  33.1 3.9 %collective-permute-start.2 = (f32[2,8,128]{2,1,0:T(8,128)S(1)}, f32[2,8,128]{2,1,0:T(8,128)S(1)}, u32[]{:S(2)}, u32[]{:S(2)}) collective-permute-start(f32[2,8,128]{2,1,0:T(8,128)S(1)} %get-tuple-element.16), channel_id=1, source_target_pairs={{0,4},{4,0},{8,12},{12,8},{16,20},{20,16},{24,28},{28,24},{1,5},{5... | collective-permute-start | bytes 24584 | tf_op jit(solution)/shard_map/ppermute | solution.py:602
  37.1 8.1 %collective-permute-start.3 = (f32[2,8,128]{2,1,0:T(8,128)S(1)}, f32[2,8,128]{2,1,0:T(8,128)S(1)}, u32[]{:S(2)}, u32[]{:S(2)}) collective-permute-start(f32[2,8,128]{2,1,0:T(8,128)S(1)} %pad_maximum_fusion), channel_id=1, source_target_pairs={{0,8},{4,12},{8,0},{12,4},{16,24},{20,28},{24,16},{28,20},{1,9},{5... | collective-permute-start | bytes 24584 | tf_op jit(solution)/shard_map/ppermute | solution.py:602
  45.2 4.9 %collective-permute-start.4 = (f32[2,8,128]{2,1,0:T(8,128)S(1)}, f32[2,8,128]{2,1,0:T(8,128)S(1)}, u32[]{:S(2)}, u32[]{:S(2)}) collective-permute-start(f32[2,8,128]{2,1,0:T(8,128)S(1)} %pad_maximum_fusion.1), channel_id=1, source_target_pairs={{0,16},{4,20},{8,24},{12,28},{16,0},{20,4},{24,8},{28,12},{1,17},{... | collective-permute-start | bytes 24584 | tf_op jit(solution)/shard_map/ppermute | solution.py:602
  52.8 1.4 %collective-permute-start.5 = (f32[8,128]{1,0:T(8,128)}, f32[8,128]{1,0:T(8,128)S(1)}, u32[]{:S(2)}, u32[]{:S(2)}) collective-permute-start(f32[8,128]{1,0:T(8,128)} %get-tuple-element.18), channel_id=1, source_target_pairs={{0,1},{1,0},{2,3},{3,2},{4,5},{5,4},{6,7},{7,6},{8,9},{9,8},{10,11... | collective-permute-start | bytes 12296 | tf_op jit(solution)/shard_map/ppermute | solution.py:602
  54.9 3.6 %collective-permute-start.6 = (f32[8,128]{1,0:T(8,128)S(1)}, f32[8,128]{1,0:T(8,128)S(1)}, u32[]{:S(2)}, u32[]{:S(2)}) collective-permute-start(f32[8,128]{1,0:T(8,128)S(1)} %add.84), channel_id=1, source_target_pairs={{0,2},{1,3},{2,0},{3,1},{4,6},{5,7},{6,4},{7,5},{8,10},{9,11},{10,... | collective-permute-start | bytes 12296 | tf_op jit(solution)/shard_map/ppermute | solution.py:602

commit v4 on v3

--- a/solution.py
+++ b/solution.py
@@ -80,9 +80,23 @@
 
 def listed(part_ref, owner, other):
     hit = jnp.bool_(False)
-    for k in range(1, part_ref.shape[1]):
-        hit = hit | (part_ref[owner, k] == other)
+    for k in range(1, part_ref.shape[0]):
+        hit = hit | (part_ref[k, owner] == other)
     return hit
+
+
+def spread(steps, work, ticks):
+    state = [0, 0]
+
+    def tick():
+        state[0] += 1
+        while state[1] < len(steps) and state[1] * ticks * 3 < state[0] * len(steps) * 4:
+            steps[state[1]]()
+            state[1] += 1
+
+    work(tick)
+    for step in steps[state[1]:]:
+        step()
 
 
 class Engine:
@@ -180,13 +194,12 @@
         for h in range(self.twos + 1):
             self.left[t, h] = stack(groups[2 * h], groups[2 * h + 1], 0).T.astype(BF16)
 
-    def build(self, slot, k, g, j):
-        for s in range(self.copies + 1):
-            y = self.v[j, s] - self.centre[g, s]
-            norm = jnp.sum(y * y, axis=0, keepdims=True)
-            a, b, c = split3((self.unit(3) + self.unit(5)) - 2.0 * y + norm * self.unit(4))
-            q, m = 64 * (s % 2), LANES * (s % 2)
-            self.right[slot][k, s // 2, q:q + 64, m:m + LANES] = jnp.concatenate([a, b, a, c, b, a, c, b], axis=0).astype(BF16)
+    def build(self, slot, k, g, j, s):
+        y = self.v[j, s] - self.centre[g, s]
+        norm = jnp.sum(y * y, axis=0, keepdims=True)
+        a, b, c = split3((self.unit(3) + self.unit(5)) - 2.0 * y + norm * self.unit(4))
+        q, m = 64 * (s % 2), LANES * (s % 2)
+        self.right[slot][k, s // 2, q:q + 64, m:m + LANES] = jnp.concatenate([a, b, a, c, b, a, c, b], axis=0).astype(BF16)
 
     def squares(self, slot, k, g, h):
         return dot(self.left[g, h], self.right[slot][k, h])
@@ -202,7 +215,7 @@
         shape = (k.stop - k.start, LANES)
         return lax.broadcasted_iota(jnp.int32, shape, 1) > lax.broadcasted_iota(jnp.int32, shape, 0) + k.start
 
-    def weigh(self, slot, cuts, share, shared):
+    def weigh(self, slot, cuts, share, shared, tick):
         total = jnp.zeros((8, LANES), F32)
         for b in range(16):
             k = slice(8 * b, 8 * b + 8)
@@ -218,9 +231,10 @@
             self.weight[slot][k, :] = w
             self.minus[slot][k, :] = -w
             total = total + w
+            tick()
         self.count[...] += total * share
 
-    def factor(self, slot, share, shared):
+    def factor(self, slot, share, shared, tick):
         for s in range(self.copies):
             h, m = s // 2, LANES * (s % 2)
             score = jnp.zeros((8, LANES), F32)
@@ -242,6 +256,7 @@
                     part = (high * self.tri[i, k, :], low * self.tri[i, k, :]) if shared else (high, low)
                     for x, start in zip(part, (16 * q, LANES + 16 * q)):
                         self.f[slot][i, h, start:start + 16, m:m + LANES] = x
+                tick()
             self.score[s] += score * share
 
     @staticmethod
@@ -257,61 +272,65 @@
         return self.fold(dot_nt(p, stack(one, two, 0)))
 
     def cross_build(self, item, slot):
-        self.build(slot, 0, item[0], item[1])
+        return [functools.partial(self.build, slot, 0, item[0], item[1], s) for s in range(self.copies + 1)]
 
     def cross_measure(self, item, slot):
-        for h in [self.twos, *range(self.twos)]:
+        def step(h):
             self.d[slot][0, h] = self.squares(slot, 0, item[0], h)
 
-    def cross_factor(self, item, slot):
+        return [functools.partial(step, h) for h in [self.twos, *range(self.twos)]]
+
+    def cross_factor(self, item, slot, tick):
         share = item[2].astype(F32) * 0.5
-        self.weigh(slot, [self.cut[item[1]]], share, False)
-        self.factor(slot, share, False)
+        self.weigh(slot, [self.cut[item[1]]], share, False, tick)
+        self.factor(slot, share, False, tick)
+
+    def add(self, t, h, parts):
+        for q in range(2):
+            self.acc[t, 2 * h + q] += parts[q]
 
     def cross_collect(self, item, slot):
-        g, j = item[0], item[1]
+        steps = []
         for h in range(self.twos):
-            f = self.f[slot][0, h]
-            x = self.along_j(self.point[g, h], f)
-            y = self.along_i(self.point[j, h], f)
-            for k in range(2):
-                self.acc[j, 2 * h + k] += x[k]
-                self.acc[g, 2 * h + k] += y[k]
+            steps.append(lambda h=h: self.add(item[1], h, self.along_j(self.point[item[0], h], self.f[slot][0, h])))
+            steps.append(lambda h=h: self.add(item[0], h, self.along_i(self.point[item[1], h], self.f[slot][0, h])))
+        return steps
 
     def self_build(self, item, slot):
-        for k in range(2):
-            self.build(slot, k, item[k], item[k])
+        return [functools.partial(self.build, slot, k, item[k], item[k], s) for s in range(self.copies + 1) for k in range(2)]
 
     def self_measure(self, item, slot):
-        for h in [self.twos, *range(self.twos)]:
-            for k in range(2):
-                self.d[slot][k, h] = self.squares(slot, k, item[k], h)
-
-    def self_factor(self, item, slot):
-        self.weigh(slot, [self.cut[item[0]], self.cut[item[1]]], 1.0, True)
-        self.factor(slot, 1.0, True)
+        def step(h, k):
+            self.d[slot][k, h] = self.squares(slot, k, item[k], h)
+
+        return [functools.partial(step, h, k) for h in [self.twos, *range(self.twos)] for k in range(2)]
+
+    def self_factor(self, item, slot, tick):
+        self.weigh(slot, [self.cut[item[0]], self.cut[item[1]]], 1.0, True, tick)
+        self.factor(slot, 1.0, True, tick)
 
     def self_collect(self, item, slot):
+        steps = []
         for h in range(self.twos):
             for k in range(2):
-                f = self.f[slot][k, h]
-                x = self.along_j(self.point[item[k], h], f)
-                y = self.along_i(self.point[item[k], h], f)
-                for q in range(2):
-                    self.acc[item[k], 2 * h + q] += x[q] + y[q]
+                for side in (self.along_j, self.along_i):
+                    steps.append(lambda h=h, k=k, side=side: self.add(item[k], h, side(self.point[item[k], h], self.f[slot][k, h])))
+        return steps
 
     def half(self, kind, items, slot):
         last, now, soon, later = items
-        getattr(self, kind + "_collect")(last, 1 - slot)
-        getattr(self, kind + "_measure")(soon, 1 - slot)
-        getattr(self, kind + "_build")(later, 1 - slot)
-        getattr(self, kind + "_factor")(now, slot)
+        steps = getattr(self, kind + "_collect")(last, 1 - slot)
+        steps += getattr(self, kind + "_measure")(soon, 1 - slot)
+        steps += getattr(self, kind + "_build")(later, 1 - slot)
+        spread(steps, lambda tick: getattr(self, kind + "_factor")(now, slot, tick), 16 + 8 * self.copies)
 
     def begin_list(self, kind, item, n):
-        getattr(self, kind + "_build")(item(0), 0)
-        getattr(self, kind + "_measure")(item(0), 0)
+        steps = getattr(self, kind + "_build")(item(0), 0)
+        steps += getattr(self, kind + "_measure")(item(0), 0)
         for i in (1, 2):
-            getattr(self, kind + "_build")(item(jnp.minimum(i, n - 1)), i % 2)
+            steps += getattr(self, kind + "_build")(item(jnp.minimum(i, n - 1)), i % 2)
+        for step in steps:
+            step()
 
     def run_list(self, kind, item, n, dummy):
         def at(p):
@@ -336,22 +355,23 @@
         return jnp.broadcast_to(jnp.sum(total, axis=1, keepdims=True), (8, LANES))
 
 
-def finish_list(e, item, n, dummy, also=lambda: None):
+def finish_list(e, item, n, dummy, also=()):
+    also = list(also)
+
     @pl.when(n % 2 == 1)
     def _():
         before = tuple(jnp.where(n > 1, z, dummy) for z in item(jnp.maximum(n - 2, 0)))
-        also()
-        e.cross_collect(before, 1)
-        e.cross_factor(item(n - 1), 0)
-        e.cross_collect(item(n - 1), 0)
+        spread(also + e.cross_collect(before, 1), lambda tick: e.cross_factor(item(n - 1), 0, tick), 16 + 8 * e.copies)
+        for step in e.cross_collect(item(n - 1), 0):
+            step()
 
     @pl.when(n % 2 == 0)
     def _():
-        also()
-        e.cross_collect(item(n - 1), 1)
-
-
-def interior_kernel(base_ref, part_ref, pred_ref, true_ref, kind_ref, pull_ref, stat_ref, x_ref, mom_ref, self_refs, *scratch, copies, tiles):
+        for step in also + e.cross_collect(item(n - 1), 1):
+            step()
+
+
+def interior_kernel(base_ref, part_ref, noise_ref, pred_ref, true_ref, kind_ref, pull_ref, stat_ref, noise_rows_ref, x_ref, mom_ref, self_refs, *scratch, copies, tiles):
     e = Engine(copies, scratch)
     own = e.for_self(self_refs)
     base = base_ref[0]
@@ -416,7 +436,7 @@
     e.begin_list("cross", item, n)
     own.run_list("self", twin, half, tiles)
     e.run_list("cross", item, n, tiles)
-    finish_list(e, item, n, tiles, lambda: own.self_collect(twin(half - 1), 1))
+    finish_list(e, item, n, tiles, own.self_collect(twin(half - 1), 1))
 
     @pl.loop(0, tiles // unroll)
     def _(m):
@@ -430,6 +450,11 @@
 
     stat_ref[0] = moments[0] + e.scores(mom_ref[0, 5, 0:1, :])
     stat_ref[1] = moments[1]
+    row = lax.broadcasted_iota(jnp.int32, (copies, LANES), 0)
+    noise = jnp.zeros((copies, LANES), F32)
+    for s in range(copies):
+        noise = jnp.where(row == s, noise_ref[s], noise)
+    noise_rows_ref[...] = noise
 
 
 def edge_kernel(base_ref, part_ref, pred_ref, true_ref, kind_ref, low_ref, high_ref, stat_ref, pull_ref, out_ref, x_ref, *scratch, copies, tiles):
@@ -482,11 +507,12 @@
     out_ref[1] = stat_ref[1]
 
 
-def solve_kernel(stat_ref, noise_ref, loss_ref, sum_ref, m_ref, k_ref, s_ref, *, copies, atoms):
+def solve_kernel(stat_ref, other_ref, noise_ref, loss_ref, sum_ref, m_ref, k_ref, s_ref, *, copies, atoms):
     rows = 3 * copies
-    for part in range(2):
-        column = jnp.broadcast_to(stat_ref[part, 0:1, :], (LANES, LANES)).T
-        s_ref[part] = column
+    stats, error = two_sum(stat_ref[0], other_ref[0])
+    low = (stat_ref[1] + other_ref[1]) + error
+    for part, x in enumerate((stats, low)):
+        s_ref[part] = jnp.broadcast_to(x[0:1], (LANES, LANES)).T
 
     def per_copy(c, q, scale):
         return tuple(s_ref[part, 16 * q + c * copies:16 * q + (c + 1) * copies, :] * scale for part in range(2))
@@ -497,9 +523,9 @@
     def wide(x):
         return tuple(jnp.broadcast_to(v, (copies, LANES)) for v in x)
 
-    weight_sum = jnp.broadcast_to(stat_ref[0, copies + 3:copies + 4, :], (copies, LANES))
-    count = jnp.broadcast_to(stat_ref[0, copies + 2:copies + 3, :], (copies, LANES)) * 16.0
-    score = stat_ref[0, 2:copies + 2, :] * 2.0 + 0.5 * count
+    weight_sum = jnp.broadcast_to(stats[copies + 3:copies + 4], (copies, LANES))
+    count = jnp.broadcast_to(stats[copies + 2:copies + 3], (copies, LANES)) * 16.0
+    score = stats[2:copies + 2] * 2.0 + 0.5 * count
     pred_sum = [wide(per_copy(c, 3, 2.0)) for c in range(3)]
     true_sum = [wide(shared(rows + c, 3, 2.0)) for c in range(3)]
     pred_mean = [pair_div(x, weight_sum) for x in pred_sum]
@@ -545,10 +571,7 @@
                 gram = (2.0 * gram[0], 2.0 * gram[1])
             square = pair_add(square, pair_mul(gram, ct[d, e]))
 
-    row = lax.broadcasted_iota(jnp.int32, (copies, LANES), 0)
-    noise = nothing
-    for s in range(copies):
-        noise = jnp.where(row == s, noise_ref[s], noise)
+    noise = noise_ref[...]
     loss_weight = (noise * noise + SIGMA * SIGMA) / (noise * SIGMA * (noise * SIGMA))
     mean_square = (square[0] + square[1]) / (3.0 * weight_sum)
     loss = loss_weight * mean_square + 1.0 - score / count
@@ -583,7 +606,7 @@
             grad_ref[c, :, start:start + LANES] -= m_ref[13] * edge_ref[c, :, t * LANES:(t + 1) * LANES]
 
 
-def pack_kernel(part_ref, noise_ref, pred_ref, true_ref, kind_ref, first_ref, last_ref, *, copies, tiles):
+def pack_kernel(pred_ref, true_ref, kind_ref, first_ref, last_ref, *, copies, tiles):
     span = BAND * LANES
     for ref, start in ((first_ref, 0), (last_ref, tiles * LANES - span)):
         sl = slice(start, start + span)
@@ -596,6 +619,7 @@
 VMEM = pl.BlockSpec(memory_space=pltpu.VMEM)
 SMEM = pl.BlockSpec(memory_space=pltpu.SMEM)
 PARAMS = pltpu.CompilerParams(vmem_limit_bytes=40 * 2**20)
+SMALL = pltpu.CompilerParams(vmem_limit_bytes=4 * 2**20)
 
 
 def swap(x, axis, step):
@@ -609,31 +633,33 @@
     size = lax.axis_size("res")
     kind = atom_kind[None]
     coords_pred = jnp.transpose(coords_pred, (1, 0, 2))
+    partners = partners.T
     base = (lax.axis_index("res") * tiles)[None].astype(jnp.int32)
     stats_shape = jax.ShapeDtypeStruct((2, 8, LANES), F32)
 
     block = jax.ShapeDtypeStruct((rows + 4, BAND * LANES), F32)
     first, last = pl.pallas_call(
         functools.partial(pack_kernel, copies=copies, tiles=tiles),
-        in_specs=[SMEM, SMEM] + [VMEM] * 3,
+        in_specs=[VMEM] * 3,
         out_specs=[VMEM, VMEM],
         out_shape=[block, block],
+        compiler_params=SMALL,
         name="pack",
-    )(partners, noise_level, coords_pred, coords_true, kind)
+    )(coords_pred, coords_true, kind)
     forward = [(i, i + 1) for i in range(size - 1)]
     low = lax.ppermute(last, "res", forward)
     high = lax.ppermute(first, "res", [(b, a) for a, b in forward])
 
-    pull, stats = pl.pallas_call(
+    pull, stats, noise = pl.pallas_call(
         functools.partial(interior_kernel, copies=copies, tiles=tiles),
-        in_specs=[SMEM, SMEM] + [VMEM] * 3,
-        out_specs=[VMEM, VMEM],
-        out_shape=[jax.ShapeDtypeStruct((3, copies, local), F32), stats_shape],
+        in_specs=[SMEM, SMEM, SMEM] + [VMEM] * 3,
+        out_specs=[VMEM, VMEM, VMEM],
+        out_shape=[jax.ShapeDtypeStruct((3, copies, local), F32), stats_shape, jax.ShapeDtypeStruct((copies, LANES), F32)],
         scratch_shapes=[pltpu.VMEM((6, 16, LANES), F32), pltpu.VMEM((2, 6, 16, LANES), F32), Engine.self_scratch(copies)] + Engine.scratch(tiles, copies, BAND * tiles),
         compiler_params=PARAMS,
         cost_estimate=pl.CostEstimate(flops=10**8, bytes_accessed=10**6, transcendentals=10**7),
         name="interior",
-    )(base, partners, coords_pred, coords_true, kind)
+    )(base, partners, noise_level, coords_pred, coords_true, kind)
     edge_pull, stats = pl.pallas_call(
         functools.partial(edge_kernel, copies=copies, tiles=tiles),
         in_specs=[SMEM, SMEM] + [VMEM] * 6,
@@ -645,15 +671,17 @@
     )(base, partners, coords_pred, coords_true, kind, low, high, stats)
 
     step = 1
-    while step < size:
+    while True:
         other = swap(stats, "res", step)
+        step *= 2
+        if step == size:
+            break
         total, error = two_sum(stats[0], other[0])
         stats = jnp.stack([total, (stats[1] + other[1]) + error])
-        step *= 2
 
     copy_loss, total, maps, centre = pl.pallas_call(
         functools.partial(solve_kernel, copies=copies, atoms=local * size),
-        in_specs=[VMEM, SMEM],
+        in_specs=[VMEM] * 3,
         out_specs=[SMEM] + [VMEM] * 3,
         out_shape=[
             jax.ShapeDtypeStruct((copies,), F32),
@@ -662,8 +690,9 @@
             jax.ShapeDtypeStruct((8, LANES), F32),
         ],
         scratch_shapes=[pltpu.VMEM((2, LANES, LANES), F32)],
+        compiler_params=SMALL,
         name="solve",
-    )(stats, noise_level)
+    )(stats, other, noise)
     step = 1
     while step < lax.axis_size("samp"):
         total = total + swap(total, "samp", step)
@@ -675,6 +704,7 @@
         out_specs=VMEM,
         out_shape=jax.ShapeDtypeStruct((3, copies, local), F32),
         cost_estimate=pl.CostEstimate(flops=10**6, bytes_accessed=10**6, transcendentals=0),
+        compiler_params=SMALL,
         name="gradient",
     )(maps, centre, coords_pred, coords_true, kind, pull, edge_pull)
     return copy_loss, mean_loss, jnp.transpose(grad, (1, 0, 2))

time: 61.6 us -> 59.6 us (0.968); the launches traced: 60.9 us -> 59.7 us
  waiting for transfers between devices: 6.51 us -> 9.12 us
  Pallas kernels: 28.1 us -> 26.1 us
  starting transfers between devices: 19.8 us -> 18.3 us
  other arithmetic: 1.33 us -> 0.03 us
  local copies, waits for them, and re-layouts: 2.59 us -> 3.58 us
    ppermute x5, waiting for transfers between devices: 6.5 us -> 9.11 us  [swap(): lax.ppermute(x, axis, [(i, i ^ step) for i in range(lax.axis_size(axis))])]
    pallas_call x1, Pallas kernels: 21.5 us -> 23.2 us  [shards(): pl.pallas_call(functools.partial(interior_kernel, copies=copies, tiles=ti...]
    pallas_call x1, Pallas kernels: 1.61 us -> 0.01 us  [shards(): pl.pallas_call(functools.partial(pack_kernel, copies=copies, tiles=tiles)...]
    ppermute x5, starting transfers between devices: 13.6 us -> 12 us  [swap(): lax.ppermute(x, axis, [(i, i ^ step) for i in range(lax.axis_size(axis))])]
    pallas_call x1, Pallas kernels: 1.84 us -> 0.81 us  [shards(): pl.pallas_call(functools.partial(gradient_kernel, copies=copies, tiles=ti...]
    unnamed x13 -> x16, local copies, waits for them, and re-layouts: 2.07 us -> 3.07 us
    pallas_call x1, Pallas kernels: 2.14 us -> 1.29 us  [shards(): pl.pallas_call(functools.partial(solve_kernel, copies=copies, atoms=local...]
    add x2, other arithmetic: 0.69 us -> 0.01 us  [shards(): total = total + swap(total, 'samp', step)]
  transfers between devices with their start and end apart: 7 -> 7, of which waited for: 5 -> 5; matrix products, arithmetic and copies ran while one was open for 0% -> 0% of each run, Pallas kernels for 38% -> 40%
where the time goes in v4:
time: 59.6 us; the launch traced here: 59.7 us
  Pallas kernels  26.1 us (44%)
  starting transfers between devices  18.3 us (31%)
  waiting for transfers between devices  9.12 us (15%)
  local copies, waits for them, and re-layouts  3.58 us (6%)
  between operations  2.52 us (4%)
    pallas_call x1, Pallas kernels, shards(): pl.pallas_call(functools.partial(interior_kernel, copies=copies, tiles=ti...  23.2 us
    ppermute x5, starting transfers between devices, swap(): lax.ppermute(x, axis, [(i, i ^ step) for i in range(lax.axis_size(axis))])  12 us
    ppermute x5, waiting for transfers between devices, swap(): lax.ppermute(x, axis, [(i, i ^ step) for i in range(lax.axis_size(axis))])  9.11 us
    ppermute x1, starting transfers between devices, shards(): low = lax.ppermute(last, 'res', forward)  4.97 us
    unnamed x16, local copies, waits for them, and re-layouts  3.07 us
    pallas_call x1, Pallas kernels, shards(): pl.pallas_call(functools.partial(solve_kernel, copies=copies, atoms=local...  1.29 us
    ppermute x1, starting transfers between devices, shards(): high = lax.ppermute(first, 'res', [(b, a) for a, b in forward])  1.29 us
  transfers between devices with their start and end apart: 7, of which 5 were waited for; matrix products, arithmetic and copies ran while one was open for 0% of the time, Pallas kernels for 40%

profile of v4, /device:TPU:0, one launch (start us, length us, event | category | flops | bytes accessed | tf_op | source)
XLA Modules:
  0.0 59.7 jit_solution(15465558146409565444)
XLA Ops:
  0.6 0.0 copy-start
  0.6 0.9 %copy-done = f32[4,3,3072]{2,0,1:T(4,128)S(1)} copy-done((f32[4,3,3072]{2,0,1:T(4,128)S(1)}, f32[4,3,3072]{2,0,1:T(4,128)}, u32[]{:S(2)}) %copy-start) | copy-done | bytes 147480
  1.5 0.0 copy-start.2
  1.5 0.8 %copy-done.2 = f32[3,3072]{1,0:T(4,128)S(1)} copy-done((f32[3,3072]{1,0:T(4,128)S(1)}, f32[3,3072]{1,0:T(4,128)}, u32[]{:S(2)}) %copy-start.2) | copy-done | bytes 36888
  2.3 0.7 %copy-done.4 = s32[3072]{0:T(1024)S(1)} copy-done((s32[3072]{0:T(1024)S(1)}, s32[3072]{0:T(1024)}, u32[]{:S(2)}) %copy-start.4) | copy-done | bytes 12312
  3.1 0.0 copy-start.5
  3.1 5.0 %collective-permute-start = (f32[16,256]{1,0:T(8,128)S(1)}, f32[16,256]{1,0:T(8,128)S(1)}, u32[]{:S(2)}, u32[]{:S(2)}) collective-permute-start(f32[16,256]{1,0:T(8,128)S(1)} %get-tuple-element.14), channel_id=1, source_target_pairs={{0,4},{4,8},{8,12},{12,16},{16,20},{20,24},{24,28},{1,5},{5,9},{9,... | collective-permute-start | bytes 49160 | tf_op jit(solution)/shard_map/ppermute | solution.py:650
  8.1 1.3 %collective-permute-start.1 = (f32[16,256]{1,0:T(8,128)S(1)}, f32[16,256]{1,0:T(8,128)S(1)}, u32[]{:S(2)}, u32[]{:S(2)}) collective-permute-start(f32[16,256]{1,0:T(8,128)S(1)} %get-tuple-element.15), channel_id=1, source_target_pairs={{4,0},{8,4},{12,8},{16,12},{20,16},{24,20},{28,24},{5,1},{9,5},{13... | collective-permute-start | bytes 49160 | tf_op jit(solution)/shard_map/ppermute | solution.py:651
  9.4 0.0 copy-start.6
  9.4 0.0 copy-start.7
  9.4 0.0 copy-done.1
  9.4 0.0 copy-done.3
  9.4 0.0 copy-done.5
  9.4 0.6 %copy-done.6 = s32[24,5]{0,1:T(8,128)S(1)} copy-done((s32[24,5]{0,1:T(8,128)S(1)}, s32[24,5]{0,1:T(8,128)}, u32[]{:S(2)}) %copy-start.6) | copy-done | bytes 504
  10.1 0.0 copy-done.7
  10.1 23.2 %interior.1 = (f32[3,4,3072]{2,1,0:T(4,128)S(1)}, f32[2,8,128]{2,1,0:T(8,128)S(1)}, f32[4,128]{1,0:T(4,128)S(1)}) custom-call(s32[1]{0:T(128)} %bitcast.base_ref, s32[5,24]{1,0:T(8,128)S(1)} %bitcast.14, f32[4]{0:T(128)S(1)} %copy-done.7, f32[3,4,3072]{2,1,0:T(4,128)S(1)} %bitcast.7, f32[3,3072]{1,0:T(4,128)S(1)} %copy-done.3, s32[1,3072]{1,0:T(1,128)S(1)} %bitcast.11), custom_call_target="tpu_custom_call" | custom-call | flops 100000000 | bytes 1000000 | tf_op jit(solution)/shard_map/interior/pallas_call | solution.py:653
  33.3 0.0 collective-permute-done.low_ref
  33.3 0.0 collective-permute-done.1.high_ref
  33.3 0.8 %edges.1 = (f32[3,4,512]{2,1,0:T(4,128)S(1)}, f32[2,8,128]{2,1,0:T(8,128)S(1)}) custom-call(s32[1]{0:T(128)} %bitcast.base_ref, s32[5,24]{1,0:T(8,128)S(1)} %bitcast.15, f32[3,4,3072]{2,1,0:T(4,128)S(1)} %bitcast.8, f32[3,3072]{1,0:T(4,128)S(1)} %copy-done.3, s32[1,3072]{1,0:T(1,128)S(1)} %bitcast.12, f32[16,256]{1,0:T(8,128)S(1)} %collective-permute-done.low_ref, ...), custom_call_target="tpu_custom_call" | custom-call | tf_op jit(solution)/shard_map/edges/pallas_call | solution.py:663
  34.1 1.9 %collective-permute-start.2 = (f32[2,8,128]{2,1,0:T(8,128)S(1)}, f32[2,8,128]{2,1,0:T(8,128)S(1)}, u32[]{:S(2)}, u32[]{:S(2)}) collective-permute-start(f32[2,8,128]{2,1,0:T(8,128)S(1)} %get-tuple-element.17), channel_id=1, source_target_pairs={{0,4},{4,0},{8,12},{12,8},{16,20},{20,16},{24,28},{28,24},{1,5},{5... | collective-permute-start | bytes 24584 | tf_op jit(solution)/shard_map/ppermute | solution.py:626
  36.0 1.8 %collective-permute-done.2 = f32[2,8,128]{2,1,0:T(8,128)S(1)} collective-permute-done((f32[2,8,128]{2,1,0:T(8,128)S(1)}, f32[2,8,128]{2,1,0:T(8,128)S(1)}, u32[]{:S(2)}, u32[]{:S(2)}) %collective-permute-start.2) | collective-permute-done | bytes 8224 | tf_op jit(solution)/shard_map/ppermute | solution.py:626
  37.8 7.2 %collective-permute-start.3 = (f32[2,8,128]{2,1,0:T(8,128)S(1)}, f32[2,8,128]{2,1,0:T(8,128)S(1)}, u32[]{:S(2)}, u32[]{:S(2)}) collective-permute-start(f32[2,8,128]{2,1,0:T(8,128)S(1)} %pad_maximum_fusion), channel_id=1, source_target_pairs={{0,8},{4,12},{8,0},{12,4},{16,24},{20,28},{24,16},{28,20},{1,9},{5... | collective-permute-start | bytes 24584 | tf_op jit(solution)/shard_map/ppermute | solution.py:626
  45.0 1.6 %collective-permute-done.3 = f32[2,8,128]{2,1,0:T(8,128)S(1)} collective-permute-done((f32[2,8,128]{2,1,0:T(8,128)S(1)}, f32[2,8,128]{2,1,0:T(8,128)S(1)}, u32[]{:S(2)}, u32[]{:S(2)}) %collective-permute-start.3) | collective-permute-done | bytes 8224 | tf_op jit(solution)/shard_map/ppermute | solution.py:626
  46.6 1.3 %collective-permute-start.4 = (f32[2,8,128]{2,1,0:T(8,128)S(1)}, f32[2,8,128]{2,1,0:T(8,128)S(1)}, u32[]{:S(2)}, u32[]{:S(2)}) collective-permute-start(f32[2,8,128]{2,1,0:T(8,128)S(1)} %pad_maximum_fusion.1.stat_ref), channel_id=1, source_target_pairs={{0,16},{4,20},{8,24},{12,28},{16,0},{20,4},{24,8},{28,12},{1,17},{... | collective-permute-start | bytes 24584 | tf_op jit(solution)/shard_map/ppermute | solution.py:626
  47.9 3.3 %collective-permute-done.4.other_ref = f32[2,8,128]{2,1,0:T(8,128)S(1)} collective-permute-done((f32[2,8,128]{2,1,0:T(8,128)S(1)}, f32[2,8,128]{2,1,0:T(8,128)S(1)}, u32[]{:S(2)}, u32[]{:S(2)}) %collective-permute-start.4) | collective-permute-done | bytes 8224 | tf_op jit(solution)/shard_map/ppermute | solution.py:626
  51.2 1.3 %solve.1 = (f32[4]{0:T(128)}, f32[8,128]{1,0:T(8,128)S(1)}, f32[14,4,128]{2,1,0:T(4,128)S(1)}, f32[8,128]{1,0:T(8,128)S(1)}) custom-call(f32[2,8,128]{2,1,0:T(8,128)S(1)} %pad_maximum_fusion.1.stat_ref, f32[2,8,128]{2,1,0:T(8,128)S(1)} %collective-permute-done.4.other_ref, f32[4,128]{1,0:T(4,128)S(1)} %get-tuple-element.18.noise_ref), custom_call_target="tpu_custom_call" | custom-call | tf_op jit(solution)/shard_map/solve/pallas_call | solution.py:682
  52.5 0.1 collective-permute-start.5
  52.6 1.2 %collective-permute-done.5 = f32[8,128]{1,0:T(8,128)S(1)} collective-permute-done((f32[8,128]{1,0:T(8,128)S(1)}, f32[8,128]{1,0:T(8,128)S(1)}, u32[]{:S(2)}, u32[]{:S(2)}) %collective-permute-start.5) | collective-permute-done | bytes 4128 | tf_op jit(solution)/shard_map/ppermute | solution.py:626
  53.8 1.5 %collective-permute-start.6 = (f32[8,128]{1,0:T(8,128)S(1)}, f32[8,128]{1,0:T(8,128)S(1)}, u32[]{:S(2)}, u32[]{:S(2)}) collective-permute-start(f32[8,128]{1,0:T(8,128)S(1)} %add.53), channel_id=1, source_target_pairs={{0,2},{1,3},{2,0},{3,1},{4,6},{5,7},{6,4},{7,5},{8,10},{9,11},{10,... | collective-permute-start | bytes 12296 | tf_op jit(solution)/shard_map/ppermute | solution.py:626
  55.3 0.8 %gradient.1 = f32[3,4,3072]{2,1,0:T(4,128)} custom-call(f32[14,4,128]{2,1,0:T(4,128)S(1)} %get-tuple-element.21.m_ref, f32[8,128]{1,0:T(8,128)S(1)} %get-tuple-element.22.k_ref, f32[3,4,3072]{2,1,0:T(4,128)S(1)} %bitcast.9, f32[3,3072]{1,0:T(4,128)S(1)} %copy-done.3, s32[1,3072]{1,0:T(1,128)S(1)} %bitcast.13, f32[3,4,3072]{2,1,0:T(4,128)S(1)} %get-tuple-element.23.pull_ref, ...), custom_call_target="tpu_custom_call" | custom-call | flops 1000000 | bytes 1000000 | tf_op jit(solution)/shard_map/gradient/pallas_call | solution.py:701
  56.1 1.3 %collective-permute-done.6 = f32[8,128]{1,0:T(8,128)S(1)} collective-permute-done((f32[8,128]{1,0:T(8,128)S(1)}, f32[8,128]{1,0:T(8,128)S(1)}, u32[]{:S(2)}, u32[]{:S(2)}) %collective-permute-start.6) | collective-permute-done | bytes 4128 | tf_op jit(solution)/shard_map/ppermute | solution.py:626
  57.4 0.5 slice.27
  (10 shorter events, 0.0 us)
Async XLA Ops:
  0.6 0.9 %copy-start = (f32[4,3,3072]{2,0,1:T(4,128)S(1)}, f32[4,3,3072]{2,0,1:T(4,128)}, u32[]{:S(2)}) copy-start(f32[4,3,3072]{2,0,1:T(4,128)} %param.5) | copy-start | bytes 442372
  1.5 0.8 %copy-start.2 = (f32[3,3072]{1,0:T(4,128)S(1)}, f32[3,3072]{1,0:T(4,128)}, u32[]{:S(2)}) copy-start(f32[3,3072]{1,0:T(4,128)} %true_ref.7) | copy-start | bytes 110596
  2.3 0.7 %copy-start.4 = (s32[3072]{0:T(1024)S(1)}, s32[3072]{0:T(1024)}, u32[]{:S(2)}) copy-start(s32[3072]{0:T(1024)} %param.7) | copy-start | bytes 36868
  3.0 6.3 %copy-start.1 = (f32[4,3,3072]{2,0,1:T(4,128)S(1)}, f32[4,3,3072]{2,0,1:T(4,128)}, u32[]{:S(2)}) copy-start(f32[4,3,3072]{2,0,1:T(4,128)} %param.5) | copy-start | bytes 442372
  3.0 6.3 %copy-start.3 = (f32[3,3072]{1,0:T(4,128)S(1)}, f32[3,3072]{1,0:T(4,128)}, u32[]{:S(2)}) copy-start(f32[3,3072]{1,0:T(4,128)} %true_ref.7) | copy-start | bytes 110596
  3.1 6.3 %copy-start.5 = (s32[3072]{0:T(1024)S(1)}, s32[3072]{0:T(1024)}, u32[]{:S(2)}) copy-start(s32[3072]{0:T(1024)} %param.7) | copy-start | bytes 36868
  3.1 30.2 %collective-permute-start = (f32[16,256]{1,0:T(8,128)S(1)}, f32[16,256]{1,0:T(8,128)S(1)}, u32[]{:S(2)}, u32[]{:S(2)}) collective-permute-start(f32[16,256]{1,0:T(8,128)S(1)} %get-tuple-element.14), channel_id=1, source_target_pairs={{0,4},{4,8},{8,12},{12,16},{16,20},{20,24},{24,28},{1,5},{5,9},{9,... | collective-permute-start | bytes 49160 | tf_op jit(solution)/shard_map/ppermute | solution.py:650
  8.1 25.2 %collective-permute-start.1 = (f32[16,256]{1,0:T(8,128)S(1)}, f32[16,256]{1,0:T(8,128)S(1)}, u32[]{:S(2)}, u32[]{:S(2)}) collective-permute-start(f32[16,256]{1,0:T(8,128)S(1)} %get-tuple-element.15), channel_id=1, source_target_pairs={{4,0},{8,4},{12,8},{16,12},{20,16},{24,20},{28,24},{5,1},{9,5},{13... | collective-permute-start | bytes 49160 | tf_op jit(solution)/shard_map/ppermute | solution.py:651
  9.4 0.7 %copy-start.6 = (s32[24,5]{0,1:T(8,128)S(1)}, s32[24,5]{0,1:T(8,128)}, u32[]{:S(2)}) copy-start(s32[24,5]{0,1:T(8,128)} %param.8) | copy-start | bytes 1444
  9.4 0.7 %copy-start.7 = (f32[4]{0:T(128)S(1)}, f32[4]{0:T(128)}, u32[]{:S(2)}) copy-start(f32[4]{0:T(128)} %noise_ref.1) | copy-start | bytes 52
  34.1 3.7 %collective-permute-start.2 = (f32[2,8,128]{2,1,0:T(8,128)S(1)}, f32[2,8,128]{2,1,0:T(8,128)S(1)}, u32[]{:S(2)}, u32[]{:S(2)}) collective-permute-start(f32[2,8,128]{2,1,0:T(8,128)S(1)} %get-tuple-element.17), channel_id=1, source_target_pairs={{0,4},{4,0},{8,12},{12,8},{16,20},{20,16},{24,28},{28,24},{1,5},{5... | collective-permute-start | bytes 24584 | tf_op jit(solution)/shard_map/ppermute | solution.py:626
  37.8 8.8 %collective-permute-start.3 = (f32[2,8,128]{2,1,0:T(8,128)S(1)}, f32[2,8,128]{2,1,0:T(8,128)S(1)}, u32[]{:S(2)}, u32[]{:S(2)}) collective-permute-start(f32[2,8,128]{2,1,0:T(8,128)S(1)} %pad_maximum_fusion), channel_id=1, source_target_pairs={{0,8},{4,12},{8,0},{12,4},{16,24},{20,28},{24,16},{28,20},{1,9},{5... | collective-permute-start | bytes 24584 | tf_op jit(solution)/shard_map/ppermute | solution.py:626
  46.6 4.6 %collective-permute-start.4 = (f32[2,8,128]{2,1,0:T(8,128)S(1)}, f32[2,8,128]{2,1,0:T(8,128)S(1)}, u32[]{:S(2)}, u32[]{:S(2)}) collective-permute-start(f32[2,8,128]{2,1,0:T(8,128)S(1)} %pad_maximum_fusion.1.stat_ref), channel_id=1, source_target_pairs={{0,16},{4,20},{8,24},{12,28},{16,0},{20,4},{24,8},{28,12},{1,17},{... | collective-permute-start | bytes 24584 | tf_op jit(solution)/shard_map/ppermute | solution.py:626
  52.5 1.2 %collective-permute-start.5 = (f32[8,128]{1,0:T(8,128)S(1)}, f32[8,128]{1,0:T(8,128)S(1)}, u32[]{:S(2)}, u32[]{:S(2)}) collective-permute-start(f32[8,128]{1,0:T(8,128)S(1)} %get-tuple-element.20), channel_id=1, source_target_pairs={{0,1},{1,0},{2,3},{3,2},{4,5},{5,4},{6,7},{7,6},{8,9},{9,8},{10,11... | collective-permute-start | bytes 12296 | tf_op jit(solution)/shard_map/ppermute | solution.py:626
  53.8 3.6 %collective-permute-start.6 = (f32[8,128]{1,0:T(8,128)S(1)}, f32[8,128]{1,0:T(8,128)S(1)}, u32[]{:S(2)}, u32[]{:S(2)}) collective-permute-start(f32[8,128]{1,0:T(8,128)S(1)} %add.53), channel_id=1, source_target_pairs={{0,2},{1,3},{2,0},{3,1},{4,6},{5,7},{6,4},{7,5},{8,10},{9,11},{10,... | collective-permute-start | bytes 12296 | tf_op jit(solution)/shard_map/ppermute | solution.py:626

commit v5 on v4

--- a/solution.py
+++ b/solution.py
@@ -371,7 +371,7 @@
             step()
 
 
-def interior_kernel(base_ref, part_ref, noise_ref, pred_ref, true_ref, kind_ref, pull_ref, stat_ref, noise_rows_ref, x_ref, mom_ref, self_refs, *scratch, copies, tiles):
+def interior_kernel(base_ref, part_ref, pred_ref, true_ref, kind_ref, pull_ref, stat_ref, x_ref, mom_ref, self_refs, *scratch, copies, tiles):
     e = Engine(copies, scratch)
     own = e.for_self(self_refs)
     base = base_ref[0]
@@ -450,11 +450,6 @@
 
     stat_ref[0] = moments[0] + e.scores(mom_ref[0, 5, 0:1, :])
     stat_ref[1] = moments[1]
-    row = lax.broadcasted_iota(jnp.int32, (copies, LANES), 0)
-    noise = jnp.zeros((copies, LANES), F32)
-    for s in range(copies):
-        noise = jnp.where(row == s, noise_ref[s], noise)
-    noise_rows_ref[...] = noise
 
 
 def edge_kernel(base_ref, part_ref, pred_ref, true_ref, kind_ref, low_ref, high_ref, stat_ref, pull_ref, out_ref, x_ref, *scratch, copies, tiles):
@@ -606,14 +601,29 @@
             grad_ref[c, :, start:start + LANES] -= m_ref[13] * edge_ref[c, :, t * LANES:(t + 1) * LANES]
 
 
-def pack_kernel(pred_ref, true_ref, kind_ref, first_ref, last_ref, *, copies, tiles):
+def pack_kernel(pred_hbm, true_hbm, kind_hbm, part_hbm, noise_hbm, first_ref, last_ref, pred_ref, true_ref, kind_ref, part_ref, noise_ref, noise_smem, sems, *, copies, tiles):
     span = BAND * LANES
+    moves = [
+        pltpu.make_async_copy(source, target, sems.at[i])
+        for i, (source, target) in enumerate(
+            ((pred_hbm, pred_ref), (true_hbm, true_ref), (kind_hbm, kind_ref), (part_hbm, part_ref), (noise_hbm, noise_smem))
+        )
+    ]
+    for move in moves:
+        move.start()
+    for move in moves:
+        move.wait()
     for ref, start in ((first_ref, 0), (last_ref, tiles * LANES - span)):
         sl = slice(start, start + span)
         for c in range(3):
             ref[c * copies:(c + 1) * copies, :] = pred_ref[c, :, sl] * 0.5
         ref[3 * copies:3 * copies + 3, :] = true_ref[:, sl] * 0.5
         ref[3 * copies + 3:3 * copies + 4, :] = jnp.where(kind_ref[:, sl] == 1, 15.0, 7.5)
+    row = lax.broadcasted_iota(jnp.int32, (copies, LANES), 0)
+    noise = jnp.zeros((copies, LANES), F32)
+    for s in range(copies):
+        noise = jnp.where(row == s, noise_smem[s], noise)
+    noise_ref[...] = noise
 
 
 VMEM = pl.BlockSpec(memory_space=pltpu.VMEM)
@@ -638,28 +648,30 @@
     stats_shape = jax.ShapeDtypeStruct((2, 8, LANES), F32)
 
     block = jax.ShapeDtypeStruct((rows + 4, BAND * LANES), F32)
-    first, last = pl.pallas_call(
+    same = [jax.ShapeDtypeStruct(x.shape, x.dtype) for x in (coords_pred, coords_true, kind, partners)]
+    first, last, coords_pred, coords_true, kind, partners, noise = pl.pallas_call(
         functools.partial(pack_kernel, copies=copies, tiles=tiles),
-        in_specs=[VMEM] * 3,
-        out_specs=[VMEM, VMEM],
-        out_shape=[block, block],
+        in_specs=[pl.BlockSpec(memory_space=pltpu.HBM)] * 5,
+        out_specs=[VMEM] * 7,
+        out_shape=[block, block, *same, jax.ShapeDtypeStruct((copies, LANES), F32)],
+        scratch_shapes=[pltpu.SMEM((copies,), F32), pltpu.SemaphoreType.DMA((5,))],
         compiler_params=SMALL,
         name="pack",
-    )(coords_pred, coords_true, kind)
+    )(*(pltpu.with_memory_space_constraint(x, pltpu.HBM) for x in (coords_pred, coords_true, kind, partners, noise_level)))
     forward = [(i, i + 1) for i in range(size - 1)]
     low = lax.ppermute(last, "res", forward)
     high = lax.ppermute(first, "res", [(b, a) for a, b in forward])
 
-    pull, stats, noise = pl.pallas_call(
+    pull, stats = pl.pallas_call(
         functools.partial(interior_kernel, copies=copies, tiles=tiles),
-        in_specs=[SMEM, SMEM, SMEM] + [VMEM] * 3,
-        out_specs=[VMEM, VMEM, VMEM],
-        out_shape=[jax.ShapeDtypeStruct((3, copies, local), F32), stats_shape, jax.ShapeDtypeStruct((copies, LANES), F32)],
+        in_specs=[SMEM, SMEM] + [VMEM] * 3,
+        out_specs=[VMEM, VMEM],
+        out_shape=[jax.ShapeDtypeStruct((3, copies, local), F32), stats_shape],
         scratch_shapes=[pltpu.VMEM((6, 16, LANES), F32), pltpu.VMEM((2, 6, 16, LANES), F32), Engine.self_scratch(copies)] + Engine.scratch(tiles, copies, BAND * tiles),
         compiler_params=PARAMS,
         cost_estimate=pl.CostEstimate(flops=10**8, bytes_accessed=10**6, transcendentals=10**7),
         name="interior",
-    )(base, partners, noise_level, coords_pred, coords_true, kind)
+    )(base, partners, coords_pred, coords_true, kind)
     edge_pull, stats = pl.pallas_call(
         functools.partial(edge_kernel, copies=copies, tiles=tiles),
         in_specs=[SMEM, SMEM] + [VMEM] * 6,

time: 59.6 us -> 57.7 us (0.968)
  local copies, waits for them, and re-layouts: 3.58 us -> 0.51 us
  Pallas kernels: 26.1 us -> 28.5 us
  starting transfers between devices: 18.3 us -> 17.1 us
    unnamed x16 -> x0, local copies, waits for them, and re-layouts: 3.07 us -> none
    pallas_call x1, Pallas kernels: 0.84 us -> 2.63 us  [shards(): pl.pallas_call(functools.partial(edge_kernel, copies=copies, tiles=tiles)...]
    ppermute x5, starting transfers between devices: 12 us -> 11 us  [swap(): lax.ppermute(x, axis, [(i, i ^ step) for i in range(lax.axis_size(axis))])]
    pallas_call x1, Pallas kernels: 0.01 us -> 0.98 us  [shards(): pl.pallas_call(functools.partial(pack_kernel, copies=copies, tiles=tiles)...]
  transfers between devices with their start and end apart: 7 -> 7, of which waited for: 5 -> 5; matrix products, arithmetic and copies ran while one was open for 0% -> 0% of each run, Pallas kernels for 40% -> 41%
where the time goes in v5:
time: 57.7 us; the launch traced here: 57.9 us
  Pallas kernels  28.5 us (49%)
  starting transfers between devices  17.1 us (30%)
  waiting for transfers between devices  9.24 us (16%)
  between operations  2.46 us (4%)
    pallas_call x1, Pallas kernels, shards(): pl.pallas_call(functools.partial(interior_kernel, copies=copies, tiles=ti...  22.8 us
    ppermute x5, starting transfers between devices, swap(): lax.ppermute(x, axis, [(i, i ^ step) for i in range(lax.axis_size(axis))])  11 us
    ppermute x5, waiting for transfers between devices, swap(): lax.ppermute(x, axis, [(i, i ^ step) for i in range(lax.axis_size(axis))])  9.24 us
    ppermute x1, starting transfers between devices, shards(): low = lax.ppermute(last, 'res', forward)  4.84 us
    pallas_call x1, Pallas kernels, shards(): pl.pallas_call(functools.partial(edge_kernel, copies=copies, tiles=tiles)...  2.63 us
    pallas_call x1, Pallas kernels, shards(): pl.pallas_call(functools.partial(solve_kernel, copies=copies, atoms=local...  1.29 us
    ppermute x1, starting transfers between devices, shards(): high = lax.ppermute(first, 'res', [(b, a) for a, b in forward])  1.29 us
  transfers between devices with their start and end apart: 7, of which 5 were waited for; matrix products, arithmetic and copies ran while one was open for 0% of the time, Pallas kernels for 41%

profile of v5, /device:TPU:0, one launch (start us, length us, event | category | flops | bytes accessed | tf_op | source)
XLA Modules:
  0.0 57.9 jit_solution(2061024729292912761)
XLA Ops:
  0.6 1.0 %pack.1 = (f32[16,256]{1,0:T(8,128)S(1)}, f32[16,256]{1,0:T(8,128)S(1)}, f32[3,4,3072]{2,1,0:T(4,128)S(1)}, f32[3,3072]{1,0:T(4,128)S(1)}, s32[1,3072]{1,0:T(1,1...) custom-call(f32[3,4,3072]{2,1,0:T(4,128)} %bitcast.6, f32[3,3072]{1,0:T(4,128)} %true_hbm.1, s32[1,3072]{1,0:T(1,128)} %bitcast.8, ...), custom_call_target="tpu_custom_call" | custom-call | tf_op jit(solution)/shard_map/pack/pallas_call | solution.py:652
  1.6 4.8 %collective-permute-start = (f32[16,256]{1,0:T(8,128)S(1)}, f32[16,256]{1,0:T(8,128)S(1)}, u32[]{:S(2)}, u32[]{:S(2)}) collective-permute-start(f32[16,256]{1,0:T(8,128)S(1)} %get-tuple-element.22), channel_id=1, source_target_pairs={{0,4},{4,8},{8,12},{12,16},{16,20},{20,24},{24,28},{1,5},{5,9},{9,... | collective-permute-start | bytes 49160 | tf_op jit(solution)/shard_map/ppermute | solution.py:662
  6.5 1.3 %collective-permute-start.1 = (f32[16,256]{1,0:T(8,128)S(1)}, f32[16,256]{1,0:T(8,128)S(1)}, u32[]{:S(2)}, u32[]{:S(2)}) collective-permute-start(f32[16,256]{1,0:T(8,128)S(1)} %get-tuple-element.23), channel_id=1, source_target_pairs={{4,0},{8,4},{12,8},{16,12},{20,16},{24,20},{28,24},{5,1},{9,5},{13... | collective-permute-start | bytes 49160 | tf_op jit(solution)/shard_map/ppermute | solution.py:663
  7.8 22.8 %interior.1 = (f32[3,4,3072]{2,1,0:T(4,128)S(1)}, f32[2,8,128]{2,1,0:T(8,128)S(1)}) custom-call(s32[1]{0:T(128)} %bitcast.base_ref, s32[5,24]{1,0:T(8,128)S(1)} %get-tuple-element.18.part_ref, f32[3,4,3072]{2,1,0:T(4,128)S(1)} %get-tuple-element.19.pred_ref, f32[3,3072]{1,0:T(4,128)S(1)} %get-tuple-element.20.true_ref, s32[1,3072]{1,0:T(1,128)S(1)} %get-tuple-element.21.kind_ref), custom_call_target="tpu_custom_call" | custom-call | flops 100000000 | bytes 1000000 | tf_op jit(solution)/shard_map/interior/pallas_call | solution.py:665
  30.6 0.0 collective-permute-done.low_ref
  30.6 0.0 collective-permute-done.1.high_ref
  30.6 2.6 %edges.1 = (f32[3,4,512]{2,1,0:T(4,128)S(1)}, f32[2,8,128]{2,1,0:T(8,128)S(1)}) custom-call(s32[1]{0:T(128)} %bitcast.base_ref, s32[5,24]{1,0:T(8,128)S(1)} %get-tuple-element.18.part_ref, f32[3,4,3072]{2,1,0:T(4,128)S(1)} %get-tuple-element.19.pred_ref, f32[3,3072]{1,0:T(4,128)S(1)} %get-tuple-element.20.true_ref, ...), custom_call_target="tpu_custom_call" | custom-call | tf_op jit(solution)/shard_map/edges/pallas_call | solution.py:675
  33.2 5.1 %collective-permute-start.2 = (f32[2,8,128]{2,1,0:T(8,128)S(1)}, f32[2,8,128]{2,1,0:T(8,128)S(1)}, u32[]{:S(2)}, u32[]{:S(2)}) collective-permute-start(f32[2,8,128]{2,1,0:T(8,128)S(1)} %get-tuple-element.25), channel_id=1, source_target_pairs={{0,4},{4,0},{8,12},{12,8},{16,20},{20,16},{24,28},{28,24},{1,5},{5... | collective-permute-start | bytes 24584 | tf_op jit(solution)/shard_map/ppermute | solution.py:636
  38.3 1.6 %collective-permute-done.2 = f32[2,8,128]{2,1,0:T(8,128)S(1)} collective-permute-done((f32[2,8,128]{2,1,0:T(8,128)S(1)}, f32[2,8,128]{2,1,0:T(8,128)S(1)}, u32[]{:S(2)}, u32[]{:S(2)}) %collective-permute-start.2) | collective-permute-done | bytes 8224 | tf_op jit(solution)/shard_map/ppermute | solution.py:636
  39.9 0.2 collective-permute-start.3
  40.1 3.6 %collective-permute-done.3 = f32[2,8,128]{2,1,0:T(8,128)S(1)} collective-permute-done((f32[2,8,128]{2,1,0:T(8,128)S(1)}, f32[2,8,128]{2,1,0:T(8,128)S(1)}, u32[]{:S(2)}, u32[]{:S(2)}) %collective-permute-start.3) | collective-permute-done | bytes 8224 | tf_op jit(solution)/shard_map/ppermute | solution.py:636
  43.7 4.2 %collective-permute-start.4 = (f32[2,8,128]{2,1,0:T(8,128)S(1)}, f32[2,8,128]{2,1,0:T(8,128)S(1)}, u32[]{:S(2)}, u32[]{:S(2)}) collective-permute-start(f32[2,8,128]{2,1,0:T(8,128)S(1)} %pad_maximum_fusion.1.stat_ref), channel_id=1, source_target_pairs={{0,16},{4,20},{8,24},{12,28},{16,0},{20,4},{24,8},{28,12},{1,17},{... | collective-permute-start | bytes 24584 | tf_op jit(solution)/shard_map/ppermute | solution.py:636
  47.8 1.6 %collective-permute-done.4.other_ref = f32[2,8,128]{2,1,0:T(8,128)S(1)} collective-permute-done((f32[2,8,128]{2,1,0:T(8,128)S(1)}, f32[2,8,128]{2,1,0:T(8,128)S(1)}, u32[]{:S(2)}, u32[]{:S(2)}) %collective-permute-start.4) | collective-permute-done | bytes 8224 | tf_op jit(solution)/shard_map/ppermute | solution.py:636
  49.5 1.3 %solve.1 = (f32[4]{0:T(128)}, f32[8,128]{1,0:T(8,128)S(1)}, f32[14,4,128]{2,1,0:T(4,128)S(1)}, f32[8,128]{1,0:T(8,128)S(1)}) custom-call(f32[2,8,128]{2,1,0:T(8,128)S(1)} %pad_maximum_fusion.1.stat_ref, f32[2,8,128]{2,1,0:T(8,128)S(1)} %collective-permute-done.4.other_ref, f32[4,128]{1,0:T(4,128)S(1)} %get-tuple-element.26.noise_ref), custom_call_target="tpu_custom_call" | custom-call | tf_op jit(solution)/shard_map/solve/pallas_call | solution.py:694
  50.8 0.1 collective-permute-start.5
  50.8 1.2 %collective-permute-done.5 = f32[8,128]{1,0:T(8,128)S(1)} collective-permute-done((f32[8,128]{1,0:T(8,128)S(1)}, f32[8,128]{1,0:T(8,128)S(1)}, u32[]{:S(2)}, u32[]{:S(2)}) %collective-permute-start.5) | collective-permute-done | bytes 4128 | tf_op jit(solution)/shard_map/ppermute | solution.py:636
  52.0 1.5 %collective-permute-start.6 = (f32[8,128]{1,0:T(8,128)S(1)}, f32[8,128]{1,0:T(8,128)S(1)}, u32[]{:S(2)}, u32[]{:S(2)}) collective-permute-start(f32[8,128]{1,0:T(8,128)S(1)} %add.53), channel_id=1, source_target_pairs={{0,2},{1,3},{2,0},{3,1},{4,6},{5,7},{6,4},{7,5},{8,10},{9,11},{10,... | collective-permute-start | bytes 12296 | tf_op jit(solution)/shard_map/ppermute | solution.py:636
  53.5 0.8 %gradient.1 = f32[3,4,3072]{2,1,0:T(4,128)} custom-call(f32[14,4,128]{2,1,0:T(4,128)S(1)} %get-tuple-element.29.m_ref, f32[8,128]{1,0:T(8,128)S(1)} %get-tuple-element.30.k_ref, f32[3,4,3072]{2,1,0:T(4,128)S(1)} %get-tuple-element.19.pred_ref, f32[3,3072]{1,0:T(4,128)S(1)} %get-tuple-element.20.true_ref, s32[1,3072]{1,0:T(1,128)S(1)} %get-tuple-element.21.kind_ref, ...), custom_call_target="tpu_custom_call" | custom-call | flops 1000000 | bytes 1000000 | tf_op jit(solution)/shard_map/gradient/pallas_call | solution.py:713
  54.3 1.3 %collective-permute-done.6 = f32[8,128]{1,0:T(8,128)S(1)} collective-permute-done((f32[8,128]{1,0:T(8,128)S(1)}, f32[8,128]{1,0:T(8,128)S(1)}, u32[]{:S(2)}, u32[]{:S(2)}) %collective-permute-start.6) | collective-permute-done | bytes 4128 | tf_op jit(solution)/shard_map/ppermute | solution.py:636
  55.6 0.5 slice.27
  (6 shorter events, 0.0 us)
Async XLA Ops:
  1.6 29.0 %collective-permute-start = (f32[16,256]{1,0:T(8,128)S(1)}, f32[16,256]{1,0:T(8,128)S(1)}, u32[]{:S(2)}, u32[]{:S(2)}) collective-permute-start(f32[16,256]{1,0:T(8,128)S(1)} %get-tuple-element.22), channel_id=1, source_target_pairs={{0,4},{4,8},{8,12},{12,16},{16,20},{20,24},{24,28},{1,5},{5,9},{9,... | collective-permute-start | bytes 49160 | tf_op jit(solution)/shard_map/ppermute | solution.py:662
  6.5 24.1 %collective-permute-start.1 = (f32[16,256]{1,0:T(8,128)S(1)}, f32[16,256]{1,0:T(8,128)S(1)}, u32[]{:S(2)}, u32[]{:S(2)}) collective-permute-start(f32[16,256]{1,0:T(8,128)S(1)} %get-tuple-element.23), channel_id=1, source_target_pairs={{4,0},{8,4},{12,8},{16,12},{20,16},{24,20},{28,24},{5,1},{9,5},{13... | collective-permute-start | bytes 49160 | tf_op jit(solution)/shard_map/ppermute | solution.py:663
  33.2 6.7 %collective-permute-start.2 = (f32[2,8,128]{2,1,0:T(8,128)S(1)}, f32[2,8,128]{2,1,0:T(8,128)S(1)}, u32[]{:S(2)}, u32[]{:S(2)}) collective-permute-start(f32[2,8,128]{2,1,0:T(8,128)S(1)} %get-tuple-element.25), channel_id=1, source_target_pairs={{0,4},{4,0},{8,12},{12,8},{16,20},{20,16},{24,28},{28,24},{1,5},{5... | collective-permute-start | bytes 24584 | tf_op jit(solution)/shard_map/ppermute | solution.py:636
  39.9 3.7 %collective-permute-start.3 = (f32[2,8,128]{2,1,0:T(8,128)S(1)}, f32[2,8,128]{2,1,0:T(8,128)S(1)}, u32[]{:S(2)}, u32[]{:S(2)}) collective-permute-start(f32[2,8,128]{2,1,0:T(8,128)S(1)} %pad_maximum_fusion), channel_id=1, source_target_pairs={{0,8},{4,12},{8,0},{12,4},{16,24},{20,28},{24,16},{28,20},{1,9},{5... | collective-permute-start | bytes 24584 | tf_op jit(solution)/shard_map/ppermute | solution.py:636
  43.7 5.8 %collective-permute-start.4 = (f32[2,8,128]{2,1,0:T(8,128)S(1)}, f32[2,8,128]{2,1,0:T(8,128)S(1)}, u32[]{:S(2)}, u32[]{:S(2)}) collective-permute-start(f32[2,8,128]{2,1,0:T(8,128)S(1)} %pad_maximum_fusion.1.stat_ref), channel_id=1, source_target_pairs={{0,16},{4,20},{8,24},{12,28},{16,0},{20,4},{24,8},{28,12},{1,17},{... | collective-permute-start | bytes 24584 | tf_op jit(solution)/shard_map/ppermute | solution.py:636
  50.8 1.2 %collective-permute-start.5 = (f32[8,128]{1,0:T(8,128)S(1)}, f32[8,128]{1,0:T(8,128)S(1)}, u32[]{:S(2)}, u32[]{:S(2)}) collective-permute-start(f32[8,128]{1,0:T(8,128)S(1)} %get-tuple-element.28), channel_id=1, source_target_pairs={{0,1},{1,0},{2,3},{3,2},{4,5},{5,4},{6,7},{7,6},{8,9},{9,8},{10,11... | collective-permute-start | bytes 12296 | tf_op jit(solution)/shard_map/ppermute | solution.py:636
  52.0 3.6 %collective-permute-start.6 = (f32[8,128]{1,0:T(8,128)S(1)}, f32[8,128]{1,0:T(8,128)S(1)}, u32[]{:S(2)}, u32[]{:S(2)}) collective-permute-start(f32[8,128]{1,0:T(8,128)S(1)} %add.53), channel_id=1, source_target_pairs={{0,2},{1,3},{2,0},{3,1},{4,6},{5,7},{6,4},{7,5},{8,10},{9,11},{10,... | collective-permute-start | bytes 12296 | tf_op jit(solution)/shard_map/ppermute | solution.py:636

commit v6 on v5

--- a/solution.py
+++ b/solution.py
@@ -100,59 +100,41 @@
 
 
 class Engine:
-    names = ("v", "cut", "centre", "left", "point", "right", "true", "weight", "minus", "d", "f", "acc", "score", "count", "tri", "items")
-
-    def __init__(self, copies, refs):
+    shared = ("v", "cut", "centre", "left", "point", "acc", "score", "count")
+    work = ("true", "weight", "minus", "right", "d", "f")
+
+    def __init__(self, copies, tiles, shared, work):
         self.copies = copies
         self.twos = copies // 2
-        for name, ref in zip(self.names, refs):
+        self.low, self.high, self.dummy = tiles, tiles + BAND, tiles + 2 * BAND
+        for name, ref in zip(self.shared + self.work, (*shared, *work)):
             setattr(self, name, ref)
 
     @staticmethod
-    def scratch(tiles, copies, items):
-        n, twos = tiles + 1, copies // 2
+    def shared_shapes(tiles, copies):
+        n, twos = tiles + 2 * BAND + 1, copies // 2
         return [
-            pltpu.VMEM((n, copies + 1, 8, LANES), F32),
-            pltpu.VMEM((n, 1, LANES), F32),
-            pltpu.VMEM((n, copies + 1, 8, LANES), F32),
-            pltpu.VMEM((n, twos + 1, LANES, LANES), BF16),
-            pltpu.VMEM((n, twos, 64, 2 * LANES), BF16),
-            [pltpu.VMEM((1, twos + 1, LANES, 2 * LANES), BF16)] * 2,
-            [pltpu.VMEM((LANES, LANES), F32)] * 2,
-            [pltpu.VMEM((LANES, LANES), F32)] * 2,
-            [pltpu.VMEM((LANES, LANES), F32)] * 2,
-            [pltpu.VMEM((1, twos + 1, LANES, 2 * LANES), F32)] * 2,
-            [pltpu.VMEM((1, twos, 2 * LANES, 2 * LANES), BF16)] * 2,
-            pltpu.VMEM((n, copies, 8, LANES), F32),
-            pltpu.VMEM((copies, 8, LANES), F32),
-            pltpu.VMEM((8, LANES), F32),
-            pltpu.VMEM((2, LANES, LANES), BF16),
-            pltpu.SMEM((4, items + 2), jnp.int32),
+            jax.ShapeDtypeStruct(shape, dtype)
+            for shape, dtype in (
+                ((n, copies + 1, 8, LANES), F32),
+                ((n, 1, LANES), F32),
+                ((n, copies + 1, 8, LANES), F32),
+                ((n, twos + 1, LANES, LANES), BF16),
+                ((n, twos, 64, 2 * LANES), BF16),
+                ((n, copies * 8, LANES), F32),
+                ((copies, 8, LANES), F32),
+                ((8, LANES), F32),
+            )
         ]
 
     @staticmethod
-    def self_scratch(copies):
+    def work_shapes(copies, parts):
         twos = copies // 2
-        return [
-            [pltpu.VMEM((2, twos + 1, LANES, 2 * LANES), BF16)] * 2,
-            [pltpu.VMEM((2, twos + 1, LANES, 2 * LANES), F32)] * 2,
-            [pltpu.VMEM((2, twos, 2 * LANES, 2 * LANES), BF16)] * 2,
+        return [[pltpu.VMEM((LANES, LANES), F32)] * 2] * 3 + [
+            [pltpu.VMEM((parts, twos + 1, LANES, 2 * LANES), BF16)] * 2,
+            [pltpu.VMEM((parts, twos + 1, LANES, 2 * LANES), F32)] * 2,
+            [pltpu.VMEM((parts, twos, 2 * LANES, 2 * LANES), BF16)] * 2,
         ]
-
-    def for_self(self, refs):
-        other = Engine(self.copies, [])
-        other.__dict__.update(self.__dict__)
-        other.right, other.d, other.f = refs
-        return other
-
-    def begin(self, tiles):
-        for ref in [self.acc, self.score, self.count, *self.f, self.v.at[tiles], self.cut.at[tiles], self.centre.at[tiles], self.left.at[tiles], self.point.at[tiles]]:
-            ref[...] = jnp.zeros_like(ref)
-        row = lax.broadcasted_iota(jnp.int32, (LANES, LANES), 0)
-        lane = lax.broadcasted_iota(jnp.int32, (LANES, LANES), 1)
-        self.tri[0] = jnp.where(lane > row, 1.0, 0.0).astype(BF16)
-        self.tri[1] = jnp.where(lane < row, 1.0, 0.0).astype(BF16)
-        self.begin_right()
 
     def begin_right(self):
         pick = jnp.where(lax.broadcasted_iota(jnp.int32, (LANES, LANES), 0) == 7, 1.0, 0.0).astype(BF16)
@@ -160,6 +142,8 @@
             ref[...] = jnp.zeros_like(ref)
             for k in range(ref.shape[0]):
                 ref[k, self.twos, :, LANES:] = pick
+        for ref in self.f:
+            ref[0] = jnp.zeros(ref.shape[1:], BF16)
 
     def place(self, t, ref):
         blank = jnp.zeros((5, LANES), F32)
@@ -287,7 +271,7 @@
 
     def add(self, t, h, parts):
         for q in range(2):
-            self.acc[t, 2 * h + q] += parts[q]
+            self.acc[t, 8 * (2 * h + q):8 * (2 * h + q) + 8, :] += parts[q]
 
     def cross_collect(self, item, slot):
         steps = []
@@ -342,9 +326,26 @@
             for slot in range(2):
                 self.half(kind, [at(p + slot - 1), at(p + slot), at(p + slot + 1), at(p + slot + 3)], slot)
 
-    def pull(self, t, s):
-        a = self.acc[t, s]
-        return (self.v[t, s] * a[3:4] - a)[0:3]
+    def end_list(self, kind, item, n, dummy):
+        def last(i, slot):
+            return getattr(self, kind + "_collect")(item(i), slot)
+
+        def odd():
+            before = tuple(jnp.where(n > 1, z, dummy) for z in item(jnp.maximum(n - 2, 0)))
+            steps = getattr(self, kind + "_collect")(before, 1)
+            spread(steps, lambda tick: getattr(self, kind + "_factor")(item(n - 1), 0, tick), 16 + 8 * self.copies)
+            for step in last(n - 1, 0):
+                step()
+
+        def even():
+            for step in last(n - 1, 1):
+                step()
+
+        if isinstance(n, int):
+            (odd if n % 2 else even)()
+        else:
+            pl.when(n % 2 == 1)(odd)
+            pl.when(n % 2 == 0)(even)
 
     def scores(self, weight_total):
         rows = [jnp.sum(self.score[s], axis=0, keepdims=True) for s in range(self.copies)]
@@ -355,31 +356,25 @@
         return jnp.broadcast_to(jnp.sum(total, axis=1, keepdims=True), (8, LANES))
 
 
-def finish_list(e, item, n, dummy, also=()):
-    also = list(also)
-
-    @pl.when(n % 2 == 1)
-    def _():
-        before = tuple(jnp.where(n > 1, z, dummy) for z in item(jnp.maximum(n - 2, 0)))
-        spread(also + e.cross_collect(before, 1), lambda tick: e.cross_factor(item(n - 1), 0, tick), 16 + 8 * e.copies)
-        for step in e.cross_collect(item(n - 1), 0):
-            step()
-
-    @pl.when(n % 2 == 0)
-    def _():
-        for step in also + e.cross_collect(item(n - 1), 1):
-            step()
-
-
-def interior_kernel(base_ref, part_ref, pred_ref, true_ref, kind_ref, pull_ref, stat_ref, x_ref, mom_ref, self_refs, *scratch, copies, tiles):
-    e = Engine(copies, scratch)
-    own = e.for_self(self_refs)
+def self_kernel(base_ref, part_ref, pred_ref, true_ref, kind_ref, *refs, copies, tiles):
+    count = len(Engine.shared)
+    shared, (items, moment_ref), (x_ref, sum_ref, tri), work = refs[:count], refs[count:count + 2], refs[count + 2:count + 5], refs[count + 5:]
+    e = Engine(copies, tiles, shared, work)
+    e.tri = tri
     base = base_ref[0]
     rows = 3 * copies
-    e.begin(tiles)
-    own.begin_right()
-    x_ref[...] = jnp.zeros_like(x_ref)
-    mom_ref[...] = jnp.zeros_like(mom_ref)
+    e.begin_right()
+    for ref in [e.acc, e.score, e.count, x_ref, sum_ref, *(r.at[e.dummy] for r in shared[:5])]:
+        ref[...] = jnp.zeros_like(ref)
+    row = lax.broadcasted_iota(jnp.int32, (LANES, LANES), 0)
+    lane = lax.broadcasted_iota(jnp.int32, (LANES, LANES), 1)
+    tri[0] = jnp.where(lane > row, 1.0, 0.0).astype(BF16)
+    tri[1] = jnp.where(lane < row, 1.0, 0.0).astype(BF16)
+
+    def append(n, owner, other, g, j, share):
+        for k, z in enumerate((g, j, share)):
+            items[k, n] = jnp.int32(z)
+        return n + jnp.where(listed(part_ref, owner, base + other), 1, 0)
 
     unroll = next(u for u in (6, 4, 3, 2, 1) if tiles % u == 0)
 
@@ -387,10 +382,8 @@
         for q in range(unroll):
             t = m * unroll + q
             for o in range(1, BAND + 1):
-                e.items[0, n] = t - o
-                e.items[1, n] = t
-                e.items[2, n] = 2
-                n = n + jnp.where(listed(part_ref, t, base + t - o) & (t >= o), 1, 0)
+                more = append(n, t, t - o, t - o, t, 2)
+                n = jnp.where(t >= o, more, n)
             sl = pl.ds(pl.multiple_of(t * LANES, LANES), LANES)
             kind = kind_ref[:, sl]
             weight = jnp.where(kind == 1, 5.0, jnp.where(kind == 2, 10.0, 1.0))
@@ -403,103 +396,66 @@
             wx = x * weight
             terms = [wx * x[rows + c:rows + c + 1] for c in range(3)] + [wx, wx * x]
             for i, term in enumerate(terms):
-                total, error = two_sum(mom_ref[0, i], term)
-                mom_ref[0, i] = total
-                mom_ref[1, i] += error
-            mom_ref[0, 5, 0:1, :] += weight
+                total, error = two_sum(sum_ref[0, i], term)
+                sum_ref[0, i] = total
+                sum_ref[1, i] += error
+            sum_ref[0, 5, 0:1, :] += weight
             e.prep(t)
         return n
 
     n = lax.fori_loop(0, tiles // unroll, prepare, jnp.int32(0))
+    for o in range(1, BAND + 1):
+        for k in range(o):
+            n = append(n, k, k - o, e.low + BAND + k - o, k, 1)
+            n = append(n, tiles - 1 - k, tiles - 1 - k + o, tiles - 1 - k, e.high + o - 1 - k, 1)
+    for k, z in enumerate((e.dummy, e.dummy, 0)):
+        items[k, 0] = jnp.where(n == 0, z, items[k, 0])
+    items[3, 0] = jnp.maximum(n, 1)
 
     blank = jnp.zeros((LANES - 80, LANES), F32)
-    high, low = (jnp.concatenate([mom_ref[part, i] for i in range(5)] + [blank], axis=0).T for part in range(2))
+    high, low = (jnp.concatenate([sum_ref[part, i] for i in range(5)] + [blank], axis=0).T for part in range(2))
     sums = [(high[8 * k:8 * k + 8], low[8 * k:8 * k + 8]) for k in range(16)]
     while len(sums) > 1:
         sums = [pair_add(a, b) for a, b in zip(sums[::2], sums[1::2])]
     sums = sums[0]
     for k in (4, 2, 1):
         sums = pair_add(sums, (roll(sums[0], k, 0), roll(sums[1], k, 0)))
-    moments = [x * e.unit(0) for x in sums]
+    for part in range(2):
+        moment_ref[part] = sums[part] * e.unit(0)
+    moment_ref[2] = jnp.broadcast_to(sum_ref[0, 5, 0:1, :], (8, LANES))
 
     def twin(i):
         return 2 * i, 2 * i + 1
 
+    half = tiles // 2
+    e.begin_list("self", twin, half)
+    e.run_list("self", twin, half, e.dummy)
+    e.end_list("self", twin, half, e.dummy)
+
+
+def cross_kernel(items, moment_ref, low_ref, high_ref, *refs, copies, tiles):
+    count = len(Engine.shared)
+    stat_ref, shared, x_ref, work = refs[count], refs[count + 1:2 * count + 1], refs[2 * count + 1], refs[2 * count + 2:]
+    e = Engine(copies, tiles, shared, work)
+    rows = 3 * copies
+    e.begin_right()
+
     def item(i):
-        return e.items[0, i], e.items[1, i], e.items[2, i]
-
-    for k, z in enumerate((tiles, tiles, 0)):
-        e.items[k, 0] = jnp.where(n == 0, z, e.items[k, 0])
-    n = jnp.maximum(n, 1)
-    half = tiles // 2
-    own.begin_list("self", twin, half)
+        return items[0, i], items[1, i], items[2, i]
+
+    n = items[3, 0]
+    for i, (ref, start) in enumerate(((low_ref, e.low), (high_ref, e.high))):
+        for q in range(BAND):
+            t = start + q
+            x_ref[BAND * i + q] = ref[:, q * LANES:(q + 1) * LANES]
+            e.place(t, x_ref.at[BAND * i + q])
+            e.cut[t] = x_ref[BAND * i + q, rows + 3:rows + 4, :]
+            e.prep(t)
     e.begin_list("cross", item, n)
-    own.run_list("self", twin, half, tiles)
-    e.run_list("cross", item, n, tiles)
-    finish_list(e, item, n, tiles, own.self_collect(twin(half - 1), 1))
-
-    @pl.loop(0, tiles // unroll)
-    def _(m):
-        for q in range(unroll):
-            t = m * unroll + q
-            sl = pl.ds(pl.multiple_of(t * LANES, LANES), LANES)
-            for s in range(copies):
-                pull = e.pull(t, s)
-                for c in range(3):
-                    pull_ref[c, s:s + 1, sl] = pull[c:c + 1]
-
-    stat_ref[0] = moments[0] + e.scores(mom_ref[0, 5, 0:1, :])
-    stat_ref[1] = moments[1]
-
-
-def edge_kernel(base_ref, part_ref, pred_ref, true_ref, kind_ref, low_ref, high_ref, stat_ref, pull_ref, out_ref, x_ref, *scratch, copies, tiles):
-    e = Engine(copies, scratch)
-    base = base_ref[0]
-    span = BAND * LANES
-    local = tiles * LANES
-    window = 4 * BAND
-    e.begin(window)
-    rows = 3 * copies
-    for q in range(BAND):
-        sl = slice(q * LANES, q * LANES + LANES)
-        for ref, t in ((low_ref, q), (high_ref, 3 * BAND + q)):
-            x_ref[t] = ref[:, sl]
-        for start, t in ((0, BAND + q), (local - span, 2 * BAND + q)):
-            sl = slice(start + q * LANES, start + q * LANES + LANES)
-            for c in range(3):
-                x_ref[t, c * copies:(c + 1) * copies, :] = pred_ref[c, :, sl] * 0.5
-            x_ref[t, rows:rows + 3, :] = true_ref[:, sl] * 0.5
-            x_ref[t, rows + 3:rows + 4, :] = jnp.where(kind_ref[:, sl] == 1, 15.0, 7.5)
-    for t in range(window):
-        e.place(t, x_ref.at[t])
-        e.cut[t] = x_ref[t, rows + 3:rows + 4, :]
-    n = jnp.int32(0)
-    for o in range(1, BAND + 1):
-        for k in range(o):
-            for owner, other, g, j in ((k, k - o, BAND + k - o, BAND + k), (tiles - 1 - k, tiles - 1 - k + o, 3 * BAND - 1 - k, 3 * BAND - 1 - k + o)):
-                e.items[0, n] = g
-                e.items[1, n] = j
-                e.items[2, n] = 1
-                n = n + jnp.where(listed(part_ref, owner, base + other), 1, 0)
-
-    def item(i):
-        return e.items[0, i], e.items[1, i], e.items[2, i]
-
-    @pl.when(n > 0)
-    def _():
-        for t in range(window):
-            e.prep(t)
-        e.begin_list("cross", item, n)
-        e.run_list("cross", item, n, window)
-        finish_list(e, item, n, window)
-
-    for t in range(2 * BAND):
-        for s in range(copies):
-            pull = e.pull(BAND + t, s)
-            for c in range(3):
-                pull_ref[c, s:s + 1, t * LANES:(t + 1) * LANES] = pull[c:c + 1]
-    out_ref[0] = stat_ref[0] + e.scores(jnp.zeros((1, LANES), F32))
-    out_ref[1] = stat_ref[1]
+    e.run_list("cross", item, n, e.dummy)
+    e.end_list("cross", item, n, e.dummy)
+    stat_ref[0] = moment_ref[0] + e.scores(moment_ref[2, 0:1, :])
+    stat_ref[1] = moment_ref[1]
 
 
 def solve_kernel(stat_ref, other_ref, noise_ref, loss_ref, sum_ref, m_ref, k_ref, s_ref, *, copies, atoms):
@@ -584,21 +540,18 @@
     m_ref[13] = grad_scale / count
 
 
-def gradient_kernel(m_ref, k_ref, pred_ref, true_ref, kind_ref, pull_ref, edge_ref, grad_ref, *, copies, tiles):
+def gradient_kernel(m_ref, k_ref, pred_ref, true_ref, kind_ref, acc_ref, grad_ref, *, copies, tiles):
     for t in range(tiles):
         sl = slice(t * LANES, (t + 1) * LANES)
         kind = kind_ref[:, sl]
         weight = jnp.where(kind == 1, 5.0, jnp.where(kind == 2, 10.0, 1.0))
         centred = true_ref[:, sl] - k_ref[0:3, :]
+        factor_sum = 0.5 * acc_ref[t, pl.ds(3, copies, stride=8), :]
         for c in range(3):
             target = m_ref[3 * c] * centred[0:1] + m_ref[3 * c + 1] * centred[1:2] + m_ref[3 * c + 2] * centred[2:3] + m_ref[9 + c]
-            deviation = pred_ref[c, :, sl] - target
-            grad_ref[c, :, sl] = m_ref[12] * weight * deviation - m_ref[13] * pull_ref[c, :, sl]
-
-    for t in range(2 * BAND):
-        start = t * LANES if t < BAND else (tiles - 2 * BAND + t) * LANES
-        for c in range(3):
-            grad_ref[c, :, start:start + LANES] -= m_ref[13] * edge_ref[c, :, t * LANES:(t + 1) * LANES]
+            pred = pred_ref[c, :, sl]
+            pull = pred * factor_sum - acc_ref[t, pl.ds(c, copies, stride=8), :]
+            grad_ref[c, :, sl] = m_ref[12] * weight * (pred - target) - m_ref[13] * pull
 
 
 def pack_kernel(pred_hbm, true_hbm, kind_hbm, part_hbm, noise_hbm, first_ref, last_ref, pred_ref, true_ref, kind_ref, part_ref, noise_ref, noise_smem, sems, *, copies, tiles):
@@ -662,25 +615,29 @@
     low = lax.ppermute(last, "res", forward)
     high = lax.ppermute(first, "res", [(b, a) for a, b in forward])
 
-    pull, stats = pl.pallas_call(
-        functools.partial(interior_kernel, copies=copies, tiles=tiles),
+    shared_shapes = Engine.shared_shapes(tiles, copies)
+    count = len(shared_shapes)
+    x_shape = pltpu.VMEM((6, 16, LANES), F32)
+    *shared, items, moments = pl.pallas_call(
+        functools.partial(self_kernel, copies=copies, tiles=tiles),
         in_specs=[SMEM, SMEM] + [VMEM] * 3,
-        out_specs=[VMEM, VMEM],
-        out_shape=[jax.ShapeDtypeStruct((3, copies, local), F32), stats_shape],
-        scratch_shapes=[pltpu.VMEM((6, 16, LANES), F32), pltpu.VMEM((2, 6, 16, LANES), F32), Engine.self_scratch(copies)] + Engine.scratch(tiles, copies, BAND * tiles),
+        out_specs=[VMEM] * count + [SMEM, VMEM],
+        out_shape=[*shared_shapes, jax.ShapeDtypeStruct((4, LANES), jnp.int32), jax.ShapeDtypeStruct((3, 8, LANES), F32)],
+        scratch_shapes=[x_shape, pltpu.VMEM((2, 6, 16, LANES), F32), pltpu.VMEM((2, LANES, LANES), BF16), *Engine.work_shapes(copies, 2)],
         compiler_params=PARAMS,
         cost_estimate=pl.CostEstimate(flops=10**8, bytes_accessed=10**6, transcendentals=10**7),
-        name="interior",
+        name="self_tiles",
     )(base, partners, coords_pred, coords_true, kind)
-    edge_pull, stats = pl.pallas_call(
-        functools.partial(edge_kernel, copies=copies, tiles=tiles),
-        in_specs=[SMEM, SMEM] + [VMEM] * 6,
-        out_specs=[VMEM, VMEM],
-        out_shape=[jax.ShapeDtypeStruct((3, copies, 2 * BAND * LANES), F32), stats_shape],
-        scratch_shapes=[pltpu.VMEM((4 * BAND, 16, LANES), F32)] + Engine.scratch(4 * BAND, copies, BAND * (BAND + 1)),
+    stats, *shared = pl.pallas_call(
+        functools.partial(cross_kernel, copies=copies, tiles=tiles),
+        in_specs=[SMEM] + [VMEM] * (3 + count),
+        out_specs=[VMEM] * (1 + count),
+        out_shape=[stats_shape, *shared_shapes],
+        input_output_aliases={4 + i: 1 + i for i in range(count)},
+        scratch_shapes=[x_shape, *Engine.work_shapes(copies, 1)],
         compiler_params=PARAMS,
-        name="edges",
-    )(base, partners, coords_pred, coords_true, kind, low, high, stats)
+        name="cross_tiles",
+    )(items, moments, low, high, *shared)
 
     step = 1
     while True:
@@ -712,13 +669,13 @@
     mean_loss = total[0, 0] / (copies * lax.axis_size("samp"))
     grad = pl.pallas_call(
         functools.partial(gradient_kernel, copies=copies, tiles=tiles),
-        in_specs=[VMEM] * 7,
+        in_specs=[VMEM] * 6,
         out_specs=VMEM,
         out_shape=jax.ShapeDtypeStruct((3, copies, local), F32),
         cost_estimate=pl.CostEstimate(flops=10**6, bytes_accessed=10**6, transcendentals=0),
         compiler_params=SMALL,
         name="gradient",
-    )(maps, centre, coords_pred, coords_true, kind, pull, edge_pull)
+    )(maps, centre, coords_pred, coords_true, kind, shared[Engine.shared.index("acc")])
     return copy_loss, mean_loss, jnp.transpose(grad, (1, 0, 2))
 
 

time: 57.7 us -> 56.9 us (0.986)
  Pallas kernels: 28.5 us -> 25.8 us
  starting transfers between devices: 17.1 us -> 18.9 us
    pallas_call x2, Pallas kernels: 25.4 us -> 22.7 us  [the longest x1 11.9 us: shards(): pl.pallas_call(functools.partial(self_kernel, copies=copies, tiles=tiles)...]
    ppermute x5, starting transfers between devices: 11 us -> 12.8 us  [swap(): lax.ppermute(x, axis, [(i, i ^ step) for i in range(lax.axis_size(axis))])]
  transfers between devices with their start and end apart: 7 -> 7, of which waited for: 5 -> 5; matrix products, arithmetic and copies ran while one was open for 0% -> 0% of each run, Pallas kernels for 41% -> 22%
where the time goes in v6:
time: 56.9 us
  Pallas kernels  25.8 us (45%)
  starting transfers between devices  18.9 us (33%)
  waiting for transfers between devices  9.12 us (16%)
  between operations  2.49 us (4%)
    ppermute x5, starting transfers between devices, swap(): lax.ppermute(x, axis, [(i, i ^ step) for i in range(lax.axis_size(axis))])  12.8 us
    pallas_call x1, Pallas kernels, shards(): pl.pallas_call(functools.partial(self_kernel, copies=copies, tiles=tiles)...  11.9 us
    pallas_call x1, Pallas kernels, shards(): pl.pallas_call(functools.partial(cross_kernel, copies=copies, tiles=tiles...  10.8 us
    ppermute x5, waiting for transfers between devices, swap(): lax.ppermute(x, axis, [(i, i ^ step) for i in range(lax.axis_size(axis))])  9.11 us
    ppermute x1, starting transfers between devices, shards(): low = lax.ppermute(last, 'res', forward)  4.84 us
    pallas_call x1, Pallas kernels, shards(): pl.pallas_call(functools.partial(solve_kernel, copies=copies, atoms=local...  1.29 us
    ppermute x1, starting transfers between devices, shards(): high = lax.ppermute(first, 'res', [(b, a) for a, b in forward])  1.29 us
  transfers between devices with their start and end apart: 7, of which 5 were waited for; matrix products, arithmetic and copies ran while one was open for 0% of the time, Pallas kernels for 22%

profile of v6, /device:TPU:0, one launch (start us, length us, event | category | flops | bytes accessed | tf_op | source)
XLA Modules:
  0.0 56.9 jit_solution(7041722962061509426)
XLA Ops:
  0.6 1.0 %pack.1 = (f32[16,256]{1,0:T(8,128)S(1)}, f32[16,256]{1,0:T(8,128)S(1)}, f32[3,4,3072]{2,1,0:T(4,128)S(1)}, f32[3,3072]{1,0:T(4,128)S(1)}, s32[1,3072]{1,0:T(1,1...) custom-call(f32[3,4,3072]{2,1,0:T(4,128)} %bitcast.6, f32[3,3072]{1,0:T(4,128)} %true_hbm.1, s32[1,3072]{1,0:T(1,128)} %bitcast.8, ...), custom_call_target="tpu_custom_call" | custom-call | tf_op jit(solution)/shard_map/pack/pallas_call | solution.py:605
  1.6 4.8 %collective-permute-start = (f32[16,256]{1,0:T(8,128)S(1)}, f32[16,256]{1,0:T(8,128)S(1)}, u32[]{:S(2)}, u32[]{:S(2)}) collective-permute-start(f32[16,256]{1,0:T(8,128)S(1)} %get-tuple-element.32), channel_id=1, source_target_pairs={{0,4},{4,8},{8,12},{12,16},{16,20},{20,24},{24,28},{1,5},{5,9},{9,... | collective-permute-start | bytes 49160 | tf_op jit(solution)/shard_map/ppermute | solution.py:615
  6.5 1.3 %collective-permute-start.1 = (f32[16,256]{1,0:T(8,128)S(1)}, f32[16,256]{1,0:T(8,128)S(1)}, u32[]{:S(2)}, u32[]{:S(2)}) collective-permute-start(f32[16,256]{1,0:T(8,128)S(1)} %get-tuple-element.33), channel_id=1, source_target_pairs={{4,0},{8,4},{12,8},{16,12},{20,16},{24,20},{28,24},{5,1},{9,5},{13... | collective-permute-start | bytes 49160 | tf_op jit(solution)/shard_map/ppermute | solution.py:616
  7.8 11.9 %self_tiles.1 = (f32[29,5,8,128]{3,2,1,0:T(8,128)S(1)}, f32[29,1,128]{2,1,0:T(1,128)S(1)}, f32[29,5,8,128]{3,2,1,0:T(8,128)S(1)}, bf16[29,3,128,128]{3,2,1,0:T(8...) custom-call(s32[1]{0:T(128)} %bitcast.base_ref, ...), custom_call_target="tpu_custom_call" | custom-call | flops 100000000 | bytes 1000000 | tf_op jit(solution)/shard_map/self_tiles/pallas_call | solution.py:621
  19.7 0.0 collective-permute-done.low_ref
  19.7 0.0 collective-permute-done.1.high_ref
  19.7 10.8 %cross_tiles.1 = (f32[2,8,128]{2,1,0:T(8,128)S(1)}, f32[29,5,8,128]{3,2,1,0:T(8,128)S(1)}, f32[29,1,128]{2,1,0:T(1,128)S(1)}, f32[29,5,8,128]{3,2,1,0:T(8,128)S(...) custom-call(s32[4,128]{1,0:T(4,128)S(1)} %get-tuple-element.30.items, ...), custom_call_target="tpu_custom_call", output_to_operand_aliasing={{1}: (4, {}), {2}: (5, {}), {3}: (6, {}), {4}: (7, {}), {5}... | custom-call | tf_op jit(solution)/shard_map/cross_tiles/pallas_call | solution.py:631
  30.5 4.7 %collective-permute-start.2 = (f32[2,8,128]{2,1,0:T(8,128)S(1)}, f32[2,8,128]{2,1,0:T(8,128)S(1)}, u32[]{:S(2)}, u32[]{:S(2)}) collective-permute-start(f32[2,8,128]{2,1,0:T(8,128)S(1)} %get-tuple-element.42), channel_id=1, source_target_pairs={{0,4},{4,0},{8,12},{12,8},{16,20},{20,16},{24,28},{28,24},{1,5},{5... | collective-permute-start | bytes 24584 | tf_op jit(solution)/shard_map/ppermute | solution.py:589
  35.3 1.6 %collective-permute-done.2 = f32[2,8,128]{2,1,0:T(8,128)S(1)} collective-permute-done((f32[2,8,128]{2,1,0:T(8,128)S(1)}, f32[2,8,128]{2,1,0:T(8,128)S(1)}, u32[]{:S(2)}, u32[]{:S(2)}) %collective-permute-start.2) | collective-permute-done | bytes 8224 | tf_op jit(solution)/shard_map/ppermute | solution.py:589
  36.9 5.2 %collective-permute-start.3 = (f32[2,8,128]{2,1,0:T(8,128)S(1)}, f32[2,8,128]{2,1,0:T(8,128)S(1)}, u32[]{:S(2)}, u32[]{:S(2)}) collective-permute-start(f32[2,8,128]{2,1,0:T(8,128)S(1)} %pad_maximum_fusion), channel_id=1, source_target_pairs={{0,8},{4,12},{8,0},{12,4},{16,24},{20,28},{24,16},{28,20},{1,9},{5... | collective-permute-start | bytes 24584 | tf_op jit(solution)/shard_map/ppermute | solution.py:589
  42.2 1.6 %collective-permute-done.3 = f32[2,8,128]{2,1,0:T(8,128)S(1)} collective-permute-done((f32[2,8,128]{2,1,0:T(8,128)S(1)}, f32[2,8,128]{2,1,0:T(8,128)S(1)}, u32[]{:S(2)}, u32[]{:S(2)}) %collective-permute-start.3) | collective-permute-done | bytes 8224 | tf_op jit(solution)/shard_map/ppermute | solution.py:589
  43.8 1.2 %collective-permute-start.4 = (f32[2,8,128]{2,1,0:T(8,128)S(1)}, f32[2,8,128]{2,1,0:T(8,128)S(1)}, u32[]{:S(2)}, u32[]{:S(2)}) collective-permute-start(f32[2,8,128]{2,1,0:T(8,128)S(1)} %pad_maximum_fusion.1.stat_ref), channel_id=1, source_target_pairs={{0,16},{4,20},{8,24},{12,28},{16,0},{20,4},{24,8},{28,12},{1,17},{... | collective-permute-start | bytes 24584 | tf_op jit(solution)/shard_map/ppermute | solution.py:589
  45.0 3.4 %collective-permute-done.4.other_ref = f32[2,8,128]{2,1,0:T(8,128)S(1)} collective-permute-done((f32[2,8,128]{2,1,0:T(8,128)S(1)}, f32[2,8,128]{2,1,0:T(8,128)S(1)}, u32[]{:S(2)}, u32[]{:S(2)}) %collective-permute-start.4) | collective-permute-done | bytes 8224 | tf_op jit(solution)/shard_map/ppermute | solution.py:589
  48.4 1.3 %solve.1 = (f32[4]{0:T(128)}, f32[8,128]{1,0:T(8,128)S(1)}, f32[14,4,128]{2,1,0:T(4,128)S(1)}, f32[8,128]{1,0:T(8,128)S(1)}) custom-call(f32[2,8,128]{2,1,0:T(8,128)S(1)} %pad_maximum_fusion.1.stat_ref, f32[2,8,128]{2,1,0:T(8,128)S(1)} %collective-permute-done.4.other_ref, f32[4,128]{1,0:T(4,128)S(1)} %get-tuple-element.43.noise_ref), custom_call_target="tpu_custom_call" | custom-call | tf_op jit(solution)/shard_map/solve/pallas_call | solution.py:651
  49.7 0.1 collective-permute-start.5
  49.8 1.2 %collective-permute-done.5 = f32[8,128]{1,0:T(8,128)S(1)} collective-permute-done((f32[8,128]{1,0:T(8,128)S(1)}, f32[8,128]{1,0:T(8,128)S(1)}, u32[]{:S(2)}, u32[]{:S(2)}) %collective-permute-start.5) | collective-permute-done | bytes 4128 | tf_op jit(solution)/shard_map/ppermute | solution.py:589
  51.0 1.5 %collective-permute-start.6 = (f32[8,128]{1,0:T(8,128)S(1)}, f32[8,128]{1,0:T(8,128)S(1)}, u32[]{:S(2)}, u32[]{:S(2)}) collective-permute-start(f32[8,128]{1,0:T(8,128)S(1)} %add.53), channel_id=1, source_target_pairs={{0,2},{1,3},{2,0},{3,1},{4,6},{5,7},{6,4},{7,5},{8,10},{9,11},{10,... | collective-permute-start | bytes 12296 | tf_op jit(solution)/shard_map/ppermute | solution.py:589
  52.5 0.8 %gradient.1 = f32[3,4,3072]{2,1,0:T(4,128)} custom-call(f32[14,4,128]{2,1,0:T(4,128)S(1)} %get-tuple-element.46.m_ref, f32[8,128]{1,0:T(8,128)S(1)} %get-tuple-element.47.k_ref, f32[3,4,3072]{2,1,0:T(4,128)S(1)} %get-tuple-element.27.pred_ref, f32[3,3072]{1,0:T(4,128)S(1)} %get-tuple-element.28.true_ref, s32[1,3072]{1,0:T(1,128)S(1)} %get-tuple-element.29.kind_ref, ...), custom_call_target="tpu_custom_call" | custom-call | flops 1000000 | bytes 1000000 | tf_op jit(solution)/shard_map/gradient/pallas_call | solution.py:670
  53.3 1.3 %collective-permute-done.6 = f32[8,128]{1,0:T(8,128)S(1)} collective-permute-done((f32[8,128]{1,0:T(8,128)S(1)}, f32[8,128]{1,0:T(8,128)S(1)}, u32[]{:S(2)}, u32[]{:S(2)}) %collective-permute-start.6) | collective-permute-done | bytes 4128 | tf_op jit(solution)/shard_map/ppermute | solution.py:589
  54.6 0.5 slice.27
  (6 shorter events, 0.0 us)
Async XLA Ops:
  1.6 18.1 %collective-permute-start = (f32[16,256]{1,0:T(8,128)S(1)}, f32[16,256]{1,0:T(8,128)S(1)}, u32[]{:S(2)}, u32[]{:S(2)}) collective-permute-start(f32[16,256]{1,0:T(8,128)S(1)} %get-tuple-element.32), channel_id=1, source_target_pairs={{0,4},{4,8},{8,12},{12,16},{16,20},{20,24},{24,28},{1,5},{5,9},{9,... | collective-permute-start | bytes 49160 | tf_op jit(solution)/shard_map/ppermute | solution.py:615
  6.5 13.3 %collective-permute-start.1 = (f32[16,256]{1,0:T(8,128)S(1)}, f32[16,256]{1,0:T(8,128)S(1)}, u32[]{:S(2)}, u32[]{:S(2)}) collective-permute-start(f32[16,256]{1,0:T(8,128)S(1)} %get-tuple-element.33), channel_id=1, source_target_pairs={{4,0},{8,4},{12,8},{16,12},{20,16},{24,20},{28,24},{5,1},{9,5},{13... | collective-permute-start | bytes 49160 | tf_op jit(solution)/shard_map/ppermute | solution.py:616
  30.5 6.4 %collective-permute-start.2 = (f32[2,8,128]{2,1,0:T(8,128)S(1)}, f32[2,8,128]{2,1,0:T(8,128)S(1)}, u32[]{:S(2)}, u32[]{:S(2)}) collective-permute-start(f32[2,8,128]{2,1,0:T(8,128)S(1)} %get-tuple-element.42), channel_id=1, source_target_pairs={{0,4},{4,0},{8,12},{12,8},{16,20},{20,16},{24,28},{28,24},{1,5},{5... | collective-permute-start | bytes 24584 | tf_op jit(solution)/shard_map/ppermute | solution.py:589
  36.9 6.9 %collective-permute-start.3 = (f32[2,8,128]{2,1,0:T(8,128)S(1)}, f32[2,8,128]{2,1,0:T(8,128)S(1)}, u32[]{:S(2)}, u32[]{:S(2)}) collective-permute-start(f32[2,8,128]{2,1,0:T(8,128)S(1)} %pad_maximum_fusion), channel_id=1, source_target_pairs={{0,8},{4,12},{8,0},{12,4},{16,24},{20,28},{24,16},{28,20},{1,9},{5... | collective-permute-start | bytes 24584 | tf_op jit(solution)/shard_map/ppermute | solution.py:589
  43.8 4.6 %collective-permute-start.4 = (f32[2,8,128]{2,1,0:T(8,128)S(1)}, f32[2,8,128]{2,1,0:T(8,128)S(1)}, u32[]{:S(2)}, u32[]{:S(2)}) collective-permute-start(f32[2,8,128]{2,1,0:T(8,128)S(1)} %pad_maximum_fusion.1.stat_ref), channel_id=1, source_target_pairs={{0,16},{4,20},{8,24},{12,28},{16,0},{20,4},{24,8},{28,12},{1,17},{... | collective-permute-start | bytes 24584 | tf_op jit(solution)/shard_map/ppermute | solution.py:589
  49.7 1.2 %collective-permute-start.5 = (f32[8,128]{1,0:T(8,128)S(1)}, f32[8,128]{1,0:T(8,128)S(1)}, u32[]{:S(2)}, u32[]{:S(2)}) collective-permute-start(f32[8,128]{1,0:T(8,128)S(1)} %get-tuple-element.45), channel_id=1, source_target_pairs={{0,1},{1,0},{2,3},{3,2},{4,5},{5,4},{6,7},{7,6},{8,9},{9,8},{10,11... | collective-permute-start | bytes 12296 | tf_op jit(solution)/shard_map/ppermute | solution.py:589
  51.0 3.6 %collective-permute-start.6 = (f32[8,128]{1,0:T(8,128)S(1)}, f32[8,128]{1,0:T(8,128)S(1)}, u32[]{:S(2)}, u32[]{:S(2)}) collective-permute-start(f32[8,128]{1,0:T(8,128)S(1)} %add.53), channel_id=1, source_target_pairs={{0,2},{1,3},{2,0},{3,1},{4,6},{5,7},{6,4},{7,5},{8,10},{9,11},{10,... | collective-permute-start | bytes 12296 | tf_op jit(solution)/shard_map/ppermute | solution.py:589
